TPU v7x, 32 devices: a whole 2x2x4 slice. The times are simulated.
32 devices in a mesh: dp: 8 (over y, x, core), mp: 4 (over z).
Axes of the slice: x: 2, y: 2, z: 4, core: 2. Of those that a mesh axis runs over, the one named last changes fastest.
Arguments:
- inputs: bfloat16 [8192, 2048], P('dp', 'mp'), may hold values from -6 to 6
- segment_ids: int32 [8, 1024], P('dp'), may hold values from 0 to 3, never falling along the last dimension, each value on 1 to 512 neighbouring positions
- width_bucket: int32 [8, 1024], P('dp'), may hold values from 0 to 3, as said below
- attn_gain: float32 [2048], P('mp'), may hold values from 0.25 to 1.75
- attn_bias: float32 [2048], P('mp'), may hold values from -1.5 to 1.5
- qkv_weight: bfloat16 [3, 2048, 2048], P(None, None, 'mp'), may hold values from -0.125 to 0.125
- proj_weight: bfloat16 [2048, 2048], P('mp'), may hold values from -0.75 to 0.75
- ffn_gain: float32 [2048], P('mp'), may hold values from 0.25 to 1.75
- ffn_bias: float32 [2048], P('mp'), may hold values from -1.5 to 1.5
- up_weight: bfloat16 [2048, 8192], P(None, 'mp'), may hold values from -0.125 to 0.125
- down_weight: bfloat16 [8192, 2048], P('mp'), may hold values from -0.0625 to 0.0625
- grad_result: bfloat16 [8192, 2048], P('dp', 'mp'), may hold values from -6 to 6
Outputs:
- block_output: bfloat16 [8192, 2048], P('dp', 'mp')
- grad_input: float32 [8192, 2048], P('dp', 'mp')
- grad_attn_gain: float32 [2048], P('mp')
- grad_attn_bias: float32 [2048], P('mp')
- grad_qkv: float32 [3, 2048, 2048], P(None, None, 'mp')
- grad_proj: float32 [2048, 2048], P('mp')
- grad_ffn_gain: float32 [2048], P('mp')
- grad_ffn_bias: float32 [2048], P('mp')
- grad_up: float32 [2048, 8192], P(None, 'mp')
- grad_down: float32 [8192, 2048], P('mp')
Inputs may be any that keep to these rules, and one draw needn't show every extreme that they name: `segment_ids`: in each row the document numbers never fall and all 4 documents appear; the longest holds exactly 512 tokens. `width_bucket`: each packed row holds exactly 256 tokens of each of the four buckets, in any order.
All inputs are finite; a program needn't handle non-finite values.
Results may differ from a plain program's by a relative error of at most 0.014.
Values may be sent and summed in bfloat16 or wider, within the bound.
No kernel may reach another device: no remote copies, remote signals or barrier semaphores. Data moves between devices by JAX's collectives and lax.ppermute only.
A program may use at most 256 MiB of HBM per device.

v0:
```python
import jax
import jax.numpy as jnp
from jax import lax
from jax.sharding import PartitionSpec as P

HEAD_DIM = 128
FF = 8192


EPSILON = 1e-05
MASKED = -1e30


def rotate(values, cosine, sine_table):
    half_dim = values.shape[-1] // 2
    former = values[..., :half_dim]
    latter = values[..., half_dim:]
    return jnp.concatenate(
        [former * cosine - latter * sine_table, latter * cosine + former * sine_table], axis=-1
    )


def rotate_back(values, cosine, sine_table):
    half_dim = values.shape[-1] // 2
    former = values[..., :half_dim]
    latter = values[..., half_dim:]
    return jnp.concatenate(
        [former * cosine + latter * sine_table, latter * cosine - former * sine_table], axis=-1
    )


def norm_forward(local_rows, gain_vec, bias_vec):
    feature_count = local_rows.shape[1] * lax.axis_size("mp")
    totals, squares = lax.psum(
        (jnp.sum(local_rows, axis=1), jnp.sum(local_rows * local_rows, axis=1)), "mp"
    )
    mean_val = totals / feature_count
    rstd_val = lax.rsqrt(squares / feature_count - mean_val * mean_val + EPSILON)
    normal_x = (local_rows - mean_val[:, None]) * rstd_val[:, None]
    normed = (normal_x * gain_vec + bias_vec).astype(jnp.bfloat16)
    return (normal_x, rstd_val, lax.all_gather(normed, "mp", axis=1, tiled=True), normed)


def norm_backward(grad_normed, normal_x, rstd_val, gain_vec):
    feature_count = grad_normed.shape[1] * lax.axis_size("mp")
    scaled = grad_normed * gain_vec
    sum_plain, sum_cross = lax.psum(
        (jnp.sum(scaled, axis=1), jnp.sum(scaled * normal_x, axis=1)), "mp"
    )
    grad_x = rstd_val[:, None] * (
        scaled
        - sum_plain[:, None] / feature_count
        - normal_x * (sum_cross[:, None] / feature_count)
    )
    return (grad_x, jnp.sum(grad_normed * normal_x, axis=0), jnp.sum(grad_normed, axis=0))


def regather(normed):
    return lax.all_gather(normed, "mp", axis=1, tiled=True)


def grad_rows(local_grad):
    return lax.all_gather(local_grad, "mp", axis=1, tiled=True)


def back_sum(partial_grad):
    return lax.psum_scatter(partial_grad, "mp", scatter_dimension=1, tiled=True)


def local(
    inputs,
    segment_ids,
    width_bucket,
    attn_gain,
    attn_bias,
    qkv_weight,
    proj_weight,
    ffn_gain,
    ffn_bias,
    up_weight,
    down_weight,
    grad_result,
):
    token_count = inputs.shape[0]
    row_len = segment_ids.shape[1]
    block_len = min(512, row_len)
    block_count = token_count // block_len
    per_row = row_len // block_len
    head_local = qkv_weight.shape[2] // HEAD_DIM
    local_cols = head_local * HEAD_DIM
    scale = HEAD_DIM ** (-0.5)
    seg_flat = segment_ids.reshape(token_count)
    positions = jnp.arange(token_count, dtype=jnp.int32) % row_len
    half_dim = HEAD_DIM // 2
    freqs = jnp.power(10000.0, -jnp.arange(half_dim, dtype=jnp.float32) / half_dim)
    angles = positions.astype(jnp.float32)[:, None] * freqs[None, :]
    cosine = jnp.cos(angles)[:, None, :]
    sine_table = jnp.sin(angles)[:, None, :]

    def project_heads(rows_in):
        projected = jnp.einsum(
            "td,sdc->stc", rows_in, qkv_weight, preferred_element_type=jnp.float32
        )
        q_rot = rotate(
            projected[0].reshape(token_count, head_local, HEAD_DIM), cosine, sine_table
        ).astype(jnp.bfloat16)
        k_rot = rotate(
            projected[1].reshape(token_count, head_local, HEAD_DIM), cosine, sine_table
        ).astype(jnp.bfloat16)
        v_heads = projected[2].reshape(token_count, head_local, HEAD_DIM).astype(jnp.bfloat16)
        return (q_rot, k_rot, v_heads)

    bucket_flat = width_bucket.reshape(token_count)
    limit = (bucket_flat + 1) * (FF // 4)
    columns = lax.axis_index("mp") * up_weight.shape[1] + jnp.arange(
        up_weight.shape[1], dtype=jnp.int32
    )
    keep_mask = (columns[None, :] < limit[:, None]).astype(jnp.float32)

    def ffn_hidden(rows_in):
        hidden = jnp.dot(rows_in, up_weight, preferred_element_type=jnp.float32)
        active = (jnp.square(jnp.maximum(hidden, 0.0)) * keep_mask).astype(jnp.bfloat16)
        return (hidden, active)

    def block_scores(block_idx, q_rot, k_rot):
        start = block_idx * block_len
        row_start = block_idx // per_row * row_len
        q_block = lax.dynamic_slice_in_dim(q_rot, start, block_len, 0)
        seg_query = lax.dynamic_slice_in_dim(seg_flat, start, block_len, 0)
        query_pos = start - row_start + jnp.arange(block_len, dtype=jnp.int32)
        key_pos = jnp.arange(row_len, dtype=jnp.int32)
        allowed = (seg_query[:, None] == seg_flat[None, :]) & (
            key_pos[None, :] <= query_pos[:, None]
        )
        raw = jnp.einsum("qhd,khd->hqk", q_block, k_rot, preferred_element_type=jnp.float32) * scale
        return (jnp.where(allowed[None], raw, MASKED), q_block, k_rot, start, row_start)

    resid_in = inputs.astype(jnp.float32)
    norm_one, rstd_one, attn_rows, attn_local = norm_forward(resid_in, attn_gain, attn_bias)
    q_rot, k_rot, v_heads = project_heads(attn_rows)

    def attend_block(block_idx):
        scores, q_block, k_row, start, row_start = block_scores(block_idx, q_rot, k_rot)
        peak = jnp.max(scores, axis=-1)
        expo = jnp.exp(scores - peak[..., None])
        totals = jnp.sum(expo, axis=-1)
        probs_low = (expo / totals[..., None]).astype(jnp.bfloat16)
        attended = jnp.einsum(
            "hqk,khd->qhd", probs_low, v_heads, preferred_element_type=jnp.float32
        ).astype(jnp.bfloat16)
        return (attended, peak + jnp.log(totals))

    attn_blocks, lse_blocks = lax.map(attend_block, jnp.arange(block_count))
    attn_flat = attn_blocks.reshape(token_count, local_cols)
    attn_part = jnp.dot(attn_flat, proj_weight, preferred_element_type=jnp.float32)
    mid_resid = resid_in + lax.psum_scatter(attn_part, "mp", scatter_dimension=1, tiled=True)
    norm_two, rstd_two, ffn_rows, ffn_local = norm_forward(mid_resid, ffn_gain, ffn_bias)
    hidden, active = ffn_hidden(ffn_rows)
    ffn_part = jnp.dot(active, down_weight, preferred_element_type=jnp.float32)
    block_output = (
        mid_resid
        + lax.psum_scatter(
            ffn_part.astype(jnp.bfloat16), "mp", scatter_dimension=1, tiled=True
        ).astype(jnp.float32)
    ).astype(jnp.bfloat16)
    grad_full = grad_rows(grad_result)
    back_ffn_rows = regather(ffn_local)
    back_hidden, back_active = ffn_hidden(back_ffn_rows)
    grad_down = jnp.einsum("tf,td->fd", back_active, grad_full, preferred_element_type=jnp.float32)
    grad_act = jnp.einsum("td,fd->tf", grad_full, down_weight, preferred_element_type=jnp.float32)
    grad_hidden = (2.0 * jnp.maximum(back_hidden, 0.0) * keep_mask * grad_act).astype(jnp.bfloat16)
    grad_up = jnp.einsum(
        "td,tf->df", back_ffn_rows, grad_hidden, preferred_element_type=jnp.float32
    )
    grad_ffn_in = back_sum(
        jnp.einsum("tf,df->td", grad_hidden, up_weight, preferred_element_type=jnp.float32)
    )
    grad_norm_two, grad_ffn_gain, grad_ffn_bias = norm_backward(
        grad_ffn_in, norm_two, rstd_two, ffn_gain
    )
    grad_mid = grad_result.astype(jnp.float32) + grad_norm_two
    grad_mid_full = grad_rows(grad_mid.astype(jnp.bfloat16))
    grad_proj = jnp.einsum(
        "tc,td->cd", attn_flat, grad_mid_full, preferred_element_type=jnp.float32
    )
    grad_att = jnp.einsum(
        "td,cd->tc", grad_mid_full, proj_weight, preferred_element_type=jnp.float32
    ).astype(jnp.bfloat16)
    grad_att = grad_att.reshape(token_count, head_local, HEAD_DIM)
    back_attn_rows = regather(attn_local)
    back_q, back_k, back_v = project_heads(back_attn_rows)

    def back_block(pair_state, block_idx):
        grad_keys, grad_vals = pair_state
        scores, q_block, k_row, start, row_start = block_scores(block_idx, back_q, back_k)
        lse_block = lse_blocks[block_idx]
        probs = jnp.exp(scores - lse_block[..., None])
        probs_low = probs.astype(jnp.bfloat16)
        grad_block = lax.dynamic_slice_in_dim(grad_att, start, block_len, 0)
        grad_probs = jnp.einsum(
            "qhd,khd->hqk", grad_block, back_v, preferred_element_type=jnp.float32
        )
        row_delta = jnp.sum(probs * grad_probs, axis=-1)
        grad_raw = (probs * (grad_probs - row_delta[..., None]) * scale).astype(jnp.bfloat16)
        grad_query = jnp.einsum("hqk,khd->qhd", grad_raw, k_row, preferred_element_type=jnp.float32)
        grad_key = jnp.einsum("hqk,qhd->khd", grad_raw, q_block, preferred_element_type=jnp.float32)
        grad_val = jnp.einsum(
            "hqk,qhd->khd", probs_low, grad_block, preferred_element_type=jnp.float32
        )
        grad_keys = grad_keys + grad_key
        grad_vals = grad_vals + grad_val
        return ((grad_keys, grad_vals), grad_query)

    zero_heads = jnp.zeros((token_count, head_local, HEAD_DIM), jnp.float32)
    (grad_keys, grad_vals), grad_queries = lax.scan(
        back_block, (zero_heads, zero_heads), jnp.arange(block_count)
    )
    grad_queries = grad_queries.reshape(token_count, head_local, HEAD_DIM)
    grad_q = (
        rotate_back(grad_queries, cosine, sine_table)
        .astype(jnp.bfloat16)
        .reshape(token_count, local_cols)
    )
    grad_k = (
        rotate_back(grad_keys, cosine, sine_table)
        .astype(jnp.bfloat16)
        .reshape(token_count, local_cols)
    )
    grad_v = grad_vals.astype(jnp.bfloat16).reshape(token_count, local_cols)
    stacked = jnp.stack([grad_q, grad_k, grad_v])
    grad_qkv = jnp.einsum(
        "td,stc->sdc", back_attn_rows, stacked, preferred_element_type=jnp.float32
    )
    grad_attn_in = back_sum(
        jnp.einsum("stc,sdc->td", stacked, qkv_weight, preferred_element_type=jnp.float32)
    )
    grad_norm_one, grad_attn_gain, grad_attn_bias = norm_backward(
        grad_attn_in, norm_one, rstd_one, attn_gain
    )
    grad_input = grad_mid + grad_norm_one
    (
        grad_qkv,
        grad_proj,
        grad_attn_gain,
        grad_attn_bias,
        grad_up,
        grad_down,
        grad_ffn_gain,
        grad_ffn_bias,
    ) = lax.psum(
        (
            grad_qkv,
            grad_proj,
            grad_attn_gain,
            grad_attn_bias,
            grad_up,
            grad_down,
            grad_ffn_gain,
            grad_ffn_bias,
        ),
        "dp",
    )
    return (
        block_output,
        grad_input,
        grad_attn_gain,
        grad_attn_bias,
        grad_qkv,
        grad_proj,
        grad_ffn_gain,
        grad_ffn_bias,
        grad_up,
        grad_down,
    )


def solution(mesh):
    placed = (
        P("dp", "mp"),
        P("dp", None),
        P("dp", None),
        P("mp"),
        P("mp"),
        P(None, None, "mp"),
        P("mp", None),
        P("mp"),
        P("mp"),
        P(None, "mp"),
        P("mp", None),
        P("dp", "mp"),
    )
    return jax.shard_map(
        local,
        mesh=mesh,
        in_specs=placed,
        out_specs=(
            P("dp", "mp"),
            P("dp", "mp"),
            P("mp"),
            P("mp"),
            P(None, None, "mp"),
            P("mp", None),
            P("mp"),
            P("mp"),
            P(None, "mp"),
            P("mp", None),
        ),
        check_vma=False,
    )
```

profile of v0, /device:TPU:0, one launch (start us, length us, event | category | flops | bytes accessed | tf_op | source)
XLA Modules:
  0.0 1783.9 jit_solution(15177743647234207747)
XLA Ops:
  9.0 13.7 all-reduce.5
  27.4 77.1 %all-gather.5.cloned.1.call-done = bf16[1024,2048]{1,0:T(8,128)(2,1)} async-done(((bf16[1024,512]{1,0:T(8,128)(2,1)}), bf16[1024,2048]{1,0:T(8,128)(2,1)}) %all-gather.5.cloned.1.call-update) | async-done | bytes 4194320 | tf_op jit(solution)/shard_map/all_gather | solution.py:41
  144.6 29.0 %while.31 = (s32[]{:T(128)}, bf16[2,512,4,128]{3,2,1,0:T(4,128)(2,1)}, f32[2,4,512]{2,1,0:T(4,128)S(1)}, s32[2]{0:T(128)S(1)}, s32[1024]{0:T(1024)S(1)}, /*index...) while((s32[]{:T(128)}, ...), condition=%wide.region_7.8_spmd, body=%wide.region_4.7_spmd.sunk | while | flops 1100741120 | bytes 44120540 | solution.py:153
  180.7 143.1 %reduce-scatter.5.cloned.1.call-done = f32[1024,512]{1,0:T(8,128)} async-done(((f32[1024,2048]{1,0:T(8,128)}), f32[1024,512]{1,0:T(8,128)}) %reduce-scatter.5.cloned.1.call-update) | async-done | bytes 2097168 | tf_op jit(solution)/shard_map/reduce_scatter | solution.py:156
  342.1 78.6 %all-gather.7.cloned.1.call-done = bf16[1024,2048]{1,0:T(8,128)(2,1)} async-done(((bf16[1024,512]{1,0:T(8,128)(2,1)}), bf16[1024,2048]{1,0:T(8,128)(2,1)}) %all-gather.7.cloned.1.call-update) | async-done | bytes 4194320 | tf_op jit(solution)/shard_map/all_gather | solution.py:41
  420.7 14.7 fusion.119
  435.4 66.1 %all-gather.9.cloned.1.call-done = bf16[1024,2048]{1,0:T(8,128)(2,1)} async-done(((bf16[1024,512]{1,0:T(8,128)(2,1)}), bf16[1024,2048]{1,0:T(8,128)(2,1)}) %all-gather.9.cloned.1.call-update) | async-done | bytes 4194320 | tf_op jit(solution)/shard_map/all_gather | solution.py:63
  501.5 13.9 fusion.79
  517.3 13.5 fusion.120
  530.9 16.1 convolution_convert_fusion
  547.1 126.9 %reduce-scatter.9.cloned.1.call-done = f32[1024,512]{1,0:T(8,128)} async-done(((f32[1024,2048]{1,0:T(8,128)}), f32[1024,512]{1,0:T(8,128)}) %reduce-scatter.9.cloned.1.call-update) | async-done | bytes 2097168 | tf_op jit(solution)/shard_map/reduce_scatter | solution.py:67
  689.2 65.2 %reduce-scatter.7.cloned.1.call-done = bf16[1024,512]{1,0:T(8,128)(2,1)} async-done(((bf16[1024,2048]{1,0:T(8,128)(2,1)}), bf16[1024,512]{1,0:T(8,128)(2,1)}) %reduce-scatter.7.cloned.1.call-update) | async-done | bytes 1048592 | tf_op jit(solution)/shard_map/reduce_scatter | solution.py:162
  759.1 81.3 %all-gather.11.cloned.1.call-done = bf16[1024,2048]{1,0:T(8,128)(2,1)} async-done(((bf16[1024,512]{1,0:T(8,128)(2,1)}), bf16[1024,2048]{1,0:T(8,128)(2,1)}) %all-gather.11.cloned.1.call-update) | async-done | bytes 4194320 | tf_op jit(solution)/shard_map/all_gather | solution.py:63
  845.9 132.4 %while.32 = (s32[]{:T(128)}, f32[1024,4,128]{0,2,1:T(8,128)}, f32[1024,4,128]{0,2,1:T(8,128)}, f32[2,512,4,128]{3,1,0,2:T(8,128)}, s32[2]{0:T(128)S(1)}, /*index...) while((s32[]{:T(128)}, f32[1024,4,128]{0,2,1:T(8,128)}, ...), condition=%wide.region_21.22_spmd.clone, body=%wide.region_19.21_spmd.clone.sunk | while | flops 2742557184 | bytes 175184544 | solution.py:215
  864.0 24.7 %bitcast_add_fusion.4 = f32[1024,4,128]{0,2,1:T(8,128)} fusion(f32[1024,4,128]{0,2,1:T(8,128)} %get-tuple-element.678, f32[4,512,1024]{2,1,0:T(8,128)} %fusion.179, f32[4,512,1024]{2,1,0:T(8,128)} %copy-done.2, f32[4,512]{1,0:T(4,128)S(1)} %dynamic-slice_bitcast_fusion.2, pred[512,1024]{1,0:T(8,128)(4,1)} %copy-done.7, pred[]{:T(512)S(6)} %compare.16, ...), kind=kOutput, calls=%fused_computation.40.clone.1 | convolution fusion | flops 560991232 | bytes 39337988 | tf_op jit(solution)/shard_map/while/body/eval_jaxpr/hqk,qhd->khd/dot_general | solution.py:206
  888.6 23.2 %fusion.182 = f32[2,512,4,128]{3,1,0,2:T(8,128)} fusion(f32[2,512,4,128]{3,1,0,2:T(8,128)} %get-tuple-element.680, s32[]{:T(128)S(6)} %copy.110, bf16[1024,4,128]{2,0,1:T(8,128)(2,1)S(1)} %get-tuple-element.703, f32[4,512,1024]{2,1,0:T(8,128)} %fusion.179, f32[4,512,1024]{2,1,0:T(8,128)} %copy-done.2, f32[4,512]{1,0:T(4,128)S(1)} %dynamic-slice_bitcast_fusion.2, ...), kind=kOutput, calls=%fused_computation.44.clone.1 | convolution fusion | flops 559942656 | bytes 36716548 | tf_op jit(solution)/shard_map/while/body/eval_jaxpr/hqk,khd->qhd/dot_general | solution.py:205
  929.7 25.2 %bitcast_add_fusion.4 = f32[1024,4,128]{0,2,1:T(8,128)} fusion(f32[1024,4,128]{0,2,1:T(8,128)} %get-tuple-element.678, f32[4,512,1024]{2,1,0:T(8,128)} %fusion.179, f32[4,512,1024]{2,1,0:T(8,128)} %copy-done.2, f32[4,512]{1,0:T(4,128)S(1)} %dynamic-slice_bitcast_fusion.2, pred[512,1024]{1,0:T(8,128)(4,1)} %copy-done.7, pred[]{:T(512)S(6)} %compare.16, ...), kind=kOutput, calls=%fused_computation.40.clone.1 | convolution fusion | flops 560991232 | bytes 39337988 | tf_op jit(solution)/shard_map/while/body/eval_jaxpr/hqk,qhd->khd/dot_general | solution.py:206
  954.9 23.2 %fusion.182 = f32[2,512,4,128]{3,1,0,2:T(8,128)} fusion(f32[2,512,4,128]{3,1,0,2:T(8,128)} %get-tuple-element.680, s32[]{:T(128)S(6)} %copy.110, bf16[1024,4,128]{2,0,1:T(8,128)(2,1)S(1)} %get-tuple-element.703, f32[4,512,1024]{2,1,0:T(8,128)} %fusion.179, f32[4,512,1024]{2,1,0:T(8,128)} %copy-done.2, f32[4,512]{1,0:T(4,128)S(1)} %dynamic-slice_bitcast_fusion.2, ...), kind=kOutput, calls=%fused_computation.44.clone.1 | convolution fusion | flops 559942656 | bytes 36716548 | tf_op jit(solution)/shard_map/while/body/eval_jaxpr/hqk,khd->qhd/dot_general | solution.py:205
  1005.8 16.0 fusion.121
  1021.8 15.3 fusion.111
  1052.1 96.7 %reduce-scatter.11.cloned.1.call-done = f32[1024,512]{1,0:T(8,128)} async-done(((f32[1024,2048]{1,0:T(8,128)}), f32[1024,512]{1,0:T(8,128)}) %reduce-scatter.11.cloned.1.call-update) | async-done | bytes 2097168 | tf_op jit(solution)/shard_map/reduce_scatter | solution.py:67
  1151.7 14.4 all-reduce
  1181.0 557.2 %all-reduce.8.cloned.1.call-done = (f32[3,2048,512]{1,2,0:T(8,128)}, f32[512,2048]{1,0:T(8,128)}, f32[2048,2048]{1,0:T(8,128)}, f32[2048,2048]{1,0:T(8,128)}) async-done(((f32[3,2048,512]{1,2,0:T(8,128)}, f32[512,2048]{1,0:T(8,128)}, f32[2048,2048]{1,0:T(8,128)}, f32[2048,2048]{1,0:T(8,128)}), (f32[3,2048,512]{1,2,0:T(8,128)}, f32[512,2048]{1,0:T(8,128)}, f32[2048,2048]{1,0:T(8,128)}, ...) | async-done | bytes 50331664 | tf_op jit(solution)/shard_map/psum | solution.py:250
  1755.6 13.6 copy.123
  (228 shorter events, 233.2 us)
Async XLA Ops:
  7.2 166.4 %copy-start = (bf16[512,2048]{1,0:T(8,128)(2,1)S(1)}, bf16[512,2048]{1,0:T(8,128)(2,1)}, u32[]{:S(2)}) copy-start(bf16[512,2048]{1,0:T(8,128)(2,1)} %param.22) | copy-start | bytes 6291460
  7.2 97.3 %all-gather.5.cloned.1.call-start = ((), (), s32[]{:S(2)}) async-start(), calls=%async_computation.4 | async-start | bytes 5242880 | tf_op jit(solution)/shard_map/all_gather | solution.py:41
  25.4 298.3 %reduce-scatter.5.cloned.1.call-start = ((), (), s32[]{:S(2)}) async-start(), calls=%async_computation.5 | async-start | bytes 10485760 | tf_op jit(solution)/shard_map/reduce_scatter | solution.py:156
  27.4 110.4 %copy-start.12 = (f32[1024,64]{1,0:T(8,128)}, f32[1024,64]{1,0:T(8,128)S(1)}, u32[]{:S(2)}) copy-start(f32[1024,64]{1,0:T(8,128)S(1)} %get-tuple-element.477) | copy-start | bytes 786436
  27.4 110.4 %copy-start.14 = (f32[1024,64]{1,0:T(8,128)}, f32[1024,64]{1,0:T(8,128)S(1)}, u32[]{:S(2)}) copy-start(f32[1024,64]{1,0:T(8,128)S(1)} %get-tuple-element.478) | copy-start | bytes 786436
  180.6 157.8 %copy-start.31 = (f32[512]{0:T(512)S(1)}, f32[512]{0:T(512)}, u32[]{:S(2)}) copy-start(f32[512]{0:T(512)} %param.23) | copy-start | bytes 6148
  180.6 157.8 %copy-start.40 = (f32[512]{0:T(512)S(1)}, f32[512]{0:T(512)}, u32[]{:S(2)}) copy-start(f32[512]{0:T(512)} %param.24) | copy-start | bytes 6148
  180.6 161.5 %copy-start.37 = (s32[1,1024]{1,0:T(1,128)S(1)}, s32[1,1024]{1,0:T(1,128)}, u32[]{:S(2)}) copy-start(s32[1,1024]{1,0:T(1,128)} %param.18) | copy-start | bytes 12292
  180.6 240.1 %all-gather.7.cloned.1.call-start = ((), (), s32[]{:S(2)}) async-start(), calls=%async_computation.6 | async-start | bytes 5242880 | tf_op jit(solution)/shard_map/all_gather | solution.py:41
  341.4 160.0 %all-gather.9.cloned.1.call-start = ((), (), s32[]{:S(2)}) async-start(), calls=%async_computation.8 | async-start | bytes 5242880 | tf_op jit(solution)/shard_map/all_gather | solution.py:63
  342.0 332.0 %reduce-scatter.9.cloned.1.call-start = ((), (), s32[]{:S(2)}) async-start(), calls=%async_computation.9 | async-start | bytes 10485760 | tf_op jit(solution)/shard_map/reduce_scatter | solution.py:67
  342.1 188.8 %copy-start.35 = (s32[2048]{0:T(1024)}, s32[2048]{0:T(1024)S(1)}, u32[]{:S(2)}) copy-start(s32[2048]{0:T(1024)S(1)} %iota_add_fusion.2) | copy-start | bytes 24580
  342.1 188.8 %copy-start.38 = (s32[1,1024]{1,0:T(1,128)}, s32[1,1024]{1,0:T(1,128)S(1)}, u32[]{:S(2)}) copy-start(s32[1,1024]{1,0:T(1,128)S(1)} %add_multiply_fusion) | copy-start | bytes 12292
  530.8 223.6 %reduce-scatter.7.cloned.1.call-start = ((), (), s32[]{:S(2)}) async-start(), calls=%async_computation.7 | async-start | bytes 5242880 | tf_op jit(solution)/shard_map/reduce_scatter | solution.py:162
  547.0 293.4 %all-gather.11.cloned.1.call-start = ((), (), s32[]{:S(2)}) async-start(), calls=%async_computation.10 | async-start | bytes 5242880 | tf_op jit(solution)/shard_map/all_gather | solution.py:63
  759.0 389.8 %reduce-scatter.11.cloned.1.call-start = ((), (), s32[]{:S(2)}) async-start(), calls=%async_computation.11 | async-start | bytes 10485760 | tf_op jit(solution)/shard_map/reduce_scatter | solution.py:67
  1005.7 732.5 %all-reduce.8.cloned.1.call-start = ((), (), s32[]{:S(2)}) async-start(), calls=%async_computation.12 | async-start | bytes 100663296 | tf_op jit(solution)/shard_map/psum | solution.py:250
  1052.1 96.8 %copy-start.6 = (bf16[1024,512]{1,0:T(8,128)(2,1)S(1)}, bf16[1024,512]{1,0:T(8,128)(2,1)}, u32[]{:S(2)}) copy-start(bf16[1024,512]{1,0:T(8,128)(2,1)} %param.16) | copy-start | bytes 3145732
  1052.1 96.8 %copy-start.28 = (f32[1024]{0:T(1024)S(1)}, f32[1024]{0:T(1024)}, u32[]{:S(2)}) copy-start(f32[1024]{0:T(1024)} %copy-done.27) | copy-start | bytes 12292
  1052.1 96.8 %copy-start.30 = (f32[1024]{0:T(1024)S(1)}, f32[1024]{0:T(1024)}, u32[]{:S(2)}) copy-start(f32[1024]{0:T(1024)} %copy-done.29) | copy-start | bytes 12292
  1052.1 96.8 %copy-start.32 = (f32[512]{0:T(512)S(1)}, f32[512]{0:T(512)}, u32[]{:S(2)}) copy-start(f32[512]{0:T(512)} %param.19) | copy-start | bytes 6148
  1052.1 99.6 %copy-start.33 = (f32[512]{0:T(512)S(1)}, f32[512]{0:T(512)}, u32[]{:S(2)}) copy-start(f32[512]{0:T(512)} %get-tuple-element.383) | copy-start | bytes 6148
  1052.1 99.6 %copy-start.34 = (f32[512]{0:T(512)S(1)}, f32[512]{0:T(512)}, u32[]{:S(2)}) copy-start(f32[512]{0:T(512)} %get-tuple-element.389) | copy-start | bytes 6148
  1148.9 29.0 %copy-start.9 = (f32[1024,512]{1,0:T(8,128)S(1)}, f32[1024,512]{1,0:T(8,128)}, u32[]{:S(2)}) copy-start(f32[1024,512]{1,0:T(8,128)} %reduce-scatter.11.cloned.1.call-done) | copy-start | bytes 6291460
  (43 other events, 255.1 us)
Sparse Core Ops, SparseCore 0:
  25.5 78.9 all-gather.4
  180.7 142.9 reduce-scatter.4
  341.6 79.1 all-gather.6
  422.2 79.2 all-gather.8
  530.9 143.0 reduce-scatter.8
  676.7 77.6 reduce-scatter.6
  759.1 81.2 all-gather.10
  1005.8 142.9 reduce-scatter.10
  1154.9 583.2 all-reduce.7
where the time goes:
time: 1790 us; the launch traced here: 1780 us
  waiting for transfers between devices  1290 us (72%)
  matrix products  267 us (15%)
  local copies, waits for them, and re-layouts  79.9 us (4%)
  blocking collectives  62.5 us (3%)
  other arithmetic  50.1 us (3%)
    psum x1, waiting for transfers between devices, local(): lax.psum((grad_qkv, grad_proj, grad_attn_gain, grad_attn_bias, grad_up, g...  557 us
    reduce_scatter x2, waiting for transfers between devices, back_sum(): return lax.psum_scatter(partial_grad, 'mp', scatter_dimension=1, tiled=True)  224 us
    all_gather x2, waiting for transfers between devices, norm_forward(): lax.all_gather(normed, 'mp', axis=1, tiled=True)  156 us
    all_gather x2, waiting for transfers between devices, grad_rows(): return lax.all_gather(local_grad, 'mp', axis=1, tiled=True)  147 us
    reduce_scatter x1, waiting for transfers between devices, local(): lax.psum_scatter(attn_part, 'mp', scatter_dimension=1, tiled=True)  143 us
    reduce_scatter x1, waiting for transfers between devices, local(): lax.psum_scatter(ffn_part.astype(jnp.bfloat16), 'mp', scatter_dimension=1...  65.2 us
    unnamed x84, local copies, waits for them, and re-layouts  53.7 us
    dot_general x2, matrix products, back_block(): jnp.einsum('hqk,qhd->khd', grad_raw, q_block, preferred_element_type=jnp....  49.9 us
  transfers between devices with their start and end apart: 9, of which 9 were waited for; matrix products, arithmetic and copies ran while one was open for 5% of the time, Pallas kernels for 0%

commit v1 on v0

v1 whole, which is shorter than its diff:
```python
import functools

import jax
import jax.numpy as jnp
from jax import lax
from jax.experimental import pallas as pl
from jax.experimental.pallas import tpu as pltpu
from jax.sharding import PartitionSpec as P

HEAD_DIM = 128
FF = 8192
EPSILON = 1e-05
MASKED = -1e30
LONGEST_DOC = 512
QUERY_BLOCK = 256

bf16 = jnp.bfloat16
f32 = jnp.float32

NT = (((1,), (1,)), ((), ()))
TN = (((0,), (0,)), ((), ()))
NN = (((1,), (0,)), ((), ()))


def dot(a, b, dims):
    return lax.dot_general(a, b, dims, preferred_element_type=f32)


def block_probs(i, rot, seg_row, seg_col, block, scale):
    start = i * block
    low = max(0, start - LONGEST_DOC)
    high = start + block
    q = rot[0, start:high, :]
    k = rot[1, low:high, :]
    scores = dot(q, k, NT) * scale
    shape = scores.shape
    q_pos = start + lax.broadcasted_iota(jnp.int32, shape, 0)
    k_pos = low + lax.broadcasted_iota(jnp.int32, shape, 1)
    allowed = (seg_col[start:high, :] == seg_row[0][:, low:high]) & (k_pos <= q_pos)
    scores = jnp.where(allowed, scores, MASKED)
    expo = jnp.exp(scores - jnp.max(scores, axis=1, keepdims=True))
    return expo * (1.0 / jnp.sum(expo, axis=1, keepdims=True)), q, k, start, low, high


def attn_fwd_kernel(block, scale, q_lin, k_lin, v_lin, cosine, sine, seg_row, seg_col, att, rot):
    cos_t = cosine[...]
    sin_t = sine[...]
    for s, lin in ((0, q_lin), (1, k_lin)):
        z = lin[...]
        rot[s] = (z * cos_t + pltpu.roll(z, HEAD_DIM // 2, 1) * sin_t).astype(bf16)
    rot[2] = v_lin[...].astype(bf16)
    for i in range(q_lin.shape[0] // block):
        probs, _, _, start, low, high = block_probs(i, rot, seg_row, seg_col, block, scale)
        att[start:high, :] = dot(probs.astype(bf16), rot[2, low:high, :], NN).astype(bf16)


def attn_bwd_kernel(block, scale, rot, g_att, cosine, sine, seg_row, seg_col, grads, dk, dv):
    cos_t = cosine[...]
    sin_t = sine[...]
    cols = grads.shape[1] // 3
    at = pl.program_id(1) * HEAD_DIM
    dk[...] = jnp.zeros_like(dk)
    dv[...] = jnp.zeros_like(dv)

    def lanes(s):
        return pl.ds(pl.multiple_of(s * cols + at, HEAD_DIM), HEAD_DIM)

    def back(z, c, s):
        return (z * c - pltpu.roll(z, HEAD_DIM // 2, 1) * s).astype(bf16)

    for i in range(rot.shape[1] // block):
        probs, q, k, start, low, high = block_probs(i, rot, seg_row, seg_col, block, scale)
        g = g_att[start:high, :]
        g_probs = dot(g, rot[2, low:high, :], NT)
        delta = jnp.sum(probs * g_probs, axis=1, keepdims=True)
        g_raw = (probs * (g_probs - delta) * scale).astype(bf16)
        grads[start:high, lanes(0)] = back(
            dot(g_raw, k, NN), cos_t[start:high, :], sin_t[start:high, :]
        )
        dk[low:high, :] += dot(g_raw, q, TN)
        dv[low:high, :] += dot(probs.astype(bf16), g, TN)
    grads[:, lanes(1)] = back(dk[...], cos_t, sin_t)
    grads[:, lanes(2)] = dv[...].astype(bf16)


def attention_specs(row_len):
    triple = pl.BlockSpec((3, row_len, HEAD_DIM), lambda r, h: (0, r, h))
    plain = pl.BlockSpec((row_len, HEAD_DIM), lambda r, h: (r, h))
    table = pl.BlockSpec((row_len, HEAD_DIM), lambda r, h: (0, 0))
    seg_row = pl.BlockSpec((1, 1, row_len), lambda r, h: (r, 0, 0))
    seg_col = pl.BlockSpec((row_len, 1), lambda r, h: (r, 0))
    return triple, plain, table, seg_row, seg_col


def attn_forward(lin, cos_t, sin_t, segs):
    tokens = lin.shape[0]
    cols = lin.shape[1] // 3
    heads = cols // HEAD_DIM
    rows, row_len = segs.shape
    triple, plain, table, seg_row, seg_col = attention_specs(row_len)
    block = min(QUERY_BLOCK, row_len)
    parts = [
        pl.BlockSpec((row_len, HEAD_DIM), lambda r, h, s=s: (r, s * heads + h)) for s in range(3)
    ]
    return pl.pallas_call(
        functools.partial(attn_fwd_kernel, block, HEAD_DIM**-0.5),
        grid=(rows, heads),
        in_specs=[*parts, table, table, seg_row, seg_col],
        out_specs=[plain, triple],
        out_shape=[
            jax.ShapeDtypeStruct((tokens, cols), bf16),
            jax.ShapeDtypeStruct((3, tokens, cols), bf16),
        ],
        compiler_params=pltpu.CompilerParams(vmem_limit_bytes=32 * 2**20),
    )(lin, lin, lin, cos_t, sin_t, segs[:, None, :], segs.reshape(tokens, 1))


def attn_backward(rot, g_att, cos_t, sin_t, segs):
    _, tokens, cols = rot.shape
    rows, row_len = segs.shape
    triple, plain, table, seg_row, seg_col = attention_specs(row_len)
    block = min(QUERY_BLOCK, row_len)
    return pl.pallas_call(
        functools.partial(attn_bwd_kernel, block, HEAD_DIM**-0.5),
        grid=(rows, cols // HEAD_DIM),
        in_specs=[triple, plain, table, table, seg_row, seg_col],
        out_specs=pl.BlockSpec((row_len, 3 * cols), lambda r, h: (r, 0)),
        out_shape=jax.ShapeDtypeStruct((tokens, 3 * cols), bf16),
        scratch_shapes=[pltpu.VMEM((row_len, HEAD_DIM), f32)] * 2,
        compiler_params=pltpu.CompilerParams(vmem_limit_bytes=32 * 2**20),
    )(rot, g_att, cos_t, sin_t, segs[:, None, :], segs.reshape(tokens, 1))


def after(value, *deps):
    return lax.optimization_barrier((value,) + deps)[0]


def join_kernel(n, chunks, *refs):
    per = 2 * n - 1
    out, sem = refs[chunks * per], refs[chunks * per + 1]
    me = lax.axis_index("mp")
    at = 0
    for c in range(chunks):
        own, right, left = refs[c * per], refs[c * per + 1 : c * per + n], refs[c * per + n : c * per + per]
        rows, cols = own.shape

        def put(src, block, at=at, rows=rows, cols=cols):
            target = out.at[
                pl.ds(at, rows), pl.ds(pl.multiple_of(block * cols, cols), cols)
            ]
            pltpu.make_async_copy(src, target, sem).start()

        at += rows
        put(own, me)
        for s in range(1, n):
            pl.when(me >= s)(functools.partial(put, right[s - 1], me - s))
            pl.when(me + s < n)(functools.partial(put, left[s - 1], me + s))
    pltpu.make_async_copy(out, out, sem).wait()


def join(parts):
    n = lax.axis_size("mp")
    rows = sum(p[0].shape[0] for p in parts)
    flat = [a for own, right, left in parts for a in (own, *right, *left)]
    shape = (rows, n * parts[0][0].shape[1])
    return pl.pallas_call(
        functools.partial(join_kernel, n, len(parts)),
        in_specs=[pl.BlockSpec(memory_space=pl.ANY)] * len(flat),
        out_specs=pl.BlockSpec(memory_space=pltpu.VMEM),
        out_shape=jax.ShapeDtypeStruct(shape, parts[0][0].dtype),
        scratch_shapes=[pltpu.SemaphoreType.DMA(())],
        compiler_params=pltpu.CompilerParams(vmem_limit_bytes=32 * 2**20),
    )(*flat)


def line_step(s, right, left):
    n = lax.axis_size("mp")
    return (
        lax.ppermute(right, "mp", [(i, i + 1) for i in range(s - 1, n - 1)]),
        lax.ppermute(left, "mp", [(i, i - 1) for i in range(1, n - s + 1)]),
    )


def line_parts(block, first=None):
    right = left = block
    rights, lefts = [], []
    for s in range(1, lax.axis_size("mp")):
        if s == 1 and first is not None:
            right, left = first
        else:
            right, left = line_step(s, right, left)
        rights.append(right)
        lefts.append(left)
    return block, rights, lefts


def line_gather(chunks):
    return join([line_parts(c) for c in chunks])


def split_rows(x, chunks=2):
    return jnp.split(x, chunks, axis=0)


def line_scatter(chunks, beside=()):
    n = lax.axis_size("mp")
    me = lax.axis_index("mp")
    cols = chunks[0].shape[1] // n

    def block(y, j):
        return lax.dynamic_slice_in_dim(y, jnp.clip(j, 0, n - 1) * cols, cols, 1)

    def add(*terms):
        return sum(t.astype(f32) for t in terms)

    pairs = [(block(y, me + n - 1), block(y, me - n + 1)) for y in chunks]
    for s in range(1, n):
        pairs = [
            (
                lax.ppermute(right, "mp", [(i, i + 1) for i in range(s)]),
                lax.ppermute(left, "mp", [(i, i - 1) for i in range(n - s, n)]),
            )
            for right, left in pairs
        ]
        if s < n - 1:
            pairs = [
                (
                    add(right, block(y, me + n - s - 1)).astype(bf16),
                    add(left, block(y, me - n + s + 1)).astype(bf16),
                )
                for (right, left), y in zip(pairs, chunks)
            ]
            if s <= len(beside):
                pairs = [tuple(after(a, beside[s - 1]) for a in pair) for pair in pairs]
    sums = [add(right, left, block(y, me)) for (right, left), y in zip(pairs, chunks)]
    return jnp.concatenate(sums) if len(sums) > 1 else sums[0]


class Halving:
    def __init__(self, make):
        size = lax.axis_size("dp")
        me = lax.axis_index("dp")
        odd = me & 1
        self.odd = odd
        rest = list(range(1, size.bit_length() - 1))
        steps = []
        for even_bit, odd_bit in zip(rest, rest[1:] + rest[:1]):
            bit = jnp.where(odd == 1, (me >> odd_bit) & 1, (me >> even_bit) & 1)
            steps.append(((even_bit, odd_bit), bit))
        self.todo = [(True, *s) for s in steps] + [(False, *s) for s in reversed(steps)]
        sent = make(1 - odd)
        self.x = kept = make(after(odd, sent))
        self.flight = (True, odd, kept, self.exchange(sent, (0, 0)))
        self.last = None

    def exchange(self, x, bits):
        size = lax.axis_size("dp")
        return lax.ppermute(x, "dp", [(i, i ^ (1 << bits[i & 1])) for i in range(size)])

    def launch(self):
        if self.flight is not None or self.last is not None:
            return
        if not self.todo:
            self.last = self.exchange(self.x, (0, 0))
            return
        halve, bits, bit = self.todo.pop(0)
        kept = sent = self.x
        if halve:
            half = self.x.shape[0] // 2
            kept = lax.dynamic_slice_in_dim(self.x, bit * half, half, 0)
            sent = lax.dynamic_slice_in_dim(self.x, (1 - bit) * half, half, 0)
        self.flight = (halve, bit, kept, self.exchange(sent, bits))

    def land(self):
        if self.flight is None:
            return
        halve, bit, kept, got = self.flight
        if halve:
            self.x = (kept.astype(f32) + got.astype(f32)).astype(bf16)
        else:
            self.x = jnp.where(
                bit == 0, jnp.concatenate([kept, got]), jnp.concatenate([got, kept])
            )
        self.flight = None

    def finish(self, groups=1):
        while self.last is None:
            self.land()
            self.launch()
        return widen(self.x, self.last, self.odd, groups)


def widen_kernel(odd, own, other, out):
    groups, _, cols = out.shape

    def put(src):
        for g in range(groups):
            out[g] = src[:, g * cols : (g + 1) * cols].astype(f32)

    pl.when(pl.program_id(0) == 0)(functools.partial(put, own))
    pl.when(pl.program_id(0) == 1)(functools.partial(put, other))


def widen(own, other, odd, groups):
    rows, cols = own.shape
    block = min(256, rows)
    count = rows // block
    wide = cols // groups
    return pl.pallas_call(
        widen_kernel,
        grid_spec=pltpu.PrefetchScalarGridSpec(
            num_scalar_prefetch=1,
            grid=(2, count),
            in_specs=[
                pl.BlockSpec((block, cols), lambda k, r, odd: (jnp.where(k == 0, r, count - 1), 0)),
                pl.BlockSpec((block, cols), lambda k, r, odd: (jnp.where(k == 1, r, 0), 0)),
            ],
            out_specs=pl.BlockSpec(
                (groups, block, wide),
                lambda k, r, odd: (0, jnp.where(k == 0, odd[0], 1 - odd[0]) * count + r, 0),
            ),
        ),
        out_shape=jax.ShapeDtypeStruct((groups, 2 * rows, wide), f32),
        compiler_params=pltpu.CompilerParams(vmem_limit_bytes=32 * 2**20),
    )(odd.reshape(1).astype(jnp.int32), own, other)


def half_lanes(x, half):
    size = x.shape[1] // 2
    return lax.dynamic_slice_in_dim(x, half * size, size, 1)


def meet(values, *sums):
    for h in sums:
        h.land()
    met = lax.optimization_barrier((*values, *(h.x for h in sums)))
    for h, x in zip(sums, met[len(values) :]):
        h.x = x
        h.launch()
    return met[: len(values)]


def butterfly_sum(x, axis):
    size = lax.axis_size(axis)
    for bit in range(size.bit_length() - 1):
        x = x + lax.ppermute(x, axis, [(i, i ^ (1 << bit)) for i in range(size)])
    return x


def split_bits(v):
    high = lax.reduce_precision(v, 8, 7)
    return [high.astype(bf16), (v - high).astype(bf16)]


def normalize(v):
    mean = jnp.mean(v, axis=1, keepdims=True)
    centred = v - mean
    rstd = lax.rsqrt(jnp.mean(centred * centred, axis=1, keepdims=True) + EPSILON)
    return centred * rstd, rstd


def local(
    inputs,
    segment_ids,
    width_bucket,
    attn_gain,
    attn_bias,
    qkv_weight,
    proj_weight,
    ffn_gain,
    ffn_bias,
    up_weight,
    down_weight,
    grad_result,
):
    tokens, feats = inputs.shape
    row_len = segment_ids.shape[1]
    mp_size = lax.axis_size("mp")
    dp_size = lax.axis_size("dp")
    mp_idx = lax.axis_index("mp")
    width = feats * mp_size

    def own(a):
        return lax.dynamic_slice_in_dim(a, mp_idx * feats, feats, a.ndim - 1)

    half = HEAD_DIM // 2
    freqs = jnp.power(10000.0, -jnp.arange(half, dtype=f32) / half)
    angles = jnp.arange(row_len, dtype=f32)[:, None] * freqs[None, :]
    cos_h, sin_h = jnp.cos(angles), jnp.sin(angles)
    cos_t = jnp.concatenate([cos_h, cos_h], axis=1)
    sin_t = jnp.concatenate([-sin_h, sin_h], axis=1)

    vectors = sum((split_bits(v) for v in (attn_gain, attn_bias, ffn_gain, ffn_bias)), [])
    packed = jnp.concatenate([jnp.stack(vectors), jnp.zeros((8, feats), bf16)])
    first, second = split_rows(inputs)
    chunks = [first, jnp.concatenate([second, packed])]
    starts = [line_step(1, c, c) for c in chunks]
    gathered = join([line_parts(c, pair) for c, pair in zip(chunks, starts)])
    vec = gathered[tokens : tokens + 8].astype(f32)
    gain_a, bias_a, gain_f, bias_f = (vec[2 * i] + vec[2 * i + 1] for i in range(4))
    x = gathered[:tokens].astype(f32)
    gy_first, gy_second = split_rows(grad_result)
    gy_first = lax.all_gather(after(gy_first, gathered), "mp", axis=1, tiled=True)

    part = width // dp_size
    slab = lax.dynamic_slice_in_dim(proj_weight, lax.axis_index("dp") * part, part, 1)
    slab = lax.all_gather(slab, "mp", axis=0, tiled=True)
    proj_full = lax.all_gather(after(slab, starts[0][0]), "dp", axis=1, tiled=True)

    qkv_all = jnp.concatenate([qkv_weight[s] for s in range(3)], axis=1)
    xhat_a, rstd_a = normalize(x)
    attn_rows = (xhat_a * gain_a + bias_a).astype(bf16)
    att, rot = attn_forward(dot(attn_rows, qkv_all, NN), cos_t, sin_t, segment_ids)
    att_full, gy_first = lax.optimization_barrier((line_gather(split_rows(att)), gy_first))
    gy_second = lax.all_gather(after(gy_second, att_full), "mp", axis=1, tiled=True)

    mid = x + dot(att_full, after(proj_full, att_full), NN)
    xhat_f, rstd_f = normalize(mid)
    ffn_rows = (xhat_f * gain_f + bias_f).astype(bf16)

    limit = (width_bucket.reshape(tokens) + 1) * (FF // 4)
    columns = mp_idx * up_weight.shape[1] + jnp.arange(up_weight.shape[1], dtype=jnp.int32)
    keep = columns[None, :] < limit[:, None]
    hidden = dot(ffn_rows, up_weight, NN)
    relu = jnp.where(keep, jnp.maximum(hidden, 0.0), 0.0)
    active = (relu * relu).astype(bf16)

    gy_first = after(gy_first, active)
    halves = []
    for g, r in zip((gy_first, gy_second), split_rows(relu)):
        halves.append((2.0 * r * dot(g, down_weight, NT)).astype(bf16))
        gy_second = after(gy_second, halves[0])
    grad_hidden = jnp.concatenate(halves)
    g_ffn_part = dot(grad_hidden, up_weight, NT).astype(bf16)
    g_ffn_own = lax.psum_scatter(g_ffn_part, "mp", scatter_dimension=1, tiled=True)

    active, gy_first, gy_second = (after(a, g_ffn_part) for a in (active, gy_first, gy_second))
    gy = jnp.concatenate([gy_first, gy_second])
    down = Halving(lambda half: dot(half_lanes(active, half), gy, TN).astype(bf16))
    grad_up = dot(after(ffn_rows, down.x), grad_hidden, TN).astype(bf16)
    (grad_up,) = meet((grad_up,), down)
    grad_up = lax.psum(grad_up, "dp")
    ffn_part = dot(after(active, down.x), down_weight, NN).astype(bf16)
    g_ffn_own, ffn_part = lax.optimization_barrier((g_ffn_own, ffn_part))
    chunks = split_rows(g_ffn_own)
    (chunks[0],) = meet((chunks[0],), down)
    parts = [(c, [], []) for c in chunks]
    ends = [(c, c) for c in chunks]
    for s in range(1, mp_size):
        ends = [line_step(s, *pair) for pair in ends]
        if s < mp_size - 1:
            ends[0] = meet(ends[0], down)
        for (_, rights, lefts), (right, left) in zip(parts, ends):
            rights.append(right)
            lefts.append(left)
    (g_ffn,) = meet((join(parts),), down)
    ffn_part = after(ffn_part, g_ffn)
    ffn_out = lax.psum_scatter(ffn_part, "mp", scatter_dimension=1, tiled=True)
    g_ffn = g_ffn.astype(f32)

    scaled = g_ffn * gain_f
    grad_mid = gy.astype(f32) + rstd_f * (
        scaled
        - jnp.mean(scaled, axis=1, keepdims=True)
        - xhat_f * jnp.mean(scaled * xhat_f, axis=1, keepdims=True)
    )
    grad_mid_low = grad_mid.astype(bf16)
    g_att = dot(grad_mid_low, proj_weight, NT).astype(bf16)
    (g_att,) = meet((g_att,), down)
    g_qkv_rows = attn_backward(rot, g_att, cos_t, sin_t, segment_ids)
    qkv = Halving(lambda half: dot(half_lanes(attn_rows, half), g_qkv_rows, TN).astype(bf16))
    later = after(g_qkv_rows, qkv.x)
    g_attn_part = dot(later, qkv_all, NT)
    g_attn_low = g_attn_part.astype(bf16)
    (g_attn_low,) = meet((g_attn_low,), qkv)
    g_attn = lax.psum_scatter(g_attn_low, "mp", scatter_dimension=1, tiled=True).astype(f32)
    mid_later = after(grad_mid_low, g_attn_low)
    proj = Halving(lambda half: dot(half_lanes(att, half), mid_later, TN).astype(bf16))
    grad_down = down.finish()[0]
    grad_qkv, grad_proj = qkv.finish(3), proj.finish()[0]

    part_scaled = g_attn_part * gain_a
    sums = butterfly_sum(
        jnp.stack([jnp.sum(part_scaled, axis=1), jnp.sum(part_scaled * xhat_a, axis=1)]), "mp"
    )
    sum_plain, sum_cross = sums[0][:, None], sums[1][:, None]
    g_ffn_mine = g_ffn_own.astype(f32)
    ffn_vec = jnp.stack(
        [jnp.sum(g_ffn_mine * own(xhat_f), axis=0), jnp.sum(g_ffn_mine, axis=0)]
    )
    attn_vec = jnp.stack([jnp.sum(g_attn_part * xhat_a, axis=0), jnp.sum(g_attn_part, axis=0)])
    attn_vec = own(butterfly_sum(attn_vec, "mp"))
    grad_vec = butterfly_sum(jnp.concatenate([attn_vec, ffn_vec]), "dp")
    grad_input = own(grad_mid) + rstd_a * (
        g_attn * attn_gain - sum_plain / width - own(xhat_a) * (sum_cross / width)
    )
    block_output = (own(mid) + ffn_out.astype(f32)).astype(bf16)
    return (
        block_output,
        grad_input,
        grad_vec[0],
        grad_vec[1],
        grad_qkv,
        grad_proj,
        grad_vec[2],
        grad_vec[3],
        grad_up.astype(f32),
        grad_down,
    )


def solution(mesh):
    placed = (
        P("dp", "mp"),
        P("dp", None),
        P("dp", None),
        P("mp"),
        P("mp"),
        P(None, None, "mp"),
        P("mp", None),
        P("mp"),
        P("mp"),
        P(None, "mp"),
        P("mp", None),
        P("dp", "mp"),
    )
    return jax.shard_map(
        local,
        mesh=mesh,
        in_specs=placed,
        out_specs=(
            P("dp", "mp"),
            P("dp", "mp"),
            P("mp"),
            P("mp"),
            P(None, None, "mp"),
            P("mp", None),
            P("mp"),
            P("mp"),
            P(None, "mp"),
            P("mp", None),
        ),
        check_vma=False,
    )
```

time: 1790 us -> 747 us (0.42)
  waiting for transfers between devices: 1290 us -> 277 us
  matrix products: 267 us -> 142 us
  starting transfers between devices: 0.37 us -> 104 us
  blocking collectives: 62.5 us -> 0 us
  Pallas kernels: 0 us -> 53 us
  other arithmetic: 50.1 us -> 88.9 us
  local copies, waits for them, and re-layouts: 79.9 us -> 54.2 us
    psum x1, waiting for transfers between devices: 557 us -> 0.01 us  [local(): grad_up = lax.psum(grad_up, 'dp')]
    reduce_scatter x4 -> x3, waiting for transfers between devices: 432 us -> 12.1 us  [the longest x1 12.1 us: local(): lax.psum_scatter(g_ffn_part, 'mp', scatter_dimension=1, tiled=True)]
    all_gather x4, waiting for transfers between devices: 303 us -> 2.14 us  [the longest x1 2.1 us: local(): lax.all_gather(after(gy_second, att_full), 'mp', axis=1, tiled=True)]
    ppermute x0 -> x61, waiting for transfers between devices: none -> 262 us  [the longest x18 148 us: line_step(): lax.ppermute(left, 'mp', [(i, i - 1) for i in range(1, n - s + 1)])]
    dot_general x26 -> x16, matrix products: 267 us -> 142 us  [dot(): return lax.dot_general(a, b, dims, preferred_element_type=f32)]
    ppermute x0 -> x61, starting transfers between devices: none -> 104 us  [the longest x18 47.1 us: line_step(): lax.ppermute(right, 'mp', [(i, i + 1) for i in range(s - 1, n - 1)])]
    psum x5 -> x0, blocking collectives: 62.5 us -> none  [the longest x2 25 us: norm_forward(): lax.psum((jnp.sum(local_rows, axis=1), jnp.sum(local_rows * local_rows, a...]
    pallas_call x0 -> x8, Pallas kernels: none -> 53 us  [the longest x3 21.2 us: widen(): pl.pallas_call(widen_kernel, grid_spec=pltpu.PrefetchScalarGridSpec(num_s...]
  transfers between devices with their start and end apart: 9 -> 69, of which waited for: 9 -> 31; matrix products, arithmetic and copies ran while one was open for 5% -> 29% of each run, Pallas kernels for 0% -> 7%
where the time goes in v1:
time: 747 us; the launch traced here: 735 us
  waiting for transfers between devices  277 us (37%)
  matrix products  142 us (19%)
  starting transfers between devices  104 us (14%)
  other arithmetic  88.9 us (12%)
  local copies, waits for them, and re-layouts  54.2 us (7%)
  Pallas kernels  53 us (7%)
  between operations  15.7 us (2%)
    ppermute x18, waiting for transfers between devices, line_step(): lax.ppermute(left, 'mp', [(i, i - 1) for i in range(1, n - s + 1)])  148 us
    dot_general x16, matrix products, dot(): return lax.dot_general(a, b, dims, preferred_element_type=f32)  142 us
    ppermute x18, waiting for transfers between devices, exchange(): lax.ppermute(x, 'dp', [(i, i ^ 1 << bits[i & 1]) for i in range(size)])  102 us
    ppermute x18, starting transfers between devices, line_step(): lax.ppermute(right, 'mp', [(i, i + 1) for i in range(s - 1, n - 1)])  47.1 us
    unnamed x131, local copies, waits for them, and re-layouts  31.9 us
    ppermute x18, starting transfers between devices, line_step(): lax.ppermute(left, 'mp', [(i, i - 1) for i in range(1, n - s + 1)])  23.4 us
    select_n x6, other arithmetic, land(): jnp.where(bit == 0, jnp.concatenate([kept, got]), jnp.concatenate([got, k...  21.4 us
    pallas_call x3, Pallas kernels, widen(): pl.pallas_call(widen_kernel, grid_spec=pltpu.PrefetchScalarGridSpec(num_s...  21.2 us
  transfers between devices with their start and end apart: 69, of which 31 were waited for; matrix products, arithmetic and copies ran while one was open for 29% of the time, Pallas kernels for 7%

profile of v1, /device:TPU:0, one launch (start us, length us, event | category | flops | bytes accessed | tf_op | source)
XLA Modules:
  0.0 735.2 jit_solution(2826699124423478779)
XLA Ops:
  43.4 25.7 %collective-permute-done.10.refs_12_ = bf16[528,512]{1,0:T(8,128)(2,1)S(1)} collective-permute-done((bf16[528,512]{1,0:T(8,128)(2,1)}, bf16[528,512]{1,0:T(8,128)(2,1)S(1)}, u32[]{:S(2)}, u32[]{:S(2)}) %collective-permute-start.10) | collective-permute-done | bytes 540704 | tf_op jit(solution)/shard_map/ppermute | solution.py:180
  84.6 18.2 %collective-permute-done.5.refs_6_ = bf16[512,512]{1,0:T(8,128)(2,1)S(1)} collective-permute-done((bf16[512,512]{1,0:T(8,128)(2,1)S(1)}, bf16[512,512]{1,0:T(8,128)(2,1)S(1)}, u32[]{:S(2)}, u32[]{:S(2)}) %collective-permute-start.5) | collective-permute-done | bytes 524320 | tf_op jit(solution)/shard_map/ppermute | solution.py:180
  124.8 11.9 %shard_map.196 = (bf16[1024,512]{1,0:T(8,128)(2,1)S(1)}, bf16[3,1024,512]{2,1,0:T(8,128)(2,1)S(1)}) custom-call(f32[1024,1536]{1,0:T(8,128)S(1)} %fusion.10.q_lin.k_lin.v_lin, f32[1024,1536]{1,0:T(8,128)S(1)} %fusion.10.q_lin.k_lin.v_lin, f32[1024,1536]{1,0:T(8,128)S(1)} %fusion.10.q_lin.k_lin.v_lin, f32[1024,128]{1,0:T(8,128)S(1)} %get-tuple-element.143.cosine, ...), custom_call_target="tpu_custom_call" | custom-call | tf_op jit(solution)/shard_map/pallas_call | solution.py:105
  151.1 12.8 %collective-permute-done.21.refs_11_ = bf16[512,512]{1,0:T(8,128)(2,1)S(1)} collective-permute-done((bf16[512,512]{1,0:T(8,128)(2,1)S(1)}, bf16[512,512]{1,0:T(8,128)(2,1)S(1)}, u32[]{:S(2)}, u32[]{:S(2)}) %collective-permute-start.21) | collective-permute-done | bytes 524320 | tf_op jit(solution)/shard_map/ppermute | solution.py:180
  209.0 11.0 %collective-permute-done.17.refs_6_ = bf16[512,512]{1,0:T(8,128)(2,1)} collective-permute-done((bf16[512,512]{1,0:T(8,128)(2,1)}, bf16[512,512]{1,0:T(8,128)(2,1)}, u32[]{:S(2)}, u32[]{:S(2)}) %collective-permute-start.17) | collective-permute-done | bytes 524320 | tf_op jit(solution)/shard_map/ppermute | solution.py:180
  229.0 13.3 %fusion.47 = (f32[1024]{0:T(1024)S(1)}, f32[1024,2048]{1,0:T(8,128)S(1)}) fusion(bf16[1024,2048]{1,0:T(8,128)(2,1)} %copy-done.8, bf16[2048,2048]{1,0:T(8,128)(2,1)} %all-gather.9.cloned.1.call-done, bf16[1040,2048]{1,0:T(8,128)(2,1)} %copy-done.1), kind=kOutput, calls=%fused_computation.137 | convolution fusion | flops 8596225024 | bytes 25169920 | tf_op jit(solution)/shard_map/dot_general | solution.py:26
  250.8 11.9 %multiply_convert_fusion = (bf16[1024,2048]{1,0:T(8,128)(2,1)}, f32[1024,2048]{1,0:T(8,128)}) fusion(bf16[1024,2048]{1,0:T(8,128)(2,1)S(1)} %get-tuple-element.64, bf16[2048,2048]{1,0:T(8,128)(2,1)S(1)} %bitcast.86, s32[1024]{0:T(1024)S(1)} %bitcast.80, s32[2048]{0:T(1024)S(1)} %iota_add_fusion), kind=kOutput, calls=%fused_computation.13 | convolution fusion | flops 8600420352 | bytes 25178112 | tf_op jit(solution)/shard_map/dot_general | solution.py:26
  262.7 10.2 %fusion.7 = bf16[512,2048]{1,0:T(8,128)(2,1)} fusion(f32[1024,2048]{1,0:T(8,128)} %get-tuple-element.139, bf16[512,2048]{1,0:T(8,128)(2,1)S(1)} %copy-done.40, bf16[2048,2048]{1,0:T(8,128)(2,1)} %param.22), kind=kOutput, calls=%fused_computation.28 | convolution fusion | flops 4298113024 | bytes 16777216 | tf_op jit(solution)/shard_map/dot_general | solution.py:26
  275.0 9.8 %fusion.5 = bf16[512,2048]{1,0:T(8,128)(2,1)S(1)} fusion(f32[1024,2048]{1,0:T(8,128)} %get-tuple-element.139, bf16[512,2048]{1,0:T(8,128)(2,1)} %all-gather.11.cloned.1.call-done, bf16[2048,2048]{1,0:T(8,128)(2,1)} %param.22), kind=kOutput, calls=%fused_computation.25 | convolution fusion | flops 4298113024 | bytes 16777216 | tf_op jit(solution)/shard_map/dot_general | solution.py:26
  286.1 12.9 %convolution_convert_fusion.2 = bf16[1024,2048]{1,0:T(8,128)(2,1)} fusion(bf16[2048,2048]{1,0:T(8,128)(2,1)} %param.21, bf16[512,2048]{1,0:T(8,128)(2,1)S(1)} %fusion.5, bf16[512,2048]{1,0:T(8,128)(2,1)S(1)} %copy-done.57), kind=kOutput, calls=%fused_computation.33 | convolution fusion | flops 8600420352 | bytes 16777216 | tf_op jit(solution)/shard_map/dot_general | solution.py:26
  316.2 10.7 %add_convert_fusion = bf16[1024,2048]{1,0:T(8,128)(2,1)} fusion(bf16[1024,2048]{1,0:T(8,128)(2,1)} %collective-permute-done.24, bf16[1024,2048]{1,0:T(8,128)(2,1)} %copy-done.32, bf16[1024,2048]{1,0:T(8,128)(2,1)} %get-tuple-element.66, s32[]{:T(128)S(6)} %select_n.121), kind=kOutput, calls=%fused_computation.12 | convolution fusion | flops 4305453056 | bytes 14680068 | tf_op jit(solution)/shard_map/dot_general | solution.py:26
  326.9 11.6 %convolution_convert_fusion = bf16[2048,2048]{1,0:T(8,128)(2,1)} fusion(bf16[1024,2048]{1,0:T(8,128)(2,1)S(1)} %copy-done.39, bf16[512,2048]{1,0:T(8,128)(2,1)S(1)} %copy-done.60, bf16[512,2048]{1,0:T(8,128)(2,1)S(1)} %copy-done.58), kind=kOutput, calls=%fused_computation.20 | convolution fusion | flops 8602517504 | bytes 16777216 | tf_op jit(solution)/shard_map/dot_general | solution.py:26
  343.1 13.8 %convolution_convert_fusion.1 = bf16[1024,2048]{1,0:T(8,128)(2,1)} fusion(bf16[1024,2048]{1,0:T(8,128)(2,1)} %get-tuple-element.66, bf16[2048,2048]{1,0:T(8,128)(2,1)} %param.22), kind=kOutput, calls=%fused_computation.32 | convolution fusion | flops 8592031744 | bytes 16777216 | tf_op jit(solution)/shard_map/dot_general | solution.py:26
  357.0 11.0 %collective-permute-done.25 = bf16[512,2048]{1,0:T(8,128)(2,1)} collective-permute-done((bf16[512,2048]{1,0:T(8,128)(2,1)}, bf16[512,2048]{1,0:T(8,128)(2,1)}, u32[]{:S(2)}, u32[]{:S(2)}) %collective-permute-start.25) | collective-permute-done | bytes 2097184 | tf_op jit(solution)/shard_map/ppermute | solution.py:258
  372.5 12.1 %reduce-scatter.4.cloned.1.call-done = bf16[1024,512]{1,0:T(8,128)(2,1)} async-done(((bf16[1024,2048]{1,0:T(8,128)(2,1)}), bf16[1024,512]{1,0:T(8,128)(2,1)}) %reduce-scatter.4.cloned.1.call-update) | async-done | bytes 1048592 | tf_op jit(solution)/shard_map/reduce_scatter | solution.py:435
  411.5 21.1 %collective-permute-done.31 = bf16[256,2048]{1,0:T(8,128)(2,1)} collective-permute-done((bf16[256,2048]{1,0:T(8,128)(2,1)}, bf16[256,2048]{1,0:T(8,128)(2,1)}, u32[]{:S(2)}, u32[]{:S(2)}) %collective-permute-start.31) | collective-permute-done | bytes 1048608 | tf_op jit(solution)/shard_map/ppermute | solution.py:258
  470.2 11.5 %collective-permute-done.39.refs_13_ = bf16[512,512]{1,0:T(8,128)(2,1)} collective-permute-done((bf16[512,512]{1,0:T(8,128)(2,1)}, bf16[512,512]{1,0:T(8,128)(2,1)}, u32[]{:S(2)}, u32[]{:S(2)}) %collective-permute-start.39) | collective-permute-done | bytes 524320 | tf_op jit(solution)/shard_map/ppermute | solution.py:180
  518.0 14.9 %shard_map.199 = bf16[1024,1536]{1,0:T(8,128)(2,1)S(1)} custom-call(bf16[3,1024,512]{2,1,0:T(8,128)(2,1)S(1)} %copy-done.10, bf16[1024,512]{1,0:T(8,128)(2,1)S(1)} %convolution_convert_fusion.9.g_att, f32[1024,128]{1,0:T(8,128)S(1)} %copy-done.5, f32[1024,128]{1,0:T(8,128)S(1)} %copy-done.7, s32[1,1,1024]{2,1,0:T(1,128)S(1)} %bitcast.54, ...), custom_call_target="tpu_custom_call" | custom-call | tf_op jit(solution)/shard_map/pallas_call | solution.py:123
  545.9 13.2 %multiply_reduce_fusion = (f32[2048]{0:T(1024)S(1)}, f32[1024]{0:T(1024)S(1)}, f32[1024]{0:T(1024)S(1)}, f32[2048]{0:T(1024)S(1)}, bf16[1024,2048]{1,0:T(8,128)(2,1)}, /*index=5*/f32[1024,2048]{1,0:T(8,128)}) fusion(f32[1024]{0:T(1024)S(1)} %copy-done.49, f32[1024]{0:T(1024)S(1)} %copy-done.51, bf16[1040,2048]{1,0:T(8,128)(2,1)} %copy-done.1, ...), kind=kOutput, calls=%fused_computation.6 | convolution fusion | flops 6484387840 | bytes 26255360 | tf_op jit(solution)/shard_map/dot_general | solution.py:26
  565.2 20.4 %collective-permute-done.49 = bf16[512,1536]{1,0:T(8,128)(2,1)S(1)} collective-permute-done((bf16[512,1536]{1,0:T(8,128)(2,1)S(1)}, bf16[512,1536]{1,0:T(8,128)(2,1)S(1)}, u32[]{:S(2)}, u32[]{:S(2)}) %collective-permute-start.49) | collective-permute-done | bytes 1572896 | tf_op jit(solution)/shard_map/ppermute | solution.py:258
  590.6 10.3 %collective-permute-done.50 = bf16[256,1536]{1,0:T(8,128)(2,1)} collective-permute-done((bf16[256,1536]{1,0:T(8,128)(2,1)}, bf16[256,1536]{1,0:T(8,128)(2,1)}, u32[]{:S(2)}, u32[]{:S(2)}) %collective-permute-start.50) | collective-permute-done | bytes 786464 | tf_op jit(solution)/shard_map/ppermute | solution.py:258
  626.0 19.3 %collective-permute-done.55 = bf16[128,2048]{1,0:T(8,128)(2,1)S(1)} collective-permute-done((bf16[128,2048]{1,0:T(8,128)(2,1)S(1)}, bf16[128,2048]{1,0:T(8,128)(2,1)S(1)}, u32[]{:S(2)}, u32[]{:S(2)}) %collective-permute-start.55) | collective-permute-done | bytes 524320 | tf_op jit(solution)/shard_map/ppermute | solution.py:258
  657.2 11.9 %convert_element_type.243 = f32[2048,2048]{1,0:T(8,128)} convert(bf16[2048,2048]{1,0:T(8,128)(2,1)} %all-reduce.2.cloned.1.call-done) | non-fusion elementwise | flops 4194304 | bytes 25165824 | tf_op jit(solution)/shard_map/convert_element_type | solution.py:507
  699.1 9.6 %shard_map.202 = f32[1,2048,2048]{2,1,0:T(8,128)} custom-call(s32[1]{0:T(128)} %bitcast.20.odd, bf16[1024,2048]{1,0:T(8,128)(2,1)S(1)} %copy-done.3, bf16[1024,2048]{1,0:T(8,128)(2,1)} %collective-permute-done.60.other), custom_call_target="tpu_custom_call" | custom-call | tf_op jit(solution)/shard_map/pallas_call | solution.py:309
  (356 shorter events, 390.7 us)
Async XLA Ops:
  7.2 99.2 %all-gather.7.cloned.1.call-start = ((), (), s32[]{:S(2)}) async-start(), calls=%async_computation.4 | async-start | bytes 1310720 | tf_op jit(solution)/shard_map/all_gather | solution.py:407
  9.4 32.0 %collective-permute-start.3 = (bf16[512,512]{1,0:T(8,128)(2,1)S(1)}, bf16[512,512]{1,0:T(8,128)(2,1)}, u32[]{:S(2)}, u32[]{:S(2)}) collective-permute-start(bf16[512,512]{1,0:T(8,128)(2,1)S(1)} %get-tuple-element.114.refs_0_), channel_id=1, source_target_pairs={{1,0},{2,1},{3,2},{5,4},{6,5},{7,6},{9,8},{10,9},{11,10},{13,12},{... | collective-permute-start | bytes 1572872 | tf_op jit(solution)/shard_map/ppermute | solution.py:180
  10.7 32.0 %collective-permute-start = (bf16[512,512]{1,0:T(8,128)(2,1)S(1)}, bf16[512,512]{1,0:T(8,128)(2,1)}, u32[]{:S(2)}, u32[]{:S(2)}) collective-permute-start(bf16[512,512]{1,0:T(8,128)(2,1)S(1)} %get-tuple-element.114.refs_0_), channel_id=1, source_target_pairs={{0,1},{1,2},{2,3},{4,5},{5,6},{6,7},{8,9},{9,10},{10,11},{12,13},{... | collective-permute-start | bytes 1572872 | tf_op jit(solution)/shard_map/ppermute | solution.py:179
  29.3 199.6 %all-gather.5.cloned.1.call-start = ((), (), s32[]{:S(2)}) async-start(), calls=%async_computation.3 | async-start | bytes 2621440 | tf_op jit(solution)/shard_map/all_gather | solution.py:403
  38.0 31.2 %collective-permute-start.10 = (bf16[528,512]{1,0:T(8,128)(2,1)}, bf16[528,512]{1,0:T(8,128)(2,1)S(1)}, u32[]{:S(2)}, u32[]{:S(2)}) collective-permute-start(bf16[528,512]{1,0:T(8,128)(2,1)} %collective-permute-done.9.refs_11_), channel_id=1, source_target_pairs={{1,0},{2,1},{5,4},{6,5},{9,8},{10,9},{13,12},{14,13},{17,16},{18,1... | collective-permute-start | bytes 1622024 | tf_op jit(solution)/shard_map/ppermute | solution.py:180
  40.7 29.7 %collective-permute-start.7 = (bf16[528,512]{1,0:T(8,128)(2,1)}, bf16[528,512]{1,0:T(8,128)(2,1)S(1)}, u32[]{:S(2)}, u32[]{:S(2)}) collective-permute-start(bf16[528,512]{1,0:T(8,128)(2,1)} %collective-permute-done.6.refs_8_), channel_id=1, source_target_pairs={{1,2},{2,3},{5,6},{6,7},{9,10},{10,11},{13,14},{14,15},{17,18},{18... | collective-permute-start | bytes 1622024 | tf_op jit(solution)/shard_map/ppermute | solution.py:179
  41.4 38.9 %collective-permute-start.4 = (bf16[512,512]{1,0:T(8,128)(2,1)}, bf16[512,512]{1,0:T(8,128)(2,1)S(1)}, u32[]{:S(2)}, u32[]{:S(2)}) collective-permute-start(bf16[512,512]{1,0:T(8,128)(2,1)} %collective-permute-done.3.refs_4_), channel_id=1, source_target_pairs={{1,0},{2,1},{5,4},{6,5},{9,8},{10,9},{13,12},{14,13},{17,16},{18,1... | collective-permute-start | bytes 1572872 | tf_op jit(solution)/shard_map/ppermute | solution.py:180
  42.7 38.9 %collective-permute-start.1 = (bf16[512,512]{1,0:T(8,128)(2,1)}, bf16[512,512]{1,0:T(8,128)(2,1)S(1)}, u32[]{:S(2)}, u32[]{:S(2)}) collective-permute-start(bf16[512,512]{1,0:T(8,128)(2,1)} %collective-permute-done.refs_1_), channel_id=1, source_target_pairs={{1,2},{2,3},{5,6},{6,7},{9,10},{10,11},{13,14},{14,15},{17,18},{18... | collective-permute-start | bytes 1572872 | tf_op jit(solution)/shard_map/ppermute | solution.py:179
  69.1 33.7 %collective-permute-start.11 = (bf16[528,512]{1,0:T(8,128)(2,1)S(1)}, bf16[528,512]{1,0:T(8,128)(2,1)S(1)}, u32[]{:S(2)}, u32[]{:S(2)}) collective-permute-start(bf16[528,512]{1,0:T(8,128)(2,1)S(1)} %collective-permute-done.10.refs_12_), channel_id=1, source_target_pairs={{1,0},{5,4},{9,8},{13,12},{17,16},{21,20},{25,24},{29,28}} | collective-permute-start | bytes 1622024 | tf_op jit(solution)/shard_map/ppermute | solution.py:180
  70.4 32.4 %collective-permute-start.8 = (bf16[528,512]{1,0:T(8,128)(2,1)S(1)}, bf16[528,512]{1,0:T(8,128)(2,1)S(1)}, u32[]{:S(2)}, u32[]{:S(2)}) collective-permute-start(bf16[528,512]{1,0:T(8,128)(2,1)S(1)} %collective-permute-done.7.refs_9_), channel_id=1, source_target_pairs={{2,3},{6,7},{10,11},{14,15},{18,19},{22,23},{26,27},{30,31}} | collective-permute-start | bytes 1622024 | tf_op jit(solution)/shard_map/ppermute | solution.py:179
  106.3 122.6 %all-gather.9.cloned.1.call-start = ((), (), s32[]{:S(2)}) async-start(), calls=%async_computation.5 | async-start | bytes 9437184 | tf_op jit(solution)/shard_map/all_gather | solution.py:408
  107.1 167.9 %all-gather.11.cloned.1.call-start = ((), (), s32[]{:S(2)}) async-start(), calls=%async_computation.6 | async-start | bytes 2621440 | tf_op jit(solution)/shard_map/all_gather | solution.py:415
  144.4 30.7 %collective-permute-start.15 = (bf16[512,512]{1,0:T(8,128)(2,1)S(1)}, bf16[512,512]{1,0:T(8,128)(2,1)S(1)}, u32[]{:S(2)}, u32[]{:S(2)}) collective-permute-start(bf16[512,512]{1,0:T(8,128)(2,1)S(1)} %get-tuple-element.112.refs_0_), channel_id=1, source_target_pairs={{1,0},{2,1},{3,2},{5,4},{6,5},{7,6},{9,8},{10,9},{11,10},{13,12},{... | collective-permute-start | bytes 1572872 | tf_op jit(solution)/shard_map/ppermute | solution.py:180
  145.7 31.5 %collective-permute-start.12 = (bf16[512,512]{1,0:T(8,128)(2,1)S(1)}, bf16[512,512]{1,0:T(8,128)(2,1)S(1)}, u32[]{:S(2)}, u32[]{:S(2)}) collective-permute-start(bf16[512,512]{1,0:T(8,128)(2,1)S(1)} %get-tuple-element.112.refs_0_), channel_id=1, source_target_pairs={{0,1},{1,2},{2,3},{4,5},{5,6},{6,7},{8,9},{9,10},{10,11},{12,13},{... | collective-permute-start | bytes 1572872 | tf_op jit(solution)/shard_map/ppermute | solution.py:179
  228.9 155.6 %reduce-scatter.4.cloned.1.call-start = ((), (), s32[]{:S(2)}) async-start(), calls=%async_computation.7 | async-start | bytes 5242880 | tf_op jit(solution)/shard_map/reduce_scatter | solution.py:435
  308.8 348.4 %all-reduce.2.cloned.1.call-start = ((), (), s32[]{:S(2)}) async-start(), calls=%async_computation.10 | async-start | bytes 16777216 | tf_op jit(solution)/shard_map/psum | solution.py:442
  408.7 302.1 %reduce-scatter.6.cloned.1.call-start = ((), (), s32[]{:S(2)}) async-start(), calls=%async_computation.8 | async-start | bytes 5242880 | tf_op jit(solution)/shard_map/reduce_scatter | solution.py:458
  408.7 28.6 %collective-permute-start.29 = (bf16[512,512]{1,0:T(8,128)(2,1)}, bf16[512,512]{1,0:T(8,128)(2,1)}, u32[]{:S(2)}, u32[]{:S(2)}) collective-permute-start(bf16[512,512]{1,0:T(8,128)(2,1)} %collective-permute-done.26.refs_1_), channel_id=1, source_target_pairs={{1,2},{2,3},{5,6},{6,7},{9,10},{10,11},{13,14},{14,15},{17,18},{18... | collective-permute-start | bytes 1572872 | tf_op jit(solution)/shard_map/ppermute | solution.py:179
  410.2 27.1 %collective-permute-start.30 = (bf16[512,512]{1,0:T(8,128)(2,1)}, bf16[512,512]{1,0:T(8,128)(2,1)}, u32[]{:S(2)}, u32[]{:S(2)}) collective-permute-start(bf16[512,512]{1,0:T(8,128)(2,1)} %collective-permute-done.27.refs_4_), channel_id=1, source_target_pairs={{1,0},{2,1},{5,4},{6,5},{9,8},{10,9},{13,12},{14,13},{17,16},{18,1... | collective-permute-start | bytes 1572872 | tf_op jit(solution)/shard_map/ppermute | solution.py:180
  437.3 54.0 %collective-permute-start.40 = (bf16[512,2048]{1,0:T(8,128)(2,1)}, bf16[512,2048]{1,0:T(8,128)(2,1)}, u32[]{:S(2)}, u32[]{:S(2)}) collective-permute-start(bf16[512,2048]{1,0:T(8,128)(2,1)} %maximum_select_fusion.3), channel_id=1, source_target_pairs={{0,8},{4,20},{8,0},{12,28},{16,24},{20,4},{24,16},{28,12},{1,9},{5... | collective-permute-start | bytes 6291464 | tf_op jit(solution)/shard_map/ppermute | solution.py:258
  504.7 218.9 %reduce-scatter.8.cloned.1.call-start = ((), (), s32[]{:S(2)}) async-start(), calls=%async_computation.9 | async-start | bytes 5242880 | tf_op jit(solution)/shard_map/reduce_scatter | solution.py:476
  619.0 29.7 %collective-permute-start.52 = (bf16[512,1536]{1,0:T(8,128)(2,1)}, bf16[512,1536]{1,0:T(8,128)(2,1)}, u32[]{:S(2)}, u32[]{:S(2)}) collective-permute-start(bf16[512,1536]{1,0:T(8,128)(2,1)} %maximum_select_fusion.4), channel_id=1, source_target_pairs={{0,8},{4,20},{8,0},{12,28},{16,24},{20,4},{24,16},{28,12},{1,9},{5... | collective-permute-start | bytes 4718600 | tf_op jit(solution)/shard_map/ppermute | solution.py:258
  625.9 73.2 %collective-permute-start.60 = (bf16[1024,2048]{1,0:T(8,128)(2,1)}, bf16[1024,2048]{1,0:T(8,128)(2,1)}, u32[]{:S(2)}, u32[]{:S(2)}) collective-permute-start(bf16[1024,2048]{1,0:T(8,128)(2,1)} %maximum_select_fusion.1.own), channel_id=1, source_target_pairs={{0,4},{4,0},{8,12},{12,8},{16,20},{20,16},{24,28},{28,24},{1,5},{5... | collective-permute-start | bytes 12582920 | tf_op jit(solution)/shard_map/ppermute | solution.py:258
  653.1 61.0 %collective-permute-start.53 = (bf16[1024,1536]{1,0:T(8,128)(2,1)}, bf16[1024,1536]{1,0:T(8,128)(2,1)}, u32[]{:S(2)}, u32[]{:S(2)}) collective-permute-start(bf16[1024,1536]{1,0:T(8,128)(2,1)} %maximum_select_fusion.2.own), channel_id=1, source_target_pairs={{0,4},{4,0},{8,12},{12,8},{16,20},{20,16},{24,28},{28,24},{1,5},{5... | collective-permute-start | bytes 9437192 | tf_op jit(solution)/shard_map/ppermute | solution.py:258
  (110 other events, 1266.0 us)
Sparse Core Ops, SparseCore 0:
  29.4 36.6 all-gather.6
  106.4 52.1 all-gather.4
  160.5 60.5 all-gather.8
  229.0 45.8 all-gather.10
  308.9 75.6 reduce-scatter.3
  408.8 148.3 all-reduce.1
  559.5 76.9 reduce-scatter.5
  638.9 78.3 reduce-scatter.7

commit v2 on v1

v2 whole, which is shorter than its diff:
```python
import functools

import jax
import jax.numpy as jnp
from jax import lax
from jax.experimental import pallas as pl
from jax.experimental.pallas import tpu as pltpu
from jax.sharding import PartitionSpec as P

HEAD_DIM = 128
FF = 8192
EPSILON = 1e-05
MASKED = -1e30
LONGEST_DOC = 512
QUERY_BLOCK = 256
VMEM = 36 * 2**20
COST = pl.CostEstimate(flops=1, bytes_accessed=1, transcendentals=0)

bf16 = jnp.bfloat16
f32 = jnp.float32

NT = (((1,), (1,)), ((), ()))
TN = (((0,), (0,)), ((), ()))
NN = (((1,), (0,)), ((), ()))


def dot(a, b, dims):
    return lax.dot_general(a, b, dims, preferred_element_type=f32)


def block_probs(i, rot, seg_row, seg_col, block, scale):
    start = i * block
    low = max(0, start - LONGEST_DOC)
    high = start + block
    q = rot[0, start:high, :]
    k = rot[1, low:high, :]
    scores = dot(q, k, NT) * scale
    shape = scores.shape
    q_pos = start + lax.broadcasted_iota(jnp.int32, shape, 0)
    k_pos = low + lax.broadcasted_iota(jnp.int32, shape, 1)
    allowed = (seg_col[start:high, :] == seg_row[0][:, low:high]) & (k_pos <= q_pos)
    scores = jnp.where(allowed, scores, MASKED)
    expo = jnp.exp(scores - jnp.max(scores, axis=1, keepdims=True))
    return expo * (1.0 / jnp.sum(expo, axis=1, keepdims=True)), q, k, start, low, high


def attn_fwd_kernel(block, scale, q_lin, k_lin, v_lin, cosine, sine, seg_row, seg_col, att, rot):
    cos_t = cosine[...]
    sin_t = sine[...]
    for s, lin in ((0, q_lin), (1, k_lin)):
        z = lin[...]
        rot[s] = (z * cos_t + pltpu.roll(z, HEAD_DIM // 2, 1) * sin_t).astype(bf16)
    rot[2] = v_lin[...].astype(bf16)
    for i in range(q_lin.shape[0] // block):
        probs, _, _, start, low, high = block_probs(i, rot, seg_row, seg_col, block, scale)
        att[start:high, :] = dot(probs.astype(bf16), rot[2, low:high, :], NN).astype(bf16)


def attn_bwd_kernel(block, scale, rot, g_att, cosine, sine, seg_row, seg_col, grads, dk, dv):
    cos_t = cosine[...]
    sin_t = sine[...]
    cols = grads.shape[1] // 3
    at = pl.program_id(1) * HEAD_DIM
    dk[...] = jnp.zeros_like(dk)
    dv[...] = jnp.zeros_like(dv)

    def lanes(s):
        return pl.ds(pl.multiple_of(s * cols + at, HEAD_DIM), HEAD_DIM)

    def back(z, c, s):
        return (z * c - pltpu.roll(z, HEAD_DIM // 2, 1) * s).astype(bf16)

    for i in range(rot.shape[1] // block):
        probs, q, k, start, low, high = block_probs(i, rot, seg_row, seg_col, block, scale)
        g = g_att[start:high, :]
        g_probs = dot(g, rot[2, low:high, :], NT)
        delta = jnp.sum(probs * g_probs, axis=1, keepdims=True)
        g_raw = (probs * (g_probs - delta) * scale).astype(bf16)
        grads[start:high, lanes(0)] = back(
            dot(g_raw, k, NN), cos_t[start:high, :], sin_t[start:high, :]
        )
        dk[low:high, :] += dot(g_raw, q, TN)
        dv[low:high, :] += dot(probs.astype(bf16), g, TN)
    grads[:, lanes(1)] = back(dk[...], cos_t, sin_t)
    grads[:, lanes(2)] = dv[...].astype(bf16)


def attention_specs(row_len):
    triple = pl.BlockSpec((3, row_len, HEAD_DIM), lambda r, h: (0, r, h))
    plain = pl.BlockSpec((row_len, HEAD_DIM), lambda r, h: (r, h))
    table = pl.BlockSpec((row_len, HEAD_DIM), lambda r, h: (0, 0))
    seg_row = pl.BlockSpec((1, 1, row_len), lambda r, h: (r, 0, 0))
    seg_col = pl.BlockSpec((row_len, 1), lambda r, h: (r, 0))
    return triple, plain, table, seg_row, seg_col


def attn_forward(lin, cos_t, sin_t, segs):
    tokens = lin.shape[0]
    cols = lin.shape[1] // 3
    heads = cols // HEAD_DIM
    rows, row_len = segs.shape
    triple, plain, table, seg_row, seg_col = attention_specs(row_len)
    block = min(QUERY_BLOCK, row_len)
    parts = [
        pl.BlockSpec((row_len, HEAD_DIM), lambda r, h, s=s: (r, s * heads + h)) for s in range(3)
    ]
    return pl.pallas_call(
        functools.partial(attn_fwd_kernel, block, HEAD_DIM**-0.5),
        grid=(rows, heads),
        in_specs=[*parts, table, table, seg_row, seg_col],
        out_specs=[plain, triple],
        out_shape=[
            jax.ShapeDtypeStruct((tokens, cols), bf16),
            jax.ShapeDtypeStruct((3, tokens, cols), bf16),
        ],
        compiler_params=pltpu.CompilerParams(vmem_limit_bytes=VMEM),
        cost_estimate=COST,
    )(lin, lin, lin, cos_t, sin_t, segs[:, None, :], segs.reshape(tokens, 1))


def attn_backward(rot, g_att, cos_t, sin_t, segs):
    _, tokens, cols = rot.shape
    rows, row_len = segs.shape
    triple, plain, table, seg_row, seg_col = attention_specs(row_len)
    block = min(QUERY_BLOCK, row_len)
    return pl.pallas_call(
        functools.partial(attn_bwd_kernel, block, HEAD_DIM**-0.5),
        grid=(rows, cols // HEAD_DIM),
        in_specs=[triple, plain, table, table, seg_row, seg_col],
        out_specs=pl.BlockSpec((row_len, 3 * cols), lambda r, h: (r, 0)),
        out_shape=jax.ShapeDtypeStruct((tokens, 3 * cols), bf16),
        scratch_shapes=[pltpu.VMEM((row_len, HEAD_DIM), f32)] * 2,
        compiler_params=pltpu.CompilerParams(vmem_limit_bytes=VMEM),
        cost_estimate=COST,
    )(rot, g_att, cos_t, sin_t, segs[:, None, :], segs.reshape(tokens, 1))


def after(value, *deps):
    return lax.optimization_barrier((value,) + deps)[0]


def join_kernel(n, chunks, *refs):
    per = 2 * n - 1
    out, sem = refs[chunks * per], refs[chunks * per + 1]
    me = lax.axis_index("mp")
    at = 0
    for c in range(chunks):
        own, right, left = refs[c * per], refs[c * per + 1 : c * per + n], refs[c * per + n : c * per + per]
        rows, cols = own.shape

        def put(src, block, at=at, rows=rows, cols=cols):
            target = out.at[
                pl.ds(at, rows), pl.ds(pl.multiple_of(block * cols, cols), cols)
            ]
            pltpu.make_async_copy(src, target, sem).start()

        at += rows
        put(own, me)
        for s in range(1, n):
            pl.when(me >= s)(functools.partial(put, right[s - 1], me - s))
            pl.when(me + s < n)(functools.partial(put, left[s - 1], me + s))
    pltpu.make_async_copy(out, out, sem).wait()


def join(parts):
    n = lax.axis_size("mp")
    rows = sum(p[0].shape[0] for p in parts)
    flat = [a for own, right, left in parts for a in (own, *right, *left)]
    shape = (rows, n * parts[0][0].shape[1])
    return pl.pallas_call(
        functools.partial(join_kernel, n, len(parts)),
        in_specs=[pl.BlockSpec(memory_space=pl.ANY)] * len(flat),
        out_specs=pl.BlockSpec(memory_space=pltpu.VMEM),
        out_shape=jax.ShapeDtypeStruct(shape, parts[0][0].dtype),
        scratch_shapes=[pltpu.SemaphoreType.DMA(())],
        compiler_params=pltpu.CompilerParams(vmem_limit_bytes=VMEM),
        cost_estimate=COST,
    )(*flat)


def line_step(s, right, left):
    n = lax.axis_size("mp")
    return (
        lax.ppermute(right, "mp", [(i, i + 1) for i in range(s - 1, n - 1)]),
        lax.ppermute(left, "mp", [(i, i - 1) for i in range(1, n - s + 1)]),
    )


def line_parts(block, first=None):
    right = left = block
    rights, lefts = [], []
    for s in range(1, lax.axis_size("mp")):
        if s == 1 and first is not None:
            right, left = first
        else:
            right, left = line_step(s, right, left)
        rights.append(right)
        lefts.append(left)
    return block, rights, lefts


def line_gather(chunks):
    return join([line_parts(c) for c in chunks])


def split_rows(x, chunks=2):
    return jnp.split(x, chunks, axis=0)


class Scatter:
    def __init__(self, y):
        self.n = lax.axis_size("mp")
        self.me = lax.axis_index("mp")
        self.y = y
        self.step = 0
        self.x = (self.block(self.n - 1), self.block(1 - self.n))
        self.flight = None
        self.launch()

    def block(self, offset):
        cols = self.y.shape[1] // self.n
        at = jnp.clip(self.me + offset, 0, self.n - 1) * cols
        return lax.dynamic_slice_in_dim(self.y, at, cols, 1)

    def launch(self):
        self.step += 1
        n, s = self.n, self.step
        if s < n:
            right, left = self.x
            self.flight = (
                lax.ppermute(right, "mp", [(i, i + 1) for i in range(s)]),
                lax.ppermute(left, "mp", [(i, i - 1) for i in range(n - s, n)]),
            )

    def land(self):
        if self.flight is not None:
            ahead = self.n - self.step - 1
            self.x = self.flight
            if ahead > 0:
                self.x = tuple(
                    (a.astype(f32) + self.block(offset).astype(f32)).astype(bf16)
                    for a, offset in zip(self.x, (ahead, -ahead))
                )
            self.flight = None

    def finish(self):
        while self.flight is not None:
            self.land()
            self.launch()
        return sum(a.astype(f32) for a in (*self.x, self.block(0)))


def dp_pairs(bits):
    return [(i, i ^ (1 << bits[i & 1])) for i in range(lax.axis_size("dp"))]


def dp_rounds():
    rest = list(range(1, lax.axis_size("dp").bit_length() - 1))
    return list(zip(rest, rest[1:] + rest[:1]))


def by_parity(odd, bits, value):
    return jnp.where(odd == 1, value(bits[1]), value(bits[0]))


class Pieces:
    def __init__(self, piece, place, rounds):
        self.x = (piece,)
        self.flight = None
        self.me = lax.axis_index("dp")
        self.owners = [self.me]
        self.place = place
        self.rounds = list(reversed(rounds))
        self.todo = self.rounds + [(0, 0)]

    def launch(self):
        if self.todo and self.flight is None:
            bits = self.todo.pop(0)
            if self.todo and len(self.x) > 1:
                self.x = (jnp.concatenate(self.x),)
            got = tuple(lax.ppermute(p, "dp", dp_pairs(bits)) for p in self.x)
            self.flight = (bits, got)

    def land(self):
        if self.flight is None:
            return
        bits, got = self.flight
        self.flight = None
        self.x = self.x + got
        if self.todo:
            flip = by_parity(self.me & 1, bits, lambda b: 1 << b)
            self.owners = self.owners + [o ^ flip for o in self.owners]
        else:
            theirs = [self.me ^ 1]
            for bits in self.rounds:
                flip = by_parity(1 - (self.me & 1), bits, lambda b: 1 << b)
                theirs = theirs + [o ^ flip for o in theirs]
            self.owners = self.owners + theirs

    def finish(self, groups=1):
        while self.todo or self.flight is not None:
            self.land()
            self.launch()
        return widen(self.x, jnp.stack([self.place(o) for o in self.owners]), groups)


class Halving:
    def __init__(self, make, whole=False):
        self.me = lax.axis_index("dp")
        odd = self.me & 1
        self.todo = dp_rounds()
        self.whole = whole
        self.pieces = None
        sent = make(1 - odd)
        self.x = (make(after(odd, sent)),)
        self.flight = lax.ppermute(sent, "dp", dp_pairs((0, 0)))

    def place(self, device):
        odd = device & 1
        at = odd
        if not self.whole:
            for bits in dp_rounds():
                at = at * 2 + by_parity(odd, bits, lambda b: (device >> b) & 1)
        return at

    def launch(self):
        if self.pieces is not None:
            self.pieces.x = self.x
            self.pieces.launch()
        elif self.todo and self.flight is None:
            bits = self.todo.pop(0)
            *kept, sent = self.x
            self.x = tuple(kept) or (sent,)
            self.flight = lax.ppermute(sent, "dp", dp_pairs(bits))

    def land(self):
        if self.pieces is not None:
            self.pieces.land()
            self.x = self.pieces.x
        elif self.flight is not None:
            (kept,) = self.x
            got = self.flight
            self.flight = None

            def add(at=0, rows=kept.shape[0]):
                terms = (lax.dynamic_slice_in_dim(a, at, rows, 0) for a in (kept, got))
                return sum(a.astype(f32) for a in terms).astype(bf16)

            if not self.todo:
                self.x = (add(),)
                rounds = [] if self.whole else dp_rounds()
                self.pieces = Pieces(self.x[0], self.place, rounds)
            elif self.whole:
                self.x = (add(),)
            else:
                half = kept.shape[0] // 2
                bit = by_parity(self.me & 1, self.todo[0], lambda b: (self.me >> b) & 1)
                self.x = (add(bit * half, half), add((1 - bit) * half, half))

    def finish(self, groups=1):
        while self.pieces is None:
            self.land()
            self.launch()
        self.pieces.x = self.x
        return self.pieces.finish(groups)


def widen_kernel(firsts, table, *refs):
    *arrays, out = refs
    groups, _, cols = out.shape
    step = pl.program_id(0)
    for k, src in enumerate(arrays):

        @pl.when((step >= firsts[k]) & (step < firsts[k + 1]))
        def _(src=src):
            for g in range(groups):
                out[g] = src[:, g * cols : (g + 1) * cols].astype(f32)


def widen(arrays, places, groups):
    total = sum(a.shape[0] for a in arrays)
    cols = arrays[0].shape[1]
    rows = total // places.shape[0]
    block = min(256, rows)
    per = rows // block
    wide = cols // groups
    firsts = [sum(a.shape[0] for a in arrays[:k]) // block for k in range(len(arrays) + 1)]

    def spec(k):
        def index(step, table):
            return (jnp.clip(step - firsts[k], 0, firsts[k + 1] - firsts[k] - 1), 0)

        return pl.BlockSpec((block, cols), index)

    def out_index(step, table):
        return (0, table[step // per] * per + step % per, 0)

    return pl.pallas_call(
        functools.partial(widen_kernel, firsts),
        grid_spec=pltpu.PrefetchScalarGridSpec(
            num_scalar_prefetch=1,
            grid=(total // block,),
            in_specs=[spec(k) for k in range(len(arrays))],
            out_specs=pl.BlockSpec((groups, block, wide), out_index),
        ),
        out_shape=jax.ShapeDtypeStruct((groups, total, wide), f32),
        compiler_params=pltpu.CompilerParams(vmem_limit_bytes=VMEM),
        cost_estimate=COST,
    )(places.astype(jnp.int32), *arrays)


def half_lanes(x, half):
    size = x.shape[1] // 2
    return lax.dynamic_slice_in_dim(x, half * size, size, 1)


def meet(values, *sums):
    for h in sums:
        h.land()
    met, xs = lax.optimization_barrier((tuple(values), tuple(h.x for h in sums)))
    for h, x in zip(sums, xs):
        h.x = x
        h.launch()
    return met


def butterfly_sum(x, axis):
    size = lax.axis_size(axis)
    for bit in range(size.bit_length() - 1):
        x = x + lax.ppermute(x, axis, [(i, i ^ (1 << bit)) for i in range(size)])
    return x


def norm_qkv_kernel(x, weight, gain, bias, rows, lin):
    v = x[...].astype(f32)
    centred = v - jnp.mean(v, axis=1, keepdims=True)
    rstd = lax.rsqrt(jnp.mean(centred * centred, axis=1, keepdims=True) + EPSILON)
    normed = (centred * rstd * gain[...] + bias[...]).astype(bf16)
    rows[...] = normed
    cols = weight.shape[2]
    for s in range(3):
        lin[:, s * cols : (s + 1) * cols] = dot(normed, weight[s], NN)


def norm_qkv(x, tokens, weight, gain, bias):
    _, width, cols = weight.shape
    block = min(256, tokens)
    rows = pl.BlockSpec((block, width), lambda r: (r, 0))
    vector = pl.BlockSpec((1, width), lambda r: (0, 0))
    return pl.pallas_call(
        norm_qkv_kernel,
        grid=(tokens // block,),
        in_specs=[rows, pl.BlockSpec((3, width, cols), lambda r: (0, 0, 0)), vector, vector],
        out_specs=[rows, pl.BlockSpec((block, 3 * cols), lambda r: (r, 0))],
        out_shape=[
            jax.ShapeDtypeStruct((tokens, width), bf16),
            jax.ShapeDtypeStruct((tokens, 3 * cols), f32),
        ],
        compiler_params=pltpu.CompilerParams(vmem_limit_bytes=VMEM),
        cost_estimate=COST,
    )(x, weight, gain[None], bias[None])


def project_norm_kernel(att, weight, x, gain, bias, mid, rows, held, sem):
    dp_size, mp_size, part, _ = weight.shape

    @pl.when(pl.program_id(0) == 0)
    def _():
        for d in range(dp_size):
            for j in range(mp_size):
                target = held.at[pl.ds((j * dp_size + d) * part, part), :]
                pltpu.make_async_copy(weight.at[d, j], target, sem).start()
        pltpu.make_async_copy(held, held, sem).wait()

    v = x[...].astype(f32) + dot(att[...], held[...], NN)
    mid[...] = v
    centred = v - jnp.mean(v, axis=1, keepdims=True)
    rstd = lax.rsqrt(jnp.mean(centred * centred, axis=1, keepdims=True) + EPSILON)
    rows[...] = (centred * rstd * gain[...] + bias[...]).astype(bf16)


def project_norm(att, weight, x, gain, bias):
    tokens, width = att.shape
    block = min(256, tokens)
    rows = pl.BlockSpec((block, width), lambda r: (r, 0))
    vector = pl.BlockSpec((1, width), lambda r: (0, 0))
    return pl.pallas_call(
        project_norm_kernel,
        grid=(tokens // block,),
        in_specs=[rows, pl.BlockSpec(memory_space=pl.ANY), rows, vector, vector],
        out_specs=[rows, rows],
        out_shape=[
            jax.ShapeDtypeStruct((tokens, width), f32),
            jax.ShapeDtypeStruct((tokens, width), bf16),
        ],
        scratch_shapes=[pltpu.VMEM((width, width), bf16), pltpu.SemaphoreType.DMA(())],
        compiler_params=pltpu.CompilerParams(vmem_limit_bytes=VMEM),
        cost_estimate=COST,
    )(att, weight, x, gain[None], bias[None])


def add_rows(vec, *arrays):
    @pl.when(pl.program_id(0) == 0)
    def _():
        vec[...] = jnp.zeros_like(vec)

    for i, a in enumerate(arrays):
        vec[i : i + 1, :] += jnp.sum(a, axis=0, keepdims=True)


def attn_in_backward_kernel(g, weight, x, gain, low, plain, cross, vec):
    cols = weight.shape[2]
    part = sum(dot(g[:, s * cols : (s + 1) * cols], weight[s], NT) for s in range(3))
    low[...] = part.astype(bf16)
    v = x[...].astype(f32)
    centred = v - jnp.mean(v, axis=1, keepdims=True)
    xhat = centred * lax.rsqrt(jnp.mean(centred * centred, axis=1, keepdims=True) + EPSILON)
    crossed = part * xhat
    plain[...] = jnp.sum(part * gain[...], axis=1, keepdims=True)
    cross[...] = jnp.sum(crossed * gain[...], axis=1, keepdims=True)
    add_rows(vec, crossed, part)


def attn_in_backward(g_rows, weight, x, gain):
    tokens, wide = g_rows.shape
    width, cols = weight.shape[1:]
    block = min(256, tokens)
    rows = pl.BlockSpec((block, width), lambda r: (r, 0))
    column = pl.BlockSpec((block, 1), lambda r: (r, 0))
    return pl.pallas_call(
        attn_in_backward_kernel,
        grid=(tokens // block,),
        in_specs=[
            pl.BlockSpec((block, wide), lambda r: (r, 0)),
            pl.BlockSpec((3, width, cols), lambda r: (0, 0, 0)),
            rows,
            pl.BlockSpec((1, width), lambda r: (0, 0)),
        ],
        out_specs=[rows, column, column, pl.BlockSpec((2, width), lambda r: (0, 0))],
        out_shape=[
            jax.ShapeDtypeStruct((tokens, width), bf16),
            jax.ShapeDtypeStruct((tokens, 1), f32),
            jax.ShapeDtypeStruct((tokens, 1), f32),
            jax.ShapeDtypeStruct((2, width), f32),
        ],
        compiler_params=pltpu.CompilerParams(vmem_limit_bytes=VMEM),
        cost_estimate=COST,
    )(g_rows, weight, x, gain[None])


def mid_backward_kernel(me, g_ffn, gy, mid, gain, low, mine, vec):
    v = mid[...]
    centred = v - jnp.mean(v, axis=1, keepdims=True)
    rstd = lax.rsqrt(jnp.mean(centred * centred, axis=1, keepdims=True) + EPSILON)
    xhat = centred * rstd
    grad_normed = g_ffn[...].astype(f32)
    add_rows(vec, grad_normed * xhat, grad_normed)
    scaled = grad_normed * gain[...]
    plain = jnp.mean(scaled, axis=1, keepdims=True)
    cross = jnp.mean(scaled * xhat, axis=1, keepdims=True)
    grad = gy[...].astype(f32) + rstd * (scaled - plain - xhat * cross)
    low[...] = grad.astype(bf16)
    cols = mine.shape[1]
    for j in range(grad.shape[1] // cols):

        @pl.when(me[0] == j)
        def _(j=j):
            mine[...] = grad[:, j * cols : (j + 1) * cols]


def mid_backward(g_ffn, gy, mid, gain):
    tokens, width = mid.shape
    feats = width // lax.axis_size("mp")
    block = min(128, tokens)
    rows = pl.BlockSpec((block, width), lambda r, me: (r, 0))
    return pl.pallas_call(
        mid_backward_kernel,
        grid_spec=pltpu.PrefetchScalarGridSpec(
            num_scalar_prefetch=1,
            grid=(tokens // block,),
            in_specs=[rows, rows, rows, pl.BlockSpec((1, width), lambda r, me: (0, 0))],
            out_specs=[
                rows,
                pl.BlockSpec((block, feats), lambda r, me: (r, 0)),
                pl.BlockSpec((2, width), lambda r, me: (0, 0)),
            ],
        ),
        out_shape=[
            jax.ShapeDtypeStruct((tokens, width), bf16),
            jax.ShapeDtypeStruct((tokens, feats), f32),
            jax.ShapeDtypeStruct((2, width), f32),
        ],
        compiler_params=pltpu.CompilerParams(vmem_limit_bytes=VMEM),
        cost_estimate=COST,
    )(lax.axis_index("mp").reshape(1).astype(jnp.int32), g_ffn, gy, mid, gain[None])


def split_bits(v):
    high = lax.reduce_precision(v, 8, 7)
    return [high.astype(bf16), (v - high).astype(bf16)]


def normalize(v):
    mean = jnp.mean(v, axis=1, keepdims=True)
    centred = v - mean
    rstd = lax.rsqrt(jnp.mean(centred * centred, axis=1, keepdims=True) + EPSILON)
    return centred * rstd, rstd


def local(
    inputs,
    segment_ids,
    width_bucket,
    attn_gain,
    attn_bias,
    qkv_weight,
    proj_weight,
    ffn_gain,
    ffn_bias,
    up_weight,
    down_weight,
    grad_result,
):
    tokens, feats = inputs.shape
    row_len = segment_ids.shape[1]
    mp_size = lax.axis_size("mp")
    dp_size = lax.axis_size("dp")
    mp_idx = lax.axis_index("mp")
    width = feats * mp_size

    def own(a):
        return lax.dynamic_slice_in_dim(a, mp_idx * feats, feats, a.ndim - 1)

    half = HEAD_DIM // 2
    freqs = jnp.power(10000.0, -jnp.arange(half, dtype=f32) / half)
    angles = jnp.arange(row_len, dtype=f32)[:, None] * freqs[None, :]
    cos_h, sin_h = jnp.cos(angles), jnp.sin(angles)
    cos_t = jnp.concatenate([cos_h, cos_h], axis=1)
    sin_t = jnp.concatenate([-sin_h, sin_h], axis=1)

    vectors = sum((split_bits(v) for v in (attn_gain, attn_bias, ffn_gain, ffn_bias)), [])
    packed = jnp.concatenate([jnp.stack(vectors), jnp.zeros((8, feats), bf16)])
    first, second = split_rows(inputs)
    chunks = [first, jnp.concatenate([second, packed])]
    starts = [line_step(1, c, c) for c in chunks]
    parts = [line_parts(c, pair) for c, pair in zip(chunks, starts)]
    gy_own = after(grad_result, *(p[1][min(1, mp_size - 2)] for p in parts))
    gathered = join(parts)
    vec = gathered[tokens : tokens + 8].astype(f32)
    gain_a, bias_a, gain_f, bias_f = (vec[2 * i] + vec[2 * i + 1] for i in range(4))
    gy_steps = [line_step(1, gy_own, gy_own)]

    part = proj_weight.shape[0] // dp_size
    slab = lax.dynamic_slice_in_dim(proj_weight, lax.axis_index("dp") * part, part, 0)
    slab = lax.all_gather(after(slab, gathered), "mp", axis=0)
    attn_rows, lin = norm_qkv(gathered, tokens, qkv_weight, gain_a, bias_a)
    att, rot = attn_forward(lin, cos_t, sin_t, segment_ids)
    att, slab, gy_steps[0] = lax.optimization_barrier((att, slab, gy_steps[0]))
    proj_full = lax.all_gather(slab, "dp", axis=0)
    att_full, proj_full = lax.optimization_barrier((line_gather(split_rows(att)), proj_full))
    gy_steps[0] = tuple(after(a, att_full) for a in gy_steps[0])
    gy_steps.append(line_step(2, *gy_steps[0]))
    mid, ffn_rows = project_norm(att_full, proj_full, gathered, gain_f, bias_f)
    ffn_rows, gy_steps[1] = lax.optimization_barrier((ffn_rows, gy_steps[1]))
    for s in range(3, mp_size):
        gy_steps.append(line_step(s, *gy_steps[-1]))

    limit = (width_bucket.reshape(tokens) + 1) * (FF // 4)
    columns = mp_idx * up_weight.shape[1] + jnp.arange(up_weight.shape[1], dtype=jnp.int32)
    keep = columns[None, :] < limit[:, None]
    hidden = dot(ffn_rows, up_weight, NN)
    relu = jnp.where(keep, jnp.maximum(hidden, 0.0), 0.0)
    active = (relu * relu).astype(bf16)

    gy = join([(gy_own, [r for r, _ in gy_steps], [l for _, l in gy_steps])])
    gy, active, relu = lax.optimization_barrier((gy, active, relu))
    grad_hidden = (2.0 * relu * dot(gy, down_weight, NT)).astype(bf16)
    g_ffn_part = dot(grad_hidden, up_weight, NT).astype(bf16)
    g_ffn_own = lax.psum_scatter(g_ffn_part, "mp", scatter_dimension=1, tiled=True)

    active, gy = (after(a, g_ffn_part) for a in (active, gy))
    down = Halving(lambda half: dot(half_lanes(active, half), gy, TN).astype(bf16))
    grad_up = dot(after(ffn_rows, down.x), grad_hidden, TN).astype(bf16)
    (grad_up,) = meet((grad_up,), down)
    grad_up = lax.psum_scatter(grad_up, "dp", scatter_dimension=0, tiled=True)
    ffn_part = dot(after(active, down.x), down_weight, NN).astype(bf16)
    down.x = after(down.x, ffn_part)
    g_ffn_own, ffn_part = meet((g_ffn_own, ffn_part), down)
    chunks = split_rows(g_ffn_own)
    starts = [line_step(1, c, c) for c in chunks]
    starts[0] = meet(starts[0], down)
    g_ffn = join([line_parts(c, pair) for c, pair in zip(chunks, starts)])
    up = Pieces(grad_up, lambda device: device, dp_rounds())
    g_ffn, ffn_part = meet((g_ffn, ffn_part), up, down)
    ffn_out = lax.psum_scatter(ffn_part, "mp", scatter_dimension=1, tiled=True)

    grad_mid_low, grad_mid_own, ffn_vec = mid_backward(g_ffn, gy, mid, gain_f)
    g_att = dot(grad_mid_low, proj_weight, NT).astype(bf16)
    g_qkv_rows = attn_backward(rot, g_att, cos_t, sin_t, segment_ids)
    (g_qkv_rows,) = meet((g_qkv_rows,), down, up)
    qkv = Halving(lambda half: dot(half_lanes(attn_rows, half), g_qkv_rows, TN).astype(bf16))
    (later,) = meet((g_qkv_rows,), qkv)
    g_attn_low, plain, cross, attn_vec = attn_in_backward(later, qkv_weight, gathered, gain_a)
    g_attn = lax.psum_scatter(g_attn_low, "mp", scatter_dimension=1, tiled=True).astype(f32)

    mid_later, _, ffn_out = meet((grad_mid_low, g_attn_low, ffn_out), down, up)
    proj = Halving(lambda half: dot(half_lanes(att, half), mid_later, TN).astype(bf16))
    proj.x = meet(proj.x, qkv, up)
    down.x = after(down.x, proj.x)
    (grad_down,) = meet((down.finish()[0],), qkv, proj)
    up.x = after(up.x, grad_down)
    (grad_up,) = meet((up.finish()[0],), qkv, proj)
    sums = jnp.concatenate([attn_vec, jnp.stack([plain, cross]).reshape(-1, width)])
    sums = butterfly_sum(sums, "mp")
    sum_plain, sum_cross = sums[2:].reshape(2, tokens, 1)
    vec = jnp.concatenate([own(sums[:2]), own(ffn_vec)])
    vec, sum_plain, g_attn = meet((vec, sum_plain, g_attn), qkv, proj)
    grad_vec = butterfly_sum(vec, "dp")
    grad_qkv, grad_proj = qkv.finish(3), proj.finish()[0]

    ffn_out = ffn_out.astype(f32)
    xhat_a, rstd_a = normalize(after(gathered, grad_up)[:tokens].astype(f32))
    grad_input = grad_mid_own + rstd_a * (
        g_attn * attn_gain - sum_plain / width - own(xhat_a) * (sum_cross / width)
    )
    block_output = (own(mid) + ffn_out).astype(bf16)
    return (
        block_output,
        grad_input,
        grad_vec[0],
        grad_vec[1],
        grad_qkv,
        grad_proj,
        grad_vec[2],
        grad_vec[3],
        grad_up,
        grad_down,
    )


def solution(mesh):
    placed = (
        P("dp", "mp"),
        P("dp", None),
        P("dp", None),
        P("mp"),
        P("mp"),
        P(None, None, "mp"),
        P("mp", None),
        P("mp"),
        P("mp"),
        P(None, "mp"),
        P("mp", None),
        P("dp", "mp"),
    )
    return jax.shard_map(
        local,
        mesh=mesh,
        in_specs=placed,
        out_specs=(
            P("dp", "mp"),
            P("dp", "mp"),
            P("mp"),
            P("mp"),
            P(None, None, "mp"),
            P("mp", None),
            P("mp"),
            P("mp"),
            P(None, "mp"),
            P("mp", None),
        ),
        check_vma=False,
    )
```

time: 747 us -> 695 us (0.930)
  Pallas kernels: 53 us -> 118 us
  other arithmetic: 88.9 us -> 48.7 us
  matrix products: 142 us -> 109 us
  waiting for transfers between devices: 277 us -> 247 us
  starting transfers between devices: 104 us -> 89.8 us
    pallas_call x3 -> x8, Pallas kernels: 21.2 us -> 86.4 us  [the longest x4 35.1 us: widen(): pl.pallas_call(functools.partial(widen_kernel, firsts), grid_spec=pltpu.P...]
    ppermute x18 -> x25, waiting for transfers between devices: 102 us -> 51.2 us  [the longest x6 32.8 us: launch(): self.flight = lax.ppermute(sent, 'dp', dp_pairs(bits))]
    dot_general x16 -> x12, matrix products: 142 us -> 109 us  [dot(): return lax.dot_general(a, b, dims, preferred_element_type=f32)]
    ppermute x18 -> x21, waiting for transfers between devices: 1.76 us -> 25.7 us  [line_step(): lax.ppermute(right, 'mp', [(i, i + 1) for i in range(s - 1, n - 1)])]
    select_n x6 -> x0, other arithmetic: 21.4 us -> none  [land(): jnp.where(bit == 0, jnp.concatenate([kept, got]), jnp.concatenate([got, k...]
    convert_element_type x12 -> x11, other arithmetic: 46.8 us -> 32 us  [the longest x9 27.6 us: add(): return sum((a.astype(f32) for a in terms)).astype(bf16)]
    unnamed x131 -> x122, local copies, waits for them, and re-layouts: 31.9 us -> 41.6 us
    ppermute x7 -> x5, starting transfers between devices: 15 us -> 5.65 us  [butterfly_sum(): x = x + lax.ppermute(x, axis, [(i, i ^ 1 << bit) for i in range(size)])]
  transfers between devices with their start and end apart: 69 -> 78, of which waited for: 31 -> 39; matrix products, arithmetic and copies ran while one was open for 29% -> 21% of each run, Pallas kernels for 7% -> 16%
where the time goes in v2:
time: 695 us; the launch traced here: 685 us
  waiting for transfers between devices  247 us (36%)
  Pallas kernels  118 us (17%)
  matrix products  109 us (16%)
  starting transfers between devices  89.8 us (13%)
  local copies, waits for them, and re-layouts  56.8 us (8%)
  other arithmetic  48.7 us (7%)
  between operations  15.8 us (2%)
    ppermute x21, waiting for transfers between devices, line_step(): lax.ppermute(left, 'mp', [(i, i - 1) for i in range(1, n - s + 1)])  151 us
    dot_general x12, matrix products, dot(): return lax.dot_general(a, b, dims, preferred_element_type=f32)  109 us
    unnamed x122, local copies, waits for them, and re-layouts  41.6 us
    ppermute x21, starting transfers between devices, line_step(): lax.ppermute(right, 'mp', [(i, i + 1) for i in range(s - 1, n - 1)])  39.7 us
    pallas_call x4, Pallas kernels, widen(): pl.pallas_call(functools.partial(widen_kernel, firsts), grid_spec=pltpu.P...  35.1 us
    ppermute x6, waiting for transfers between devices, launch(): self.flight = lax.ppermute(sent, 'dp', dp_pairs(bits))  32.8 us
    ppermute x21, starting transfers between devices, line_step(): lax.ppermute(left, 'mp', [(i, i - 1) for i in range(1, n - s + 1)])  27.7 us
    convert_element_type x9, other arithmetic, add(): return sum((a.astype(f32) for a in terms)).astype(bf16)  27.6 us
  transfers between devices with their start and end apart: 78, of which 39 were waited for; matrix products, arithmetic and copies ran while one was open for 21% of the time, Pallas kernels for 16%

profile of v2, /device:TPU:0, one launch (start us, length us, event | category | flops | bytes accessed | tf_op | source)
XLA Modules:
  0.0 684.7 jit_solution(17236291670115872969)
XLA Ops:
  72.5 19.3 %collective-permute-done.5.refs_6_ = bf16[512,512]{1,0:T(8,128)(2,1)} collective-permute-done((bf16[512,512]{1,0:T(8,128)(2,1)}, bf16[512,512]{1,0:T(8,128)(2,1)}, u32[]{:S(2)}, u32[]{:S(2)}) %collective-permute-start.5) | collective-permute-done | bytes 524320 | tf_op jit(solution)/shard_map/ppermute | solution.py:185
  112.3 12.3 %shard_map.196 = (bf16[1024,2048]{1,0:T(8,128)(2,1)S(1)}, f32[1024,1536]{1,0:T(8,128)S(1)}) custom-call(bf16[1040,2048]{1,0:T(8,128)(2,1)S(1)} %copy-done.2, bf16[3,2048,512]{2,1,0:T(8,128)(2,1)} %weight.3, f32[1,2048]{1,0:T(1,128)S(1)} %get-tuple-element.231.gain, f32[1,2048]{1,0:T(1,128)S(1)} %get-tuple-element.229.bias), custom_call_target="tpu_custom_call" | custom-call | flops 1 | bytes 1 | tf_op jit(solution)/shard_map/pallas_call | solution.py:450
  124.7 11.9 %shard_map.197 = (bf16[1024,512]{1,0:T(8,128)(2,1)S(1)}, bf16[3,1024,512]{2,1,0:T(8,128)(2,1)S(1)}) custom-call(f32[1024,1536]{1,0:T(8,128)S(1)} %get-tuple-element.109.q_lin.k_lin.v_lin, f32[1024,1536]{1,0:T(8,128)S(1)} %get-tuple-element.109.q_lin.k_lin.v_lin, f32[1024,1536]{1,0:T(8,128)S(1)} %get-tuple-element.109.q_lin.k_lin.v_lin, ...), custom_call_target="tpu_custom_call" | custom-call | flops 1 | bytes 1 | tf_op jit(solution)/shard_map/pallas_call | solution.py:107
  177.8 9.2 %collective-permute-done.18.refs_5_ = bf16[512,512]{1,0:T(8,128)(2,1)S(1)} collective-permute-done((bf16[512,512]{1,0:T(8,128)(2,1)S(1)}, bf16[512,512]{1,0:T(8,128)(2,1)S(1)}, u32[]{:S(2)}, u32[]{:S(2)}) %collective-permute-start.18) | collective-permute-done | bytes 524320 | tf_op jit(solution)/shard_map/ppermute | solution.py:185
  189.0 9.2 %collective-permute-done.24.refs_12_ = bf16[512,512]{1,0:T(8,128)(2,1)S(1)} collective-permute-done((bf16[512,512]{1,0:T(8,128)(2,1)S(1)}, bf16[512,512]{1,0:T(8,128)(2,1)S(1)}, u32[]{:S(2)}, u32[]{:S(2)}) %collective-permute-start.24) | collective-permute-done | bytes 524320 | tf_op jit(solution)/shard_map/ppermute | solution.py:185
  199.5 9.9 %collective-permute-done.19.refs_6_ = bf16[512,512]{1,0:T(8,128)(2,1)S(1)} collective-permute-done((bf16[512,512]{1,0:T(8,128)(2,1)S(1)}, bf16[512,512]{1,0:T(8,128)(2,1)S(1)}, u32[]{:S(2)}, u32[]{:S(2)}) %collective-permute-start.19) | collective-permute-done | bytes 524320 | tf_op jit(solution)/shard_map/ppermute | solution.py:185
  228.7 16.1 %shard_map.199 = (f32[1024,2048]{1,0:T(8,128)}, bf16[1024,2048]{1,0:T(8,128)(2,1)S(1)}) custom-call(bf16[1024,2048]{1,0:T(8,128)(2,1)S(1)} %copy-done.9, bf16[8,4,64,2048]{3,2,1,0:T(8,128)(2,1)} %bitcast.63, bf16[1040,2048]{1,0:T(8,128)(2,1)S(1)} %copy-done.3, f32[1,2048]{1,0:T(1,128)S(1)} %get-tuple-element.230.gain, f32[1,2048]{1,0:T(1,128)S(1)} %get-tuple-element.228.bias), custom_call_target="tpu_custom_call" | custom-call | flops 1 | bytes 1 | tf_op jit(solution)/shard_map/pallas_call | solution.py:487
  249.4 14.1 %multiply_convert_fusion.1 = (bf16[1024,2048]{1,0:T(8,128)(2,1)}, f32[1024,2048]{1,0:T(8,128)}) fusion(bf16[1024,2048]{1,0:T(8,128)(2,1)S(1)} %get-tuple-element.132, bf16[2048,2048]{1,0:T(8,128)(2,1)} %param.21, s32[1024]{0:T(1024)S(1)} %bitcast.72, s32[2048]{0:T(1024)S(1)} %iota_add_fusion), kind=kOutput, calls=%fused_computation.4 | convolution fusion | flops 8600420352 | bytes 25178112 | tf_op jit(solution)/shard_map/dot_general | solution.py:28
  273.6 14.3 %multiply_convert_fusion = bf16[1024,2048]{1,0:T(8,128)(2,1)S(1)} fusion(f32[1024,2048]{1,0:T(8,128)} %get-tuple-element.126, bf16[1024,2048]{1,0:T(8,128)(2,1)S(1)} %shard_map.200.gy, bf16[2048,2048]{1,0:T(8,128)(2,1)} %param.22), kind=kOutput, calls=%fused_computation.3 | convolution fusion | flops 8596226048 | bytes 25165824 | tf_op jit(solution)/shard_map/dot_general | solution.py:28
  289.9 12.8 %convolution_convert_fusion.2 = bf16[1024,2048]{1,0:T(8,128)(2,1)} fusion(bf16[1024,2048]{1,0:T(8,128)(2,1)S(1)} %multiply_convert_fusion, bf16[2048,2048]{1,0:T(8,128)(2,1)} %param.21), kind=kOutput, calls=%fused_computation.10 | convolution fusion | flops 8592031744 | bytes 16777216 | tf_op jit(solution)/shard_map/dot_general | solution.py:28
  303.1 9.5 %convolution_convert_fusion.6 = bf16[1024,2048]{1,0:T(8,128)(2,1)} fusion(bf16[1024,2048]{1,0:T(8,128)(2,1)} %copy-done.4, bf16[1024,2048]{1,0:T(8,128)(2,1)} %get-tuple-element.134, s32[]{:T(128)S(6)} %select_n.184), kind=kOutput, calls=%fused_computation.14 | convolution fusion | flops 4297064448 | bytes 10485764 | tf_op jit(solution)/shard_map/dot_general | solution.py:28
  312.5 9.6 %convolution_convert_fusion.5 = bf16[1024,2048]{1,0:T(8,128)(2,1)} fusion(bf16[1024,2048]{1,0:T(8,128)(2,1)} %copy-done.4, bf16[1024,2048]{1,0:T(8,128)(2,1)} %get-tuple-element.134, s32[]{:T(128)S(6)} %select_n.185), kind=kOutput, calls=%fused_computation.13 | convolution fusion | flops 4297064448 | bytes 10485764 | tf_op jit(solution)/shard_map/dot_general | solution.py:28
  322.1 11.8 %convolution_convert_fusion = bf16[2048,2048]{1,0:T(8,128)(2,1)} fusion(bf16[1024,2048]{1,0:T(8,128)(2,1)S(1)} %copy-done.43, bf16[1024,2048]{1,0:T(8,128)(2,1)S(1)} %copy-done.54), kind=kOutput, calls=%fused_computation.6 | convolution fusion | flops 8594128896 | bytes 16777216 | tf_op jit(solution)/shard_map/dot_general | solution.py:28
  343.4 13.8 %convolution_convert_fusion.1 = bf16[1024,2048]{1,0:T(8,128)(2,1)} fusion(bf16[1024,2048]{1,0:T(8,128)(2,1)} %get-tuple-element.134, bf16[2048,2048]{1,0:T(8,128)(2,1)} %param.22), kind=kOutput, calls=%fused_computation.9 | convolution fusion | flops 8592031744 | bytes 16777216 | tf_op jit(solution)/shard_map/dot_general | solution.py:28
  357.2 11.1 %collective-permute-done.31 = bf16[512,2048]{1,0:T(8,128)(2,1)} collective-permute-done((bf16[512,2048]{1,0:T(8,128)(2,1)}, bf16[512,2048]{1,0:T(8,128)(2,1)}, u32[]{:S(2)}, u32[]{:S(2)}) %collective-permute-start.31) | collective-permute-done | bytes 2097184 | tf_op jit(solution)/shard_map/ppermute | solution.py:334
  435.8 9.9 %collective-permute-done.44.refs_13_ = bf16[512,512]{1,0:T(8,128)(2,1)S(1)} collective-permute-done((bf16[512,512]{1,0:T(8,128)(2,1)S(1)}, bf16[512,512]{1,0:T(8,128)(2,1)S(1)}, u32[]{:S(2)}, u32[]{:S(2)}) %collective-permute-start.44) | collective-permute-done | bytes 524320 | tf_op jit(solution)/shard_map/ppermute | solution.py:185
  445.7 9.8 %collective-permute-done.38.refs_6_ = bf16[512,512]{1,0:T(8,128)(2,1)S(1)} collective-permute-done((bf16[512,512]{1,0:T(8,128)(2,1)S(1)}, bf16[512,512]{1,0:T(8,128)(2,1)S(1)}, u32[]{:S(2)}, u32[]{:S(2)}) %collective-permute-start.38) | collective-permute-done | bytes 524320 | tf_op jit(solution)/shard_map/ppermute | solution.py:185
  471.4 10.2 %shard_map.202 = (bf16[1024,2048]{1,0:T(8,128)(2,1)S(1)}, f32[1024,512]{1,0:T(8,128)S(1)}, f32[2,2048]{1,0:T(2,128)S(1)}) custom-call(s32[1]{0:T(128)} %bitcast.4.me, bf16[1024,2048]{1,0:T(8,128)(2,1)S(1)} %copy-done.7, bf16[1024,2048]{1,0:T(8,128)(2,1)S(1)} %copy-done.5, f32[1024,2048]{1,0:T(8,128)} %get-tuple-element.117.mid, ...), custom_call_target="tpu_custom_call" | custom-call | flops 1 | bytes 1 | tf_op jit(solution)/shard_map/pallas_call | solution.py:576
  485.9 14.9 %shard_map.203.g = bf16[1024,1536]{1,0:T(8,128)(2,1)S(1)} custom-call(bf16[3,1024,512]{2,1,0:T(8,128)(2,1)S(1)} %copy-done.18, bf16[1024,512]{1,0:T(8,128)(2,1)S(1)} %convolution_convert_fusion.9.g_att, f32[1024,128]{1,0:T(8,128)S(1)} %get-tuple-element.251.cosine, f32[1024,128]{1,0:T(8,128)S(1)} %get-tuple-element.252.sine, s32[1,1,1024]{2,1,0:T(1,128)S(1)} %bitcast.60, ...), custom_call_target="tpu_custom_call" | custom-call | flops 1 | bytes 1 | tf_op jit(solution)/shard_map/pallas_call | solution.py:126
  526.6 12.7 %shard_map.204 = (bf16[1024,2048]{1,0:T(8,128)(2,1)S(1)}, f32[1024,1]{1,0:T(8,128)S(1)}, f32[1024,1]{1,0:T(8,128)S(1)}, f32[2,2048]{1,0:T(2,128)S(1)}) custom-call(bf16[1024,1536]{1,0:T(8,128)(2,1)S(1)} %copy-done.11, bf16[3,2048,512]{2,1,0:T(8,128)(2,1)} %weight.3, bf16[1040,2048]{1,0:T(8,128)(2,1)S(1)} %bitcast.55, f32[1,2048]{1,0:T(1,128)S(1)} %copy-done.37), custom_call_target="tpu_custom_call" | custom-call | flops 1 | bytes 1 | tf_op jit(solution)/shard_map/pallas_call | solution.py:530
  549.6 14.2 %collective-permute-done.52 = bf16[512,1536]{1,0:T(8,128)(2,1)} collective-permute-done((bf16[512,1536]{1,0:T(8,128)(2,1)}, bf16[512,1536]{1,0:T(8,128)(2,1)}, u32[]{:S(2)}, u32[]{:S(2)}) %collective-permute-start.52) | collective-permute-done | bytes 1572896 | tf_op jit(solution)/shard_map/ppermute | solution.py:334
  578.3 10.4 %shard_map.205 = f32[1,2048,2048]{2,1,0:T(8,128)} custom-call(s32[8]{0:T(128)S(1)} %stack.130.table, bf16[512,2048]{1,0:T(8,128)(2,1)S(1)} %copy-done.15, bf16[512,2048]{1,0:T(8,128)(2,1)S(1)} %copy-done.22, bf16[512,2048]{1,0:T(8,128)(2,1)} %collective-permute-done.49.refs_2_, bf16[512,2048]{1,0:T(8,128)(2,1)} %collective-permute-done.50.refs_3_), custom_call_target="tpu_custom_call" | custom-call | flops 1 | bytes 1 | tf_op jit(solution)/shard_map/pallas_call | solution.py:398
  603.1 12.3 %shard_map.206 = f32[1,2048,2048]{2,1,0:T(8,128)} custom-call(s32[8]{0:T(128)S(1)} %stack.121.table, bf16[512,2048]{1,0:T(8,128)(2,1)} %constant_dynamic-update-slice_fusion.2.refs_0_, bf16[512,2048]{1,0:T(8,128)(2,1)} %collective-permute-done.51.refs_1_, bf16[512,2048]{1,0:T(8,128)(2,1)} %collective-permute-done.53.refs_2_, ...), custom_call_target="tpu_custom_call" | custom-call | flops 1 | bytes 1 | tf_op jit(solution)/shard_map/pallas_call | solution.py:398
  635.4 9.1 %collective-permute-done.61.refs_1_ = bf16[512,1536]{1,0:T(8,128)(2,1)} collective-permute-done((bf16[512,1536]{1,0:T(8,128)(2,1)}, bf16[512,1536]{1,0:T(8,128)(2,1)}, u32[]{:S(2)}, u32[]{:S(2)}) %collective-permute-start.61) | collective-permute-done | bytes 1572896 | tf_op jit(solution)/shard_map/ppermute | solution.py:281
  (352 shorter events, 380.5 us)
Async XLA Ops:
  7.2 137.7 %all-gather.5.cloned.1.call-start = ((), (), s32[]{:S(2)}) async-start(), calls=%async_computation.8 | async-start | bytes 1310720 | tf_op jit(solution)/shard_map/all_gather | solution.py:655
  49.6 42.2 %collective-permute-start.8 = (bf16[528,512]{1,0:T(8,128)(2,1)}, bf16[528,512]{1,0:T(8,128)(2,1)}, u32[]{:S(2)}, u32[]{:S(2)}) collective-permute-start(bf16[528,512]{1,0:T(8,128)(2,1)} %collective-permute-done.7.refs_9_), channel_id=1, source_target_pairs={{2,3},{6,7},{10,11},{14,15},{18,19},{22,23},{26,27},{30,31}} | collective-permute-start | bytes 1622024 | tf_op jit(solution)/shard_map/ppermute | solution.py:184
  59.2 32.6 %collective-permute-start.11 = (bf16[528,512]{1,0:T(8,128)(2,1)}, bf16[528,512]{1,0:T(8,128)(2,1)}, u32[]{:S(2)}, u32[]{:S(2)}) collective-permute-start(bf16[528,512]{1,0:T(8,128)(2,1)} %collective-permute-done.10.refs_12_), channel_id=1, source_target_pairs={{1,0},{5,4},{9,8},{13,12},{17,16},{21,20},{25,24},{29,28}} | collective-permute-start | bytes 1622024 | tf_op jit(solution)/shard_map/ppermute | solution.py:185
  99.8 121.0 %all-gather.7.cloned.1.call-start = ((), (), s32[]{:S(2)}) async-start(), calls=%async_computation.9 | async-start | bytes 9437184 | tf_op jit(solution)/shard_map/all_gather | solution.py:659
  99.9 40.0 %collective-permute-start.12 = (bf16[1024,512]{1,0:T(8,128)(2,1)}, bf16[1024,512]{1,0:T(8,128)(2,1)}, u32[]{:S(2)}, u32[]{:S(2)}) collective-permute-start(bf16[1024,512]{1,0:T(8,128)(2,1)} %refs_0_), channel_id=1, source_target_pairs={{0,1},{1,2},{2,3},{4,5},{5,6},{6,7},{8,9},{9,10},{10,11},{12,13},{... | collective-permute-start | bytes 3145736 | tf_op jit(solution)/shard_map/ppermute | solution.py:184
  102.2 42.8 %collective-permute-start.13 = (bf16[1024,512]{1,0:T(8,128)(2,1)}, bf16[1024,512]{1,0:T(8,128)(2,1)}, u32[]{:S(2)}, u32[]{:S(2)}) collective-permute-start(bf16[1024,512]{1,0:T(8,128)(2,1)} %refs_0_), channel_id=1, source_target_pairs={{1,0},{2,1},{3,2},{5,4},{6,5},{7,6},{9,8},{10,9},{11,10},{13,12},{... | collective-permute-start | bytes 3145736 | tf_op jit(solution)/shard_map/ppermute | solution.py:185
  145.0 232.9 %reduce-scatter.5.cloned.1.call-start = ((), (), s32[]{:S(2)}) async-start(), calls=%async_computation.4 | async-start | bytes 5242880 | tf_op jit(solution)/shard_map/reduce_scatter | solution.py:679
  222.5 24.8 %collective-permute-start.27 = (bf16[1024,512]{1,0:T(8,128)(2,1)}, bf16[1024,512]{1,0:T(8,128)(2,1)}, u32[]{:S(2)}, u32[]{:S(2)}) collective-permute-start(bf16[1024,512]{1,0:T(8,128)(2,1)} %collective-permute-done.13.refs_4_), channel_id=1, source_target_pairs={{1,0},{2,1},{5,4},{6,5},{9,8},{10,9},{13,12},{14,13},{17,16},{18,1... | collective-permute-start | bytes 3145736 | tf_op jit(solution)/shard_map/ppermute | solution.py:185
  302.8 161.4 %reduce-scatter.7.cloned.1.call-start = ((), (), s32[]{:S(2)}) async-start(), calls=%async_computation.5 | async-start | bytes 9437184 | tf_op jit(solution)/shard_map/reduce_scatter | solution.py:685
  341.9 202.5 %reduce-scatter.9.cloned.1.call-start = ((), (), s32[]{:S(2)}) async-start(), calls=%async_computation.6 | async-start | bytes 5242880 | tf_op jit(solution)/shard_map/reduce_scatter | solution.py:695
  341.9 26.4 %collective-permute-start.31 = (bf16[512,2048]{1,0:T(8,128)(2,1)}, bf16[512,2048]{1,0:T(8,128)(2,1)}, u32[]{:S(2)}, u32[]{:S(2)}) collective-permute-start(bf16[512,2048]{1,0:T(8,128)(2,1)} %get-tuple-element.136), channel_id=1, source_target_pairs={{0,8},{4,20},{8,0},{12,28},{16,24},{20,4},{24,16},{28,12},{1,9},{5... | collective-permute-start | bytes 6291464 | tf_op jit(solution)/shard_map/ppermute | solution.py:334
  377.8 24.2 %collective-permute-start.34 = (bf16[256,2048]{1,0:T(8,128)(2,1)}, bf16[256,2048]{1,0:T(8,128)(2,1)S(1)}, u32[]{:S(2)}, u32[]{:S(2)}) collective-permute-start(bf16[256,2048]{1,0:T(8,128)(2,1)} %get-tuple-element.139), channel_id=1, source_target_pairs={{0,16},{4,12},{8,24},{12,4},{16,0},{20,28},{24,8},{28,20},{1,17},{... | collective-permute-start | bytes 3145736 | tf_op jit(solution)/shard_map/ppermute | solution.py:334
  414.0 44.2 %collective-permute-start.45 = (bf16[256,2048]{1,0:T(8,128)(2,1)S(1)}, bf16[256,2048]{1,0:T(8,128)(2,1)}, u32[]{:S(2)}, u32[]{:S(2)}) collective-permute-start(bf16[256,2048]{1,0:T(8,128)(2,1)S(1)} %add_convert_fusion.5), channel_id=1, source_target_pairs={{0,16},{4,12},{8,24},{12,4},{16,0},{20,28},{24,8},{28,20},{1,17},{... | collective-permute-start | bytes 3145736 | tf_op jit(solution)/shard_map/ppermute | solution.py:281
  464.2 169.7 %reduce-scatter.11.cloned.1.call-start = ((), (), s32[]{:S(2)}) async-start(), calls=%async_computation.7 | async-start | bytes 5242880 | tf_op jit(solution)/shard_map/reduce_scatter | solution.py:704
  467.1 37.3 %collective-permute-start.46 = (bf16[512,2048]{1,0:T(8,128)(2,1)S(1)}, bf16[512,2048]{1,0:T(8,128)(2,1)S(1)}, u32[]{:S(2)}, u32[]{:S(2)}) collective-permute-start(bf16[512,2048]{1,0:T(8,128)(2,1)S(1)} %constant_dynamic-update-slice_fusion.refs_0_), channel_id=1, source_target_pairs={{0,8},{4,20},{8,0},{12,28},{16,24},{20,4},{24,16},{28,12},{1,9},{5... | collective-permute-start | bytes 6291464 | tf_op jit(solution)/shard_map/ppermute | solution.py:281
  468.6 32.3 %collective-permute-start.47 = (bf16[256,2048]{1,0:T(8,128)(2,1)}, bf16[256,2048]{1,0:T(8,128)(2,1)S(1)}, u32[]{:S(2)}, u32[]{:S(2)}) collective-permute-start(bf16[256,2048]{1,0:T(8,128)(2,1)} %reduce-scatter.7.cloned.1.call-done), channel_id=1, source_target_pairs={{0,16},{4,12},{8,24},{12,4},{16,0},{20,28},{24,8},{28,20},{1,17},{... | collective-permute-start | bytes 3145736 | tf_op jit(solution)/shard_map/ppermute | solution.py:281
  509.8 34.6 %collective-permute-start.49 = (bf16[512,2048]{1,0:T(8,128)(2,1)}, bf16[512,2048]{1,0:T(8,128)(2,1)}, u32[]{:S(2)}, u32[]{:S(2)}) collective-permute-start(bf16[512,2048]{1,0:T(8,128)(2,1)} %copy-done.14), channel_id=1, source_target_pairs={{0,4},{4,0},{8,12},{12,8},{16,20},{20,16},{24,28},{28,24},{1,5},{5... | collective-permute-start | bytes 6291464 | tf_op jit(solution)/shard_map/ppermute | solution.py:281
  510.3 34.1 %collective-permute-start.50 = (bf16[512,2048]{1,0:T(8,128)(2,1)}, bf16[512,2048]{1,0:T(8,128)(2,1)}, u32[]{:S(2)}, u32[]{:S(2)}) collective-permute-start(bf16[512,2048]{1,0:T(8,128)(2,1)} %copy-done.21), channel_id=1, source_target_pairs={{0,4},{4,0},{8,12},{12,8},{16,20},{20,16},{24,28},{28,24},{1,5},{5... | collective-permute-start | bytes 6291464 | tf_op jit(solution)/shard_map/ppermute | solution.py:281
  515.0 29.3 %collective-permute-start.51 = (bf16[512,2048]{1,0:T(8,128)(2,1)}, bf16[512,2048]{1,0:T(8,128)(2,1)}, u32[]{:S(2)}, u32[]{:S(2)}) collective-permute-start(bf16[512,2048]{1,0:T(8,128)(2,1)} %constant_dynamic-update-slice_fusion.2.refs_0_), channel_id=1, source_target_pairs={{0,8},{4,20},{8,0},{12,28},{16,24},{20,4},{24,16},{28,12},{1,9},{5... | collective-permute-start | bytes 6291464 | tf_op jit(solution)/shard_map/ppermute | solution.py:281
  544.4 26.9 %collective-permute-start.53 = (bf16[512,2048]{1,0:T(8,128)(2,1)}, bf16[512,2048]{1,0:T(8,128)(2,1)}, u32[]{:S(2)}, u32[]{:S(2)}) collective-permute-start(bf16[512,2048]{1,0:T(8,128)(2,1)} %constant_dynamic-update-slice_fusion.2.refs_0_), channel_id=1, source_target_pairs={{0,4},{4,0},{8,12},{12,8},{16,20},{20,16},{24,28},{28,24},{1,5},{5... | collective-permute-start | bytes 6291464 | tf_op jit(solution)/shard_map/ppermute | solution.py:281
  544.4 26.8 %collective-permute-start.54 = (bf16[512,2048]{1,0:T(8,128)(2,1)}, bf16[512,2048]{1,0:T(8,128)(2,1)}, u32[]{:S(2)}, u32[]{:S(2)}) collective-permute-start(bf16[512,2048]{1,0:T(8,128)(2,1)} %collective-permute-done.51.refs_1_), channel_id=1, source_target_pairs={{0,4},{4,0},{8,12},{12,8},{16,20},{20,16},{24,28},{28,24},{1,5},{5... | collective-permute-start | bytes 6291464 | tf_op jit(solution)/shard_map/ppermute | solution.py:281
  549.5 39.1 %collective-permute-start.56 = (bf16[256,2048]{1,0:T(8,128)(2,1)}, bf16[256,2048]{1,0:T(8,128)(2,1)}, u32[]{:S(2)}, u32[]{:S(2)}) collective-permute-start(bf16[256,2048]{1,0:T(8,128)(2,1)} %convolution_convert_fusion.8), channel_id=1, source_target_pairs={{0,4},{4,0},{8,12},{12,8},{16,20},{20,16},{24,28},{28,24},{1,5},{5... | collective-permute-start | bytes 3145736 | tf_op jit(solution)/shard_map/ppermute | solution.py:316
  645.0 24.1 %collective-permute-start.66 = (bf16[512,1536]{1,0:T(8,128)(2,1)}, bf16[512,1536]{1,0:T(8,128)(2,1)S(1)}, u32[]{:S(2)}, u32[]{:S(2)}) collective-permute-start(bf16[512,1536]{1,0:T(8,128)(2,1)} %constant_dynamic-update-slice_fusion.4.refs_0_), channel_id=1, source_target_pairs={{0,4},{4,0},{8,12},{12,8},{16,20},{20,16},{24,28},{28,24},{1,5},{5... | collective-permute-start | bytes 4718600 | tf_op jit(solution)/shard_map/ppermute | solution.py:281
  645.0 24.1 %collective-permute-start.67 = (bf16[512,1536]{1,0:T(8,128)(2,1)}, bf16[512,1536]{1,0:T(8,128)(2,1)S(1)}, u32[]{:S(2)}, u32[]{:S(2)}) collective-permute-start(bf16[512,1536]{1,0:T(8,128)(2,1)} %collective-permute-done.61.refs_1_), channel_id=1, source_target_pairs={{0,4},{4,0},{8,12},{12,8},{16,20},{20,16},{24,28},{28,24},{1,5},{5... | collective-permute-start | bytes 4718600 | tf_op jit(solution)/shard_map/ppermute | solution.py:281
  (113 other events, 1570.6 us)
Sparse Core Ops, SparseCore 0:
  99.9 38.9 all-gather.4
  145.1 53.0 all-gather.6
  302.9 74.8 reduce-scatter.4
  382.1 81.9 reduce-scatter.6
  466.9 76.7 reduce-scatter.8
  546.5 78.6 reduce-scatter.10

commit v3 on v2

--- a/solution.py
+++ b/solution.py
@@ -94,12 +94,12 @@
     return triple, plain, table, seg_row, seg_col
 
 
-def attn_forward(lin, cos_t, sin_t, segs):
+def attn_forward(lin, cos_t, sin_t, segs, seg_col):
     tokens = lin.shape[0]
     cols = lin.shape[1] // 3
     heads = cols // HEAD_DIM
     rows, row_len = segs.shape
-    triple, plain, table, seg_row, seg_col = attention_specs(row_len)
+    triple, plain, table, row_spec, col_spec = attention_specs(row_len)
     block = min(QUERY_BLOCK, row_len)
     parts = [
         pl.BlockSpec((row_len, HEAD_DIM), lambda r, h, s=s: (r, s * heads + h)) for s in range(3)
@@ -107,7 +107,7 @@
     return pl.pallas_call(
         functools.partial(attn_fwd_kernel, block, HEAD_DIM**-0.5),
         grid=(rows, heads),
-        in_specs=[*parts, table, table, seg_row, seg_col],
+        in_specs=[*parts, table, table, row_spec, col_spec],
         out_specs=[plain, triple],
         out_shape=[
             jax.ShapeDtypeStruct((tokens, cols), bf16),
@@ -115,24 +115,24 @@
         ],
         compiler_params=pltpu.CompilerParams(vmem_limit_bytes=VMEM),
         cost_estimate=COST,
-    )(lin, lin, lin, cos_t, sin_t, segs[:, None, :], segs.reshape(tokens, 1))
-
-
-def attn_backward(rot, g_att, cos_t, sin_t, segs):
+    )(lin, lin, lin, cos_t, sin_t, segs[:, None, :], seg_col)
+
+
+def attn_backward(rot, g_att, cos_t, sin_t, segs, seg_col):
     _, tokens, cols = rot.shape
     rows, row_len = segs.shape
-    triple, plain, table, seg_row, seg_col = attention_specs(row_len)
+    triple, plain, table, row_spec, col_spec = attention_specs(row_len)
     block = min(QUERY_BLOCK, row_len)
     return pl.pallas_call(
         functools.partial(attn_bwd_kernel, block, HEAD_DIM**-0.5),
         grid=(rows, cols // HEAD_DIM),
-        in_specs=[triple, plain, table, table, seg_row, seg_col],
+        in_specs=[triple, plain, table, table, row_spec, col_spec],
         out_specs=pl.BlockSpec((row_len, 3 * cols), lambda r, h: (r, 0)),
         out_shape=jax.ShapeDtypeStruct((tokens, 3 * cols), bf16),
         scratch_shapes=[pltpu.VMEM((row_len, HEAD_DIM), f32)] * 2,
         compiler_params=pltpu.CompilerParams(vmem_limit_bytes=VMEM),
         cost_estimate=COST,
-    )(rot, g_att, cos_t, sin_t, segs[:, None, :], segs.reshape(tokens, 1))
+    )(rot, g_att, cos_t, sin_t, segs[:, None, :], seg_col)
 
 
 def after(value, *deps):
@@ -643,6 +643,9 @@
     first, second = split_rows(inputs)
     chunks = [first, jnp.concatenate([second, packed])]
     starts = [line_step(1, c, c) for c in chunks]
+    starts[0], cos_t, sin_t, seg_col = lax.optimization_barrier(
+        (starts[0], cos_t, sin_t, segment_ids.reshape(tokens, 1))
+    )
     parts = [line_parts(c, pair) for c, pair in zip(chunks, starts)]
     gy_own = after(grad_result, *(p[1][min(1, mp_size - 2)] for p in parts))
     gathered = join(parts)
@@ -654,7 +657,7 @@
     slab = lax.dynamic_slice_in_dim(proj_weight, lax.axis_index("dp") * part, part, 0)
     slab = lax.all_gather(after(slab, gathered), "mp", axis=0)
     attn_rows, lin = norm_qkv(gathered, tokens, qkv_weight, gain_a, bias_a)
-    att, rot = attn_forward(lin, cos_t, sin_t, segment_ids)
+    att, rot = attn_forward(lin, cos_t, sin_t, segment_ids, seg_col)
     att, slab, gy_steps[0] = lax.optimization_barrier((att, slab, gy_steps[0]))
     proj_full = lax.all_gather(slab, "dp", axis=0)
     att_full, proj_full = lax.optimization_barrier((line_gather(split_rows(att)), proj_full))
@@ -696,18 +699,19 @@
 
     grad_mid_low, grad_mid_own, ffn_vec = mid_backward(g_ffn, gy, mid, gain_f)
     g_att = dot(grad_mid_low, proj_weight, NT).astype(bf16)
-    g_qkv_rows = attn_backward(rot, g_att, cos_t, sin_t, segment_ids)
-    (g_qkv_rows,) = meet((g_qkv_rows,), down, up)
+    g_qkv_rows = attn_backward(rot, g_att, cos_t, sin_t, segment_ids, seg_col)
+    (g_qkv_rows,) = meet((g_qkv_rows,), down)
     qkv = Halving(lambda half: dot(half_lanes(attn_rows, half), g_qkv_rows, TN).astype(bf16))
-    (later,) = meet((g_qkv_rows,), qkv)
+    (later,) = meet((g_qkv_rows,), qkv, up)
     g_attn_low, plain, cross, attn_vec = attn_in_backward(later, qkv_weight, gathered, gain_a)
     g_attn = lax.psum_scatter(g_attn_low, "mp", scatter_dimension=1, tiled=True).astype(f32)
 
-    mid_later, _, ffn_out = meet((grad_mid_low, g_attn_low, ffn_out), down, up)
+    mid_later, _, ffn_out = meet((grad_mid_low, g_attn_low, ffn_out), down)
     proj = Halving(lambda half: dot(half_lanes(att, half), mid_later, TN).astype(bf16))
-    proj.x = meet(proj.x, qkv, up)
+    proj.x = meet(proj.x, qkv)
     down.x = after(down.x, proj.x)
-    (grad_down,) = meet((down.finish()[0],), qkv, proj)
+    (grad_down,) = meet((down.finish()[0],), qkv, proj, up)
+    (grad_down,) = meet((grad_down,), qkv, proj)
     up.x = after(up.x, grad_down)
     (grad_up,) = meet((up.finish()[0],), qkv, proj)
     sums = jnp.concatenate([attn_vec, jnp.stack([plain, cross]).reshape(-1, width)])

time: 695 us -> 685 us (0.986)
  waiting for transfers between devices: 247 us -> 239 us
    ppermute x16 -> x17, waiting for transfers between devices: 18.5 us -> 5.87 us  [launch(): got = tuple((lax.ppermute(p, 'dp', dp_pairs(bits)) for p in self.x))]
    unnamed x122 -> x125, local copies, waits for them, and re-layouts: 41.6 us -> 42.1 us
  transfers between devices with their start and end apart: 78 -> 79, of which waited for: 39 -> 38; matrix products, arithmetic and copies ran while one was open for 21% -> 21% of each run, Pallas kernels for 16% -> 17%
where the time goes in v3:
time: 685 us; the launch traced here: 675 us
  waiting for transfers between devices  239 us (35%)
  Pallas kernels  120 us (18%)
  matrix products  109 us (16%)
  starting transfers between devices  91.1 us (13%)
  local copies, waits for them, and re-layouts  55.4 us (8%)
  other arithmetic  43.9 us (6%)
  between operations  15.8 us (2%)
    ppermute x21, waiting for transfers between devices, line_step(): lax.ppermute(left, 'mp', [(i, i - 1) for i in range(1, n - s + 1)])  151 us
    dot_general x12, matrix products, dot(): return lax.dot_general(a, b, dims, preferred_element_type=f32)  109 us
    unnamed x125, local copies, waits for them, and re-layouts  42.1 us
    ppermute x21, starting transfers between devices, line_step(): lax.ppermute(right, 'mp', [(i, i + 1) for i in range(s - 1, n - 1)])  39.7 us
    pallas_call x4, Pallas kernels, widen(): pl.pallas_call(functools.partial(widen_kernel, firsts), grid_spec=pltpu.P...  37.2 us
    ppermute x6, waiting for transfers between devices, launch(): self.flight = lax.ppermute(sent, 'dp', dp_pairs(bits))  36.3 us
    ppermute x21, waiting for transfers between devices, line_step(): lax.ppermute(right, 'mp', [(i, i + 1) for i in range(s - 1, n - 1)])  28.9 us
    ppermute x21, starting transfers between devices, line_step(): lax.ppermute(left, 'mp', [(i, i - 1) for i in range(1, n - s + 1)])  27.7 us
  transfers between devices with their start and end apart: 79, of which 38 were waited for; matrix products, arithmetic and copies ran while one was open for 21% of the time, Pallas kernels for 17%

profile of v3, /device:TPU:0, one launch (start us, length us, event | category | flops | bytes accessed | tf_op | source)
XLA Modules:
  0.0 674.7 jit_solution(11480010426589215003)
XLA Ops:
  70.7 19.3 %collective-permute-done.5.refs_6_ = bf16[512,512]{1,0:T(8,128)(2,1)} collective-permute-done((bf16[512,512]{1,0:T(8,128)(2,1)}, bf16[512,512]{1,0:T(8,128)(2,1)}, u32[]{:S(2)}, u32[]{:S(2)}) %collective-permute-start.5) | collective-permute-done | bytes 524320 | tf_op jit(solution)/shard_map/ppermute | solution.py:185
  106.9 12.3 %shard_map.196 = (bf16[1024,2048]{1,0:T(8,128)(2,1)S(1)}, f32[1024,1536]{1,0:T(8,128)S(1)}) custom-call(bf16[1040,2048]{1,0:T(8,128)(2,1)S(1)} %copy-done.2, bf16[3,2048,512]{2,1,0:T(8,128)(2,1)} %weight.3, f32[1,2048]{1,0:T(1,128)S(1)} %get-tuple-element.243.gain, f32[1,2048]{1,0:T(1,128)S(1)} %get-tuple-element.241.bias), custom_call_target="tpu_custom_call" | custom-call | flops 1 | bytes 1 | tf_op jit(solution)/shard_map/pallas_call | solution.py:450
  119.2 11.9 %shard_map.197 = (bf16[1024,512]{1,0:T(8,128)(2,1)S(1)}, bf16[3,1024,512]{2,1,0:T(8,128)(2,1)S(1)}) custom-call(f32[1024,1536]{1,0:T(8,128)S(1)} %get-tuple-element.117.q_lin.k_lin.v_lin, f32[1024,1536]{1,0:T(8,128)S(1)} %get-tuple-element.117.q_lin.k_lin.v_lin, f32[1024,1536]{1,0:T(8,128)S(1)} %get-tuple-element.117.q_lin.k_lin.v_lin, ...), custom_call_target="tpu_custom_call" | custom-call | flops 1 | bytes 1 | tf_op jit(solution)/shard_map/pallas_call | solution.py:107
  177.0 9.2 %collective-permute-done.18.refs_5_ = bf16[512,512]{1,0:T(8,128)(2,1)S(1)} collective-permute-done((bf16[512,512]{1,0:T(8,128)(2,1)S(1)}, bf16[512,512]{1,0:T(8,128)(2,1)S(1)}, u32[]{:S(2)}, u32[]{:S(2)}) %collective-permute-start.18) | collective-permute-done | bytes 524320 | tf_op jit(solution)/shard_map/ppermute | solution.py:185
  188.3 9.2 %collective-permute-done.24.refs_12_ = bf16[512,512]{1,0:T(8,128)(2,1)S(1)} collective-permute-done((bf16[512,512]{1,0:T(8,128)(2,1)S(1)}, bf16[512,512]{1,0:T(8,128)(2,1)S(1)}, u32[]{:S(2)}, u32[]{:S(2)}) %collective-permute-start.24) | collective-permute-done | bytes 524320 | tf_op jit(solution)/shard_map/ppermute | solution.py:185
  198.8 9.9 %collective-permute-done.19.refs_6_ = bf16[512,512]{1,0:T(8,128)(2,1)S(1)} collective-permute-done((bf16[512,512]{1,0:T(8,128)(2,1)S(1)}, bf16[512,512]{1,0:T(8,128)(2,1)S(1)}, u32[]{:S(2)}, u32[]{:S(2)}) %collective-permute-start.19) | collective-permute-done | bytes 524320 | tf_op jit(solution)/shard_map/ppermute | solution.py:185
  228.0 16.1 %shard_map.199 = (f32[1024,2048]{1,0:T(8,128)}, bf16[1024,2048]{1,0:T(8,128)(2,1)S(1)}) custom-call(bf16[1024,2048]{1,0:T(8,128)(2,1)S(1)} %copy-done.9, bf16[8,4,64,2048]{3,2,1,0:T(8,128)(2,1)} %bitcast.63, bf16[1040,2048]{1,0:T(8,128)(2,1)S(1)} %copy-done.3, f32[1,2048]{1,0:T(1,128)S(1)} %get-tuple-element.242.gain, f32[1,2048]{1,0:T(1,128)S(1)} %get-tuple-element.240.bias), custom_call_target="tpu_custom_call" | custom-call | flops 1 | bytes 1 | tf_op jit(solution)/shard_map/pallas_call | solution.py:487
  248.7 14.1 %multiply_convert_fusion.1 = (bf16[1024,2048]{1,0:T(8,128)(2,1)}, f32[1024,2048]{1,0:T(8,128)}) fusion(bf16[1024,2048]{1,0:T(8,128)(2,1)S(1)} %get-tuple-element.143, bf16[2048,2048]{1,0:T(8,128)(2,1)} %param.21, s32[1024]{0:T(1024)S(1)} %bitcast.72, s32[2048]{0:T(1024)S(1)} %iota_add_fusion), kind=kOutput, calls=%fused_computation.4 | convolution fusion | flops 8600420352 | bytes 25178112 | tf_op jit(solution)/shard_map/dot_general | solution.py:28
  272.9 14.3 %multiply_convert_fusion = bf16[1024,2048]{1,0:T(8,128)(2,1)S(1)} fusion(f32[1024,2048]{1,0:T(8,128)} %get-tuple-element.137, bf16[1024,2048]{1,0:T(8,128)(2,1)S(1)} %shard_map.200.gy, bf16[2048,2048]{1,0:T(8,128)(2,1)} %param.22), kind=kOutput, calls=%fused_computation.3 | convolution fusion | flops 8596226048 | bytes 25165824 | tf_op jit(solution)/shard_map/dot_general | solution.py:28
  289.2 12.9 %convolution_convert_fusion.2 = bf16[1024,2048]{1,0:T(8,128)(2,1)} fusion(bf16[1024,2048]{1,0:T(8,128)(2,1)S(1)} %multiply_convert_fusion, bf16[2048,2048]{1,0:T(8,128)(2,1)} %param.21), kind=kOutput, calls=%fused_computation.10 | convolution fusion | flops 8592031744 | bytes 16777216 | tf_op jit(solution)/shard_map/dot_general | solution.py:28
  302.4 9.4 %convolution_convert_fusion.6 = bf16[1024,2048]{1,0:T(8,128)(2,1)} fusion(bf16[1024,2048]{1,0:T(8,128)(2,1)} %copy-done.4, bf16[1024,2048]{1,0:T(8,128)(2,1)} %get-tuple-element.145, s32[]{:T(128)S(6)} %select_n.184), kind=kOutput, calls=%fused_computation.14 | convolution fusion | flops 4297064448 | bytes 10485764 | tf_op jit(solution)/shard_map/dot_general | solution.py:28
  311.9 9.6 %convolution_convert_fusion.5 = bf16[1024,2048]{1,0:T(8,128)(2,1)} fusion(bf16[1024,2048]{1,0:T(8,128)(2,1)} %copy-done.4, bf16[1024,2048]{1,0:T(8,128)(2,1)} %get-tuple-element.145, s32[]{:T(128)S(6)} %select_n.185), kind=kOutput, calls=%fused_computation.13 | convolution fusion | flops 4297064448 | bytes 10485764 | tf_op jit(solution)/shard_map/dot_general | solution.py:28
  321.5 11.8 %convolution_convert_fusion = bf16[2048,2048]{1,0:T(8,128)(2,1)} fusion(bf16[1024,2048]{1,0:T(8,128)(2,1)S(1)} %copy-done.47, bf16[1024,2048]{1,0:T(8,128)(2,1)S(1)} %copy-done.56), kind=kOutput, calls=%fused_computation.6 | convolution fusion | flops 8594128896 | bytes 16777216 | tf_op jit(solution)/shard_map/dot_general | solution.py:28
  342.8 13.8 %convolution_convert_fusion.1 = bf16[1024,2048]{1,0:T(8,128)(2,1)} fusion(bf16[1024,2048]{1,0:T(8,128)(2,1)} %get-tuple-element.145, bf16[2048,2048]{1,0:T(8,128)(2,1)} %param.22), kind=kOutput, calls=%fused_computation.9 | convolution fusion | flops 8592031744 | bytes 16777216 | tf_op jit(solution)/shard_map/dot_general | solution.py:28
  356.6 11.1 %collective-permute-done.31 = bf16[512,2048]{1,0:T(8,128)(2,1)} collective-permute-done((bf16[512,2048]{1,0:T(8,128)(2,1)}, bf16[512,2048]{1,0:T(8,128)(2,1)}, u32[]{:S(2)}, u32[]{:S(2)}) %collective-permute-start.31) | collective-permute-done | bytes 2097184 | tf_op jit(solution)/shard_map/ppermute | solution.py:334
  435.1 9.9 %collective-permute-done.44.refs_13_ = bf16[512,512]{1,0:T(8,128)(2,1)S(1)} collective-permute-done((bf16[512,512]{1,0:T(8,128)(2,1)S(1)}, bf16[512,512]{1,0:T(8,128)(2,1)S(1)}, u32[]{:S(2)}, u32[]{:S(2)}) %collective-permute-start.44) | collective-permute-done | bytes 524320 | tf_op jit(solution)/shard_map/ppermute | solution.py:185
  445.1 9.8 %collective-permute-done.38.refs_6_ = bf16[512,512]{1,0:T(8,128)(2,1)S(1)} collective-permute-done((bf16[512,512]{1,0:T(8,128)(2,1)S(1)}, bf16[512,512]{1,0:T(8,128)(2,1)S(1)}, u32[]{:S(2)}, u32[]{:S(2)}) %collective-permute-start.38) | collective-permute-done | bytes 524320 | tf_op jit(solution)/shard_map/ppermute | solution.py:185
  470.1 10.3 %shard_map.202 = (bf16[1024,2048]{1,0:T(8,128)(2,1)S(1)}, f32[1024,512]{1,0:T(8,128)S(1)}, f32[2,2048]{1,0:T(2,128)S(1)}) custom-call(s32[1]{0:T(128)} %bitcast.4.me, bf16[1024,2048]{1,0:T(8,128)(2,1)S(1)} %copy-done.7, bf16[1024,2048]{1,0:T(8,128)(2,1)S(1)} %copy-done.5, f32[1024,2048]{1,0:T(8,128)} %get-tuple-element.128.mid, ...), custom_call_target="tpu_custom_call" | custom-call | flops 1 | bytes 1 | tf_op jit(solution)/shard_map/pallas_call | solution.py:576
  484.8 14.9 %shard_map.203.g = bf16[1024,1536]{1,0:T(8,128)(2,1)S(1)} custom-call(bf16[3,1024,512]{2,1,0:T(8,128)(2,1)S(1)} %copy-done.18, bf16[1024,512]{1,0:T(8,128)(2,1)S(1)} %convolution_convert_fusion.9.g_att, f32[1024,128]{1,0:T(8,128)S(1)} %get-tuple-element.118.cosine, f32[1024,128]{1,0:T(8,128)S(1)} %get-tuple-element.119.sine, s32[1,1,1024]{2,1,0:T(1,128)S(1)} %bitcast.60, ...), custom_call_target="tpu_custom_call" | custom-call | flops 1 | bytes 1 | tf_op jit(solution)/shard_map/pallas_call | solution.py:126
  521.0 12.7 %shard_map.204 = (bf16[1024,2048]{1,0:T(8,128)(2,1)S(1)}, f32[1024,1]{1,0:T(8,128)S(1)}, f32[1024,1]{1,0:T(8,128)S(1)}, f32[2,2048]{1,0:T(2,128)S(1)}) custom-call(bf16[1024,1536]{1,0:T(8,128)(2,1)S(1)} %copy-done.11, bf16[3,2048,512]{2,1,0:T(8,128)(2,1)} %weight.3, bf16[1040,2048]{1,0:T(8,128)(2,1)S(1)} %bitcast.55, f32[1,2048]{1,0:T(1,128)S(1)} %copy-done.41), custom_call_target="tpu_custom_call" | custom-call | flops 1 | bytes 1 | tf_op jit(solution)/shard_map/pallas_call | solution.py:530
  559.3 10.6 %shard_map.205 = f32[1,2048,2048]{2,1,0:T(8,128)} custom-call(s32[8]{0:T(128)S(1)} %stack.130.table, bf16[512,2048]{1,0:T(8,128)(2,1)S(1)} %copy-done.15, bf16[512,2048]{1,0:T(8,128)(2,1)S(1)} %copy-done.24, bf16[512,2048]{1,0:T(8,128)(2,1)} %collective-permute-done.49.refs_2_, bf16[512,2048]{1,0:T(8,128)(2,1)} %collective-permute-done.50.refs_3_), custom_call_target="tpu_custom_call" | custom-call | flops 1 | bytes 1 | tf_op jit(solution)/shard_map/pallas_call | solution.py:398
  581.5 13.6 %collective-permute-done.56 = bf16[128,2048]{1,0:T(8,128)(2,1)} collective-permute-done((bf16[128,2048]{1,0:T(8,128)(2,1)}, bf16[128,2048]{1,0:T(8,128)(2,1)}, u32[]{:S(2)}, u32[]{:S(2)}) %collective-permute-start.56) | collective-permute-done | bytes 524320 | tf_op jit(solution)/shard_map/ppermute | solution.py:334
  612.2 12.4 %shard_map.206 = f32[1,2048,2048]{2,1,0:T(8,128)} custom-call(s32[8]{0:T(128)S(1)} %stack.121.table, bf16[512,2048]{1,0:T(8,128)(2,1)} %constant_dynamic-update-slice_fusion.2.refs_0_, bf16[512,2048]{1,0:T(8,128)(2,1)} %collective-permute-done.54.refs_1_, bf16[512,2048]{1,0:T(8,128)(2,1)} %collective-permute-done.57.refs_2_, ...), custom_call_target="tpu_custom_call" | custom-call | flops 1 | bytes 1 | tf_op jit(solution)/shard_map/pallas_call | solution.py:398
  652.6 10.1 %shard_map.207 = f32[3,2048,512]{2,1,0:T(8,128)} custom-call(s32[8]{0:T(128)S(1)} %stack.130.table, bf16[512,1536]{1,0:T(8,128)(2,1)} %constant_dynamic-update-slice_fusion.4.refs_0_, bf16[512,1536]{1,0:T(8,128)(2,1)} %collective-permute-done.59.refs_1_, bf16[512,1536]{1,0:T(8,128)(2,1)} %collective-permute-done.63.refs_2_, ...), custom_call_target="tpu_custom_call" | custom-call | flops 1 | bytes 1 | tf_op jit(solution)/shard_map/pallas_call | solution.py:398
  (357 shorter events, 369.5 us)
Async XLA Ops:
  7.2 137.0 %all-gather.5.cloned.1.call-start = ((), (), s32[]{:S(2)}) async-start(), calls=%async_computation.8 | async-start | bytes 1310720 | tf_op jit(solution)/shard_map/all_gather | solution.py:658
  50.1 39.9 %collective-permute-start.8 = (bf16[528,512]{1,0:T(8,128)(2,1)}, bf16[528,512]{1,0:T(8,128)(2,1)}, u32[]{:S(2)}, u32[]{:S(2)}) collective-permute-start(bf16[528,512]{1,0:T(8,128)(2,1)} %collective-permute-done.7.refs_9_), channel_id=1, source_target_pairs={{2,3},{6,7},{10,11},{14,15},{18,19},{22,23},{26,27},{30,31}} | collective-permute-start | bytes 1622024 | tf_op jit(solution)/shard_map/ppermute | solution.py:184
  57.4 32.6 %collective-permute-start.11 = (bf16[528,512]{1,0:T(8,128)(2,1)}, bf16[528,512]{1,0:T(8,128)(2,1)}, u32[]{:S(2)}, u32[]{:S(2)}) collective-permute-start(bf16[528,512]{1,0:T(8,128)(2,1)} %collective-permute-done.10.refs_12_), channel_id=1, source_target_pairs={{1,0},{5,4},{9,8},{13,12},{17,16},{21,20},{25,24},{29,28}} | collective-permute-start | bytes 1622024 | tf_op jit(solution)/shard_map/ppermute | solution.py:185
  99.1 121.0 %all-gather.7.cloned.1.call-start = ((), (), s32[]{:S(2)}) async-start(), calls=%async_computation.9 | async-start | bytes 9437184 | tf_op jit(solution)/shard_map/all_gather | solution.py:662
  99.1 40.0 %collective-permute-start.12 = (bf16[1024,512]{1,0:T(8,128)(2,1)}, bf16[1024,512]{1,0:T(8,128)(2,1)}, u32[]{:S(2)}, u32[]{:S(2)}) collective-permute-start(bf16[1024,512]{1,0:T(8,128)(2,1)} %refs_0_), channel_id=1, source_target_pairs={{0,1},{1,2},{2,3},{4,5},{5,6},{6,7},{8,9},{9,10},{10,11},{12,13},{... | collective-permute-start | bytes 3145736 | tf_op jit(solution)/shard_map/ppermute | solution.py:184
  101.4 42.8 %collective-permute-start.13 = (bf16[1024,512]{1,0:T(8,128)(2,1)}, bf16[1024,512]{1,0:T(8,128)(2,1)}, u32[]{:S(2)}, u32[]{:S(2)}) collective-permute-start(bf16[1024,512]{1,0:T(8,128)(2,1)} %refs_0_), channel_id=1, source_target_pairs={{1,0},{2,1},{3,2},{5,4},{6,5},{7,6},{9,8},{10,9},{11,10},{13,12},{... | collective-permute-start | bytes 3145736 | tf_op jit(solution)/shard_map/ppermute | solution.py:185
  144.2 233.0 %reduce-scatter.5.cloned.1.call-start = ((), (), s32[]{:S(2)}) async-start(), calls=%async_computation.4 | async-start | bytes 5242880 | tf_op jit(solution)/shard_map/reduce_scatter | solution.py:682
  220.1 24.1 %collective-permute-start.26 = (bf16[1024,512]{1,0:T(8,128)(2,1)}, bf16[1024,512]{1,0:T(8,128)(2,1)}, u32[]{:S(2)}, u32[]{:S(2)}) collective-permute-start(bf16[1024,512]{1,0:T(8,128)(2,1)} %collective-permute-done.12.refs_1_), channel_id=1, source_target_pairs={{1,2},{2,3},{5,6},{6,7},{9,10},{10,11},{13,14},{14,15},{17,18},{18... | collective-permute-start | bytes 3145736 | tf_op jit(solution)/shard_map/ppermute | solution.py:184
  221.8 24.8 %collective-permute-start.27 = (bf16[1024,512]{1,0:T(8,128)(2,1)}, bf16[1024,512]{1,0:T(8,128)(2,1)}, u32[]{:S(2)}, u32[]{:S(2)}) collective-permute-start(bf16[1024,512]{1,0:T(8,128)(2,1)} %collective-permute-done.13.refs_4_), channel_id=1, source_target_pairs={{1,0},{2,1},{5,4},{6,5},{9,8},{10,9},{13,12},{14,13},{17,16},{18,1... | collective-permute-start | bytes 3145736 | tf_op jit(solution)/shard_map/ppermute | solution.py:185
  247.3 23.8 %collective-permute-start.29 = (bf16[1024,512]{1,0:T(8,128)(2,1)}, bf16[1024,512]{1,0:T(8,128)(2,1)S(1)}, u32[]{:S(2)}, u32[]{:S(2)}) collective-permute-start(bf16[1024,512]{1,0:T(8,128)(2,1)} %collective-permute-done.27.refs_5_), channel_id=1, source_target_pairs={{1,0},{5,4},{9,8},{13,12},{17,16},{21,20},{25,24},{29,28}} | collective-permute-start | bytes 3145736 | tf_op jit(solution)/shard_map/ppermute | solution.py:185
  302.2 161.3 %reduce-scatter.7.cloned.1.call-start = ((), (), s32[]{:S(2)}) async-start(), calls=%async_computation.5 | async-start | bytes 9437184 | tf_op jit(solution)/shard_map/reduce_scatter | solution.py:688
  341.2 205.2 %reduce-scatter.9.cloned.1.call-start = ((), (), s32[]{:S(2)}) async-start(), calls=%async_computation.6 | async-start | bytes 5242880 | tf_op jit(solution)/shard_map/reduce_scatter | solution.py:698
  341.3 26.4 %collective-permute-start.31 = (bf16[512,2048]{1,0:T(8,128)(2,1)}, bf16[512,2048]{1,0:T(8,128)(2,1)}, u32[]{:S(2)}, u32[]{:S(2)}) collective-permute-start(bf16[512,2048]{1,0:T(8,128)(2,1)} %get-tuple-element.147), channel_id=1, source_target_pairs={{0,8},{4,20},{8,0},{12,28},{16,24},{20,4},{24,16},{28,12},{1,9},{5... | collective-permute-start | bytes 6291464 | tf_op jit(solution)/shard_map/ppermute | solution.py:334
  377.2 24.2 %collective-permute-start.34 = (bf16[256,2048]{1,0:T(8,128)(2,1)}, bf16[256,2048]{1,0:T(8,128)(2,1)S(1)}, u32[]{:S(2)}, u32[]{:S(2)}) collective-permute-start(bf16[256,2048]{1,0:T(8,128)(2,1)} %get-tuple-element.150), channel_id=1, source_target_pairs={{0,16},{4,12},{8,24},{12,4},{16,0},{20,28},{24,8},{28,20},{1,17},{... | collective-permute-start | bytes 3145736 | tf_op jit(solution)/shard_map/ppermute | solution.py:334
  413.3 44.2 %collective-permute-start.45 = (bf16[256,2048]{1,0:T(8,128)(2,1)S(1)}, bf16[256,2048]{1,0:T(8,128)(2,1)}, u32[]{:S(2)}, u32[]{:S(2)}) collective-permute-start(bf16[256,2048]{1,0:T(8,128)(2,1)S(1)} %add_convert_fusion.5), channel_id=1, source_target_pairs={{0,16},{4,12},{8,24},{12,4},{16,0},{20,28},{24,8},{28,20},{1,17},{... | collective-permute-start | bytes 3145736 | tf_op jit(solution)/shard_map/ppermute | solution.py:281
  463.5 171.9 %reduce-scatter.11.cloned.1.call-start = ((), (), s32[]{:S(2)}) async-start(), calls=%async_computation.7 | async-start | bytes 5242880 | tf_op jit(solution)/shard_map/reduce_scatter | solution.py:707
  466.5 33.2 %collective-permute-start.46 = (bf16[512,2048]{1,0:T(8,128)(2,1)S(1)}, bf16[512,2048]{1,0:T(8,128)(2,1)S(1)}, u32[]{:S(2)}, u32[]{:S(2)}) collective-permute-start(bf16[512,2048]{1,0:T(8,128)(2,1)S(1)} %constant_dynamic-update-slice_fusion.refs_0_), channel_id=1, source_target_pairs={{0,8},{4,20},{8,0},{12,28},{16,24},{20,4},{24,16},{28,12},{1,9},{5... | collective-permute-start | bytes 6291464 | tf_op jit(solution)/shard_map/ppermute | solution.py:281
  505.9 40.5 %collective-permute-start.49 = (bf16[512,2048]{1,0:T(8,128)(2,1)}, bf16[512,2048]{1,0:T(8,128)(2,1)}, u32[]{:S(2)}, u32[]{:S(2)}) collective-permute-start(bf16[512,2048]{1,0:T(8,128)(2,1)} %copy-done.14), channel_id=1, source_target_pairs={{0,4},{4,0},{8,12},{12,8},{16,20},{20,16},{24,28},{28,24},{1,5},{5... | collective-permute-start | bytes 6291464 | tf_op jit(solution)/shard_map/ppermute | solution.py:281
  506.0 40.3 %collective-permute-start.50 = (bf16[512,2048]{1,0:T(8,128)(2,1)}, bf16[512,2048]{1,0:T(8,128)(2,1)}, u32[]{:S(2)}, u32[]{:S(2)}) collective-permute-start(bf16[512,2048]{1,0:T(8,128)(2,1)} %copy-done.23), channel_id=1, source_target_pairs={{0,4},{4,0},{8,12},{12,8},{16,20},{20,16},{24,28},{28,24},{1,5},{5... | collective-permute-start | bytes 6291464 | tf_op jit(solution)/shard_map/ppermute | solution.py:281
  520.2 23.2 %collective-permute-start.51 = (bf16[512,1536]{1,0:T(8,128)(2,1)}, bf16[512,1536]{1,0:T(8,128)(2,1)}, u32[]{:S(2)}, u32[]{:S(2)}) collective-permute-start(bf16[512,1536]{1,0:T(8,128)(2,1)} %get-tuple-element.179), channel_id=1, source_target_pairs={{0,8},{4,20},{8,0},{12,28},{16,24},{20,4},{24,16},{28,12},{1,9},{5... | collective-permute-start | bytes 4718600 | tf_op jit(solution)/shard_map/ppermute | solution.py:334
  542.1 36.9 %collective-permute-start.54 = (bf16[512,2048]{1,0:T(8,128)(2,1)}, bf16[512,2048]{1,0:T(8,128)(2,1)}, u32[]{:S(2)}, u32[]{:S(2)}) collective-permute-start(bf16[512,2048]{1,0:T(8,128)(2,1)} %constant_dynamic-update-slice_fusion.2.refs_0_), channel_id=1, source_target_pairs={{0,8},{4,20},{8,0},{12,28},{16,24},{20,4},{24,16},{28,12},{1,9},{5... | collective-permute-start | bytes 6291464 | tf_op jit(solution)/shard_map/ppermute | solution.py:281
  581.0 31.2 %collective-permute-start.57 = (bf16[512,2048]{1,0:T(8,128)(2,1)}, bf16[512,2048]{1,0:T(8,128)(2,1)}, u32[]{:S(2)}, u32[]{:S(2)}) collective-permute-start(bf16[512,2048]{1,0:T(8,128)(2,1)} %constant_dynamic-update-slice_fusion.2.refs_0_), channel_id=1, source_target_pairs={{0,4},{4,0},{8,12},{12,8},{16,20},{20,16},{24,28},{28,24},{1,5},{5... | collective-permute-start | bytes 6291464 | tf_op jit(solution)/shard_map/ppermute | solution.py:281
  581.0 31.2 %collective-permute-start.58 = (bf16[512,2048]{1,0:T(8,128)(2,1)}, bf16[512,2048]{1,0:T(8,128)(2,1)}, u32[]{:S(2)}, u32[]{:S(2)}) collective-permute-start(bf16[512,2048]{1,0:T(8,128)(2,1)} %collective-permute-done.54.refs_1_), channel_id=1, source_target_pairs={{0,4},{4,0},{8,12},{12,8},{16,20},{20,16},{24,28},{28,24},{1,5},{5... | collective-permute-start | bytes 6291464 | tf_op jit(solution)/shard_map/ppermute | solution.py:281
  601.3 23.3 %collective-permute-start.59 = (bf16[512,1536]{1,0:T(8,128)(2,1)}, bf16[512,1536]{1,0:T(8,128)(2,1)}, u32[]{:S(2)}, u32[]{:S(2)}) collective-permute-start(bf16[512,1536]{1,0:T(8,128)(2,1)} %constant_dynamic-update-slice_fusion.4.refs_0_), channel_id=1, source_target_pairs={{0,8},{4,20},{8,0},{12,28},{16,24},{20,4},{24,16},{28,12},{1,9},{5... | collective-permute-start | bytes 4718600 | tf_op jit(solution)/shard_map/ppermute | solution.py:281
  (116 other events, 1653.1 us)
Sparse Core Ops, SparseCore 0:
  99.2 38.9 all-gather.4
  144.3 53.0 all-gather.6
  302.3 74.8 reduce-scatter.4
  381.5 81.9 reduce-scatter.6
  466.2 76.7 reduce-scatter.8
  545.8 77.9 reduce-scatter.10

commit v4 on v3

--- a/solution.py
+++ b/solution.py
@@ -707,11 +707,18 @@
     g_attn = lax.psum_scatter(g_attn_low, "mp", scatter_dimension=1, tiled=True).astype(f32)
 
     mid_later, _, ffn_out = meet((grad_mid_low, g_attn_low, ffn_out), down)
-    proj = Halving(lambda half: dot(half_lanes(att, half), mid_later, TN).astype(bf16))
-    proj.x = meet(proj.x, qkv)
-    down.x = after(down.x, proj.x)
-    (grad_down,) = meet((down.finish()[0],), qkv, proj, up)
-    (grad_down,) = meet((grad_down,), qkv, proj)
+    made = []
+
+    def make_proj(half):
+        rows = mid_later
+        if made:
+            rows, _ = meet((mid_later, made[0]), qkv)
+        made.append(dot(half_lanes(att, half), rows, TN).astype(bf16))
+        return made[-1]
+
+    proj = Halving(make_proj)
+    (down.x,) = meet((after(down.x, proj.x),), qkv, proj, up)
+    (grad_down,) = meet((down.finish()[0],), qkv, proj)
     up.x = after(up.x, grad_down)
     (grad_up,) = meet((up.finish()[0],), qkv, proj)
     sums = jnp.concatenate([attn_vec, jnp.stack([plain, cross]).reshape(-1, width)])

time: 685 us -> 684 us (level)
  no operation moved by 1% of the time
where the time goes in v4:
time: 684 us; the launch traced here: 673 us
  waiting for transfers between devices  238 us (35%)
  Pallas kernels  120 us (18%)
  matrix products  108 us (16%)
  starting transfers between devices  90.9 us (13%)
  local copies, waits for them, and re-layouts  55.5 us (8%)
  other arithmetic  44.7 us (7%)
  between operations  15.9 us (2%)
    ppermute x21, waiting for transfers between devices, line_step(): lax.ppermute(left, 'mp', [(i, i - 1) for i in range(1, n - s + 1)])  151 us
    dot_general x12, matrix products, dot(): return lax.dot_general(a, b, dims, preferred_element_type=f32)  108 us
    unnamed x125, local copies, waits for them, and re-layouts  42.1 us
    ppermute x21, starting transfers between devices, line_step(): lax.ppermute(right, 'mp', [(i, i + 1) for i in range(s - 1, n - 1)])  39.7 us
    pallas_call x4, Pallas kernels, widen(): pl.pallas_call(functools.partial(widen_kernel, firsts), grid_spec=pltpu.P...  37.2 us
    ppermute x6, waiting for transfers between devices, launch(): self.flight = lax.ppermute(sent, 'dp', dp_pairs(bits))  34.1 us
    ppermute x21, waiting for transfers between devices, line_step(): lax.ppermute(right, 'mp', [(i, i + 1) for i in range(s - 1, n - 1)])  28.9 us
    convert_element_type x9, other arithmetic, add(): return sum((a.astype(f32) for a in terms)).astype(bf16)  28.2 us
  transfers between devices with their start and end apart: 79, of which 38 were waited for; matrix products, arithmetic and copies ran while one was open for 21% of the time, Pallas kernels for 17%

profile of v4, /device:TPU:0, one launch (start us, length us, event | category | flops | bytes accessed | tf_op | source)
XLA Modules:
  0.0 673.2 jit_solution(10995902791005762436)
XLA Ops:
  70.7 19.3 %collective-permute-done.5.refs_6_ = bf16[512,512]{1,0:T(8,128)(2,1)} collective-permute-done((bf16[512,512]{1,0:T(8,128)(2,1)}, bf16[512,512]{1,0:T(8,128)(2,1)}, u32[]{:S(2)}, u32[]{:S(2)}) %collective-permute-start.5) | collective-permute-done | bytes 524320 | tf_op jit(solution)/shard_map/ppermute | solution.py:185
  106.9 12.3 %shard_map.196 = (bf16[1024,2048]{1,0:T(8,128)(2,1)S(1)}, f32[1024,1536]{1,0:T(8,128)S(1)}) custom-call(bf16[1040,2048]{1,0:T(8,128)(2,1)S(1)} %copy-done.2, bf16[3,2048,512]{2,1,0:T(8,128)(2,1)} %weight.3, f32[1,2048]{1,0:T(1,128)S(1)} %get-tuple-element.249.gain, f32[1,2048]{1,0:T(1,128)S(1)} %get-tuple-element.247.bias), custom_call_target="tpu_custom_call" | custom-call | flops 1 | bytes 1 | tf_op jit(solution)/shard_map/pallas_call | solution.py:450
  119.2 11.9 %shard_map.197 = (bf16[1024,512]{1,0:T(8,128)(2,1)S(1)}, bf16[3,1024,512]{2,1,0:T(8,128)(2,1)S(1)}) custom-call(f32[1024,1536]{1,0:T(8,128)S(1)} %get-tuple-element.120.q_lin.k_lin.v_lin, f32[1024,1536]{1,0:T(8,128)S(1)} %get-tuple-element.120.q_lin.k_lin.v_lin, f32[1024,1536]{1,0:T(8,128)S(1)} %get-tuple-element.120.q_lin.k_lin.v_lin, ...), custom_call_target="tpu_custom_call" | custom-call | flops 1 | bytes 1 | tf_op jit(solution)/shard_map/pallas_call | solution.py:107
  177.0 9.2 %collective-permute-done.18.refs_5_ = bf16[512,512]{1,0:T(8,128)(2,1)S(1)} collective-permute-done((bf16[512,512]{1,0:T(8,128)(2,1)S(1)}, bf16[512,512]{1,0:T(8,128)(2,1)S(1)}, u32[]{:S(2)}, u32[]{:S(2)}) %collective-permute-start.18) | collective-permute-done | bytes 524320 | tf_op jit(solution)/shard_map/ppermute | solution.py:185
  188.3 9.2 %collective-permute-done.24.refs_12_ = bf16[512,512]{1,0:T(8,128)(2,1)S(1)} collective-permute-done((bf16[512,512]{1,0:T(8,128)(2,1)S(1)}, bf16[512,512]{1,0:T(8,128)(2,1)S(1)}, u32[]{:S(2)}, u32[]{:S(2)}) %collective-permute-start.24) | collective-permute-done | bytes 524320 | tf_op jit(solution)/shard_map/ppermute | solution.py:185
  198.8 9.9 %collective-permute-done.19.refs_6_ = bf16[512,512]{1,0:T(8,128)(2,1)S(1)} collective-permute-done((bf16[512,512]{1,0:T(8,128)(2,1)S(1)}, bf16[512,512]{1,0:T(8,128)(2,1)S(1)}, u32[]{:S(2)}, u32[]{:S(2)}) %collective-permute-start.19) | collective-permute-done | bytes 524320 | tf_op jit(solution)/shard_map/ppermute | solution.py:185
  228.0 16.1 %shard_map.199 = (f32[1024,2048]{1,0:T(8,128)}, bf16[1024,2048]{1,0:T(8,128)(2,1)S(1)}) custom-call(bf16[1024,2048]{1,0:T(8,128)(2,1)S(1)} %copy-done.9, bf16[8,4,64,2048]{3,2,1,0:T(8,128)(2,1)} %bitcast.63, bf16[1040,2048]{1,0:T(8,128)(2,1)S(1)} %copy-done.3, f32[1,2048]{1,0:T(1,128)S(1)} %get-tuple-element.248.gain, f32[1,2048]{1,0:T(1,128)S(1)} %get-tuple-element.246.bias), custom_call_target="tpu_custom_call" | custom-call | flops 1 | bytes 1 | tf_op jit(solution)/shard_map/pallas_call | solution.py:487
  248.7 14.1 %multiply_convert_fusion.1 = (bf16[1024,2048]{1,0:T(8,128)(2,1)}, f32[1024,2048]{1,0:T(8,128)}) fusion(bf16[1024,2048]{1,0:T(8,128)(2,1)S(1)} %get-tuple-element.146, bf16[2048,2048]{1,0:T(8,128)(2,1)} %param.21, s32[1024]{0:T(1024)S(1)} %bitcast.72, s32[2048]{0:T(1024)S(1)} %iota_add_fusion), kind=kOutput, calls=%fused_computation.4 | convolution fusion | flops 8600420352 | bytes 25178112 | tf_op jit(solution)/shard_map/dot_general | solution.py:28
  272.9 14.3 %multiply_convert_fusion = bf16[1024,2048]{1,0:T(8,128)(2,1)S(1)} fusion(f32[1024,2048]{1,0:T(8,128)} %get-tuple-element.140, bf16[1024,2048]{1,0:T(8,128)(2,1)S(1)} %shard_map.200.gy, bf16[2048,2048]{1,0:T(8,128)(2,1)} %param.22), kind=kOutput, calls=%fused_computation.3 | convolution fusion | flops 8596226048 | bytes 25165824 | tf_op jit(solution)/shard_map/dot_general | solution.py:28
  289.2 12.9 %convolution_convert_fusion.2 = bf16[1024,2048]{1,0:T(8,128)(2,1)} fusion(bf16[1024,2048]{1,0:T(8,128)(2,1)S(1)} %multiply_convert_fusion, bf16[2048,2048]{1,0:T(8,128)(2,1)} %param.21), kind=kOutput, calls=%fused_computation.10 | convolution fusion | flops 8592031744 | bytes 16777216 | tf_op jit(solution)/shard_map/dot_general | solution.py:28
  302.4 9.4 %convolution_convert_fusion.6 = bf16[1024,2048]{1,0:T(8,128)(2,1)} fusion(bf16[1024,2048]{1,0:T(8,128)(2,1)} %copy-done.4, bf16[1024,2048]{1,0:T(8,128)(2,1)} %get-tuple-element.148, s32[]{:T(128)S(6)} %select_n.184), kind=kOutput, calls=%fused_computation.14 | convolution fusion | flops 4297064448 | bytes 10485764 | tf_op jit(solution)/shard_map/dot_general | solution.py:28
  311.9 9.6 %convolution_convert_fusion.5 = bf16[1024,2048]{1,0:T(8,128)(2,1)} fusion(bf16[1024,2048]{1,0:T(8,128)(2,1)} %copy-done.4, bf16[1024,2048]{1,0:T(8,128)(2,1)} %get-tuple-element.148, s32[]{:T(128)S(6)} %select_n.185), kind=kOutput, calls=%fused_computation.13 | convolution fusion | flops 4297064448 | bytes 10485764 | tf_op jit(solution)/shard_map/dot_general | solution.py:28
  321.5 11.8 %convolution_convert_fusion = bf16[2048,2048]{1,0:T(8,128)(2,1)} fusion(bf16[1024,2048]{1,0:T(8,128)(2,1)S(1)} %copy-done.47, bf16[1024,2048]{1,0:T(8,128)(2,1)S(1)} %copy-done.56), kind=kOutput, calls=%fused_computation.6 | convolution fusion | flops 8594128896 | bytes 16777216 | tf_op jit(solution)/shard_map/dot_general | solution.py:28
  342.8 13.8 %convolution_convert_fusion.1 = bf16[1024,2048]{1,0:T(8,128)(2,1)} fusion(bf16[1024,2048]{1,0:T(8,128)(2,1)} %get-tuple-element.148, bf16[2048,2048]{1,0:T(8,128)(2,1)} %param.22), kind=kOutput, calls=%fused_computation.9 | convolution fusion | flops 8592031744 | bytes 16777216 | tf_op jit(solution)/shard_map/dot_general | solution.py:28
  356.6 11.1 %collective-permute-done.31 = bf16[512,2048]{1,0:T(8,128)(2,1)} collective-permute-done((bf16[512,2048]{1,0:T(8,128)(2,1)}, bf16[512,2048]{1,0:T(8,128)(2,1)}, u32[]{:S(2)}, u32[]{:S(2)}) %collective-permute-start.31) | collective-permute-done | bytes 2097184 | tf_op jit(solution)/shard_map/ppermute | solution.py:334
  435.1 9.9 %collective-permute-done.44.refs_13_ = bf16[512,512]{1,0:T(8,128)(2,1)S(1)} collective-permute-done((bf16[512,512]{1,0:T(8,128)(2,1)S(1)}, bf16[512,512]{1,0:T(8,128)(2,1)S(1)}, u32[]{:S(2)}, u32[]{:S(2)}) %collective-permute-start.44) | collective-permute-done | bytes 524320 | tf_op jit(solution)/shard_map/ppermute | solution.py:185
  445.1 9.8 %collective-permute-done.38.refs_6_ = bf16[512,512]{1,0:T(8,128)(2,1)S(1)} collective-permute-done((bf16[512,512]{1,0:T(8,128)(2,1)S(1)}, bf16[512,512]{1,0:T(8,128)(2,1)S(1)}, u32[]{:S(2)}, u32[]{:S(2)}) %collective-permute-start.38) | collective-permute-done | bytes 524320 | tf_op jit(solution)/shard_map/ppermute | solution.py:185
  470.1 10.3 %shard_map.202 = (bf16[1024,2048]{1,0:T(8,128)(2,1)S(1)}, f32[1024,512]{1,0:T(8,128)S(1)}, f32[2,2048]{1,0:T(2,128)S(1)}) custom-call(s32[1]{0:T(128)} %bitcast.4.me, bf16[1024,2048]{1,0:T(8,128)(2,1)S(1)} %copy-done.7, bf16[1024,2048]{1,0:T(8,128)(2,1)S(1)} %copy-done.5, f32[1024,2048]{1,0:T(8,128)} %get-tuple-element.131.mid, ...), custom_call_target="tpu_custom_call" | custom-call | flops 1 | bytes 1 | tf_op jit(solution)/shard_map/pallas_call | solution.py:576
  484.8 14.9 %shard_map.203.g = bf16[1024,1536]{1,0:T(8,128)(2,1)S(1)} custom-call(bf16[3,1024,512]{2,1,0:T(8,128)(2,1)S(1)} %copy-done.18, bf16[1024,512]{1,0:T(8,128)(2,1)S(1)} %convolution_convert_fusion.9.g_att, f32[1024,128]{1,0:T(8,128)S(1)} %get-tuple-element.121.cosine, f32[1024,128]{1,0:T(8,128)S(1)} %get-tuple-element.122.sine, s32[1,1,1024]{2,1,0:T(1,128)S(1)} %bitcast.60, ...), custom_call_target="tpu_custom_call" | custom-call | flops 1 | bytes 1 | tf_op jit(solution)/shard_map/pallas_call | solution.py:126
  521.0 12.7 %shard_map.204 = (bf16[1024,2048]{1,0:T(8,128)(2,1)S(1)}, f32[1024,1]{1,0:T(8,128)S(1)}, f32[1024,1]{1,0:T(8,128)S(1)}, f32[2,2048]{1,0:T(2,128)S(1)}) custom-call(bf16[1024,1536]{1,0:T(8,128)(2,1)S(1)} %copy-done.11, bf16[3,2048,512]{2,1,0:T(8,128)(2,1)} %weight.3, bf16[1040,2048]{1,0:T(8,128)(2,1)S(1)} %bitcast.55, f32[1,2048]{1,0:T(1,128)S(1)} %copy-done.41), custom_call_target="tpu_custom_call" | custom-call | flops 1 | bytes 1 | tf_op jit(solution)/shard_map/pallas_call | solution.py:530
  555.8 15.9 %collective-permute-done.52 = bf16[256,1536]{1,0:T(8,128)(2,1)} collective-permute-done((bf16[256,1536]{1,0:T(8,128)(2,1)}, bf16[256,1536]{1,0:T(8,128)(2,1)}, u32[]{:S(2)}, u32[]{:S(2)}) %collective-permute-start.52) | collective-permute-done | bytes 786464 | tf_op jit(solution)/shard_map/ppermute | solution.py:334
  582.9 10.6 %shard_map.205 = f32[1,2048,2048]{2,1,0:T(8,128)} custom-call(s32[8]{0:T(128)S(1)} %stack.130.table, bf16[512,2048]{1,0:T(8,128)(2,1)S(1)} %copy-done.15, bf16[512,2048]{1,0:T(8,128)(2,1)S(1)} %copy-done.24, bf16[512,2048]{1,0:T(8,128)(2,1)} %collective-permute-done.49.refs_2_, bf16[512,2048]{1,0:T(8,128)(2,1)} %collective-permute-done.50.refs_3_), custom_call_target="tpu_custom_call" | custom-call | flops 1 | bytes 1 | tf_op jit(solution)/shard_map/pallas_call | solution.py:398
  611.2 12.4 %shard_map.206 = f32[1,2048,2048]{2,1,0:T(8,128)} custom-call(s32[8]{0:T(128)S(1)} %stack.121.table, bf16[512,2048]{1,0:T(8,128)(2,1)} %constant_dynamic-update-slice_fusion.2.refs_0_, bf16[512,2048]{1,0:T(8,128)(2,1)} %collective-permute-done.54.refs_1_, bf16[512,2048]{1,0:T(8,128)(2,1)} %collective-permute-done.57.refs_2_, ...), custom_call_target="tpu_custom_call" | custom-call | flops 1 | bytes 1 | tf_op jit(solution)/shard_map/pallas_call | solution.py:398
  651.1 10.1 %shard_map.207 = f32[3,2048,512]{2,1,0:T(8,128)} custom-call(s32[8]{0:T(128)S(1)} %stack.130.table, bf16[512,1536]{1,0:T(8,128)(2,1)} %constant_dynamic-update-slice_fusion.4.refs_0_, bf16[512,1536]{1,0:T(8,128)(2,1)} %collective-permute-done.59.refs_1_, bf16[512,1536]{1,0:T(8,128)(2,1)} %collective-permute-done.63.refs_2_, ...), custom_call_target="tpu_custom_call" | custom-call | flops 1 | bytes 1 | tf_op jit(solution)/shard_map/pallas_call | solution.py:398
  (357 shorter events, 365.7 us)
Async XLA Ops:
  7.2 137.0 %all-gather.5.cloned.1.call-start = ((), (), s32[]{:S(2)}) async-start(), calls=%async_computation.8 | async-start | bytes 1310720 | tf_op jit(solution)/shard_map/all_gather | solution.py:658
  50.1 39.9 %collective-permute-start.8 = (bf16[528,512]{1,0:T(8,128)(2,1)}, bf16[528,512]{1,0:T(8,128)(2,1)}, u32[]{:S(2)}, u32[]{:S(2)}) collective-permute-start(bf16[528,512]{1,0:T(8,128)(2,1)} %collective-permute-done.7.refs_9_), channel_id=1, source_target_pairs={{2,3},{6,7},{10,11},{14,15},{18,19},{22,23},{26,27},{30,31}} | collective-permute-start | bytes 1622024 | tf_op jit(solution)/shard_map/ppermute | solution.py:184
  57.4 32.6 %collective-permute-start.11 = (bf16[528,512]{1,0:T(8,128)(2,1)}, bf16[528,512]{1,0:T(8,128)(2,1)}, u32[]{:S(2)}, u32[]{:S(2)}) collective-permute-start(bf16[528,512]{1,0:T(8,128)(2,1)} %collective-permute-done.10.refs_12_), channel_id=1, source_target_pairs={{1,0},{5,4},{9,8},{13,12},{17,16},{21,20},{25,24},{29,28}} | collective-permute-start | bytes 1622024 | tf_op jit(solution)/shard_map/ppermute | solution.py:185
  99.1 121.0 %all-gather.7.cloned.1.call-start = ((), (), s32[]{:S(2)}) async-start(), calls=%async_computation.9 | async-start | bytes 9437184 | tf_op jit(solution)/shard_map/all_gather | solution.py:662
  99.1 40.0 %collective-permute-start.12 = (bf16[1024,512]{1,0:T(8,128)(2,1)}, bf16[1024,512]{1,0:T(8,128)(2,1)}, u32[]{:S(2)}, u32[]{:S(2)}) collective-permute-start(bf16[1024,512]{1,0:T(8,128)(2,1)} %refs_0_), channel_id=1, source_target_pairs={{0,1},{1,2},{2,3},{4,5},{5,6},{6,7},{8,9},{9,10},{10,11},{12,13},{... | collective-permute-start | bytes 3145736 | tf_op jit(solution)/shard_map/ppermute | solution.py:184
  101.4 42.8 %collective-permute-start.13 = (bf16[1024,512]{1,0:T(8,128)(2,1)}, bf16[1024,512]{1,0:T(8,128)(2,1)}, u32[]{:S(2)}, u32[]{:S(2)}) collective-permute-start(bf16[1024,512]{1,0:T(8,128)(2,1)} %refs_0_), channel_id=1, source_target_pairs={{1,0},{2,1},{3,2},{5,4},{6,5},{7,6},{9,8},{10,9},{11,10},{13,12},{... | collective-permute-start | bytes 3145736 | tf_op jit(solution)/shard_map/ppermute | solution.py:185
  144.2 233.0 %reduce-scatter.5.cloned.1.call-start = ((), (), s32[]{:S(2)}) async-start(), calls=%async_computation.4 | async-start | bytes 5242880 | tf_op jit(solution)/shard_map/reduce_scatter | solution.py:682
  220.1 24.1 %collective-permute-start.26 = (bf16[1024,512]{1,0:T(8,128)(2,1)}, bf16[1024,512]{1,0:T(8,128)(2,1)}, u32[]{:S(2)}, u32[]{:S(2)}) collective-permute-start(bf16[1024,512]{1,0:T(8,128)(2,1)} %collective-permute-done.12.refs_1_), channel_id=1, source_target_pairs={{1,2},{2,3},{5,6},{6,7},{9,10},{10,11},{13,14},{14,15},{17,18},{18... | collective-permute-start | bytes 3145736 | tf_op jit(solution)/shard_map/ppermute | solution.py:184
  221.8 24.8 %collective-permute-start.27 = (bf16[1024,512]{1,0:T(8,128)(2,1)}, bf16[1024,512]{1,0:T(8,128)(2,1)}, u32[]{:S(2)}, u32[]{:S(2)}) collective-permute-start(bf16[1024,512]{1,0:T(8,128)(2,1)} %collective-permute-done.13.refs_4_), channel_id=1, source_target_pairs={{1,0},{2,1},{5,4},{6,5},{9,8},{10,9},{13,12},{14,13},{17,16},{18,1... | collective-permute-start | bytes 3145736 | tf_op jit(solution)/shard_map/ppermute | solution.py:185
  247.3 23.8 %collective-permute-start.29 = (bf16[1024,512]{1,0:T(8,128)(2,1)}, bf16[1024,512]{1,0:T(8,128)(2,1)S(1)}, u32[]{:S(2)}, u32[]{:S(2)}) collective-permute-start(bf16[1024,512]{1,0:T(8,128)(2,1)} %collective-permute-done.27.refs_5_), channel_id=1, source_target_pairs={{1,0},{5,4},{9,8},{13,12},{17,16},{21,20},{25,24},{29,28}} | collective-permute-start | bytes 3145736 | tf_op jit(solution)/shard_map/ppermute | solution.py:185
  302.2 161.3 %reduce-scatter.7.cloned.1.call-start = ((), (), s32[]{:S(2)}) async-start(), calls=%async_computation.5 | async-start | bytes 9437184 | tf_op jit(solution)/shard_map/reduce_scatter | solution.py:688
  341.2 205.2 %reduce-scatter.9.cloned.1.call-start = ((), (), s32[]{:S(2)}) async-start(), calls=%async_computation.6 | async-start | bytes 5242880 | tf_op jit(solution)/shard_map/reduce_scatter | solution.py:698
  341.3 26.4 %collective-permute-start.31 = (bf16[512,2048]{1,0:T(8,128)(2,1)}, bf16[512,2048]{1,0:T(8,128)(2,1)}, u32[]{:S(2)}, u32[]{:S(2)}) collective-permute-start(bf16[512,2048]{1,0:T(8,128)(2,1)} %get-tuple-element.150), channel_id=1, source_target_pairs={{0,8},{4,20},{8,0},{12,28},{16,24},{20,4},{24,16},{28,12},{1,9},{5... | collective-permute-start | bytes 6291464 | tf_op jit(solution)/shard_map/ppermute | solution.py:334
  377.2 24.2 %collective-permute-start.34 = (bf16[256,2048]{1,0:T(8,128)(2,1)}, bf16[256,2048]{1,0:T(8,128)(2,1)S(1)}, u32[]{:S(2)}, u32[]{:S(2)}) collective-permute-start(bf16[256,2048]{1,0:T(8,128)(2,1)} %get-tuple-element.153), channel_id=1, source_target_pairs={{0,16},{4,12},{8,24},{12,4},{16,0},{20,28},{24,8},{28,20},{1,17},{... | collective-permute-start | bytes 3145736 | tf_op jit(solution)/shard_map/ppermute | solution.py:334
  413.3 44.2 %collective-permute-start.45 = (bf16[256,2048]{1,0:T(8,128)(2,1)S(1)}, bf16[256,2048]{1,0:T(8,128)(2,1)}, u32[]{:S(2)}, u32[]{:S(2)}) collective-permute-start(bf16[256,2048]{1,0:T(8,128)(2,1)S(1)} %add_convert_fusion.5), channel_id=1, source_target_pairs={{0,16},{4,12},{8,24},{12,4},{16,0},{20,28},{24,8},{28,20},{1,17},{... | collective-permute-start | bytes 3145736 | tf_op jit(solution)/shard_map/ppermute | solution.py:281
  463.5 170.4 %reduce-scatter.11.cloned.1.call-start = ((), (), s32[]{:S(2)}) async-start(), calls=%async_computation.7 | async-start | bytes 5242880 | tf_op jit(solution)/shard_map/reduce_scatter | solution.py:707
  466.5 33.2 %collective-permute-start.46 = (bf16[512,2048]{1,0:T(8,128)(2,1)S(1)}, bf16[512,2048]{1,0:T(8,128)(2,1)S(1)}, u32[]{:S(2)}, u32[]{:S(2)}) collective-permute-start(bf16[512,2048]{1,0:T(8,128)(2,1)S(1)} %constant_dynamic-update-slice_fusion.refs_0_), channel_id=1, source_target_pairs={{0,8},{4,20},{8,0},{12,28},{16,24},{20,4},{24,16},{28,12},{1,9},{5... | collective-permute-start | bytes 6291464 | tf_op jit(solution)/shard_map/ppermute | solution.py:281
  505.9 40.5 %collective-permute-start.49 = (bf16[512,2048]{1,0:T(8,128)(2,1)}, bf16[512,2048]{1,0:T(8,128)(2,1)}, u32[]{:S(2)}, u32[]{:S(2)}) collective-permute-start(bf16[512,2048]{1,0:T(8,128)(2,1)} %copy-done.14), channel_id=1, source_target_pairs={{0,4},{4,0},{8,12},{12,8},{16,20},{20,16},{24,28},{28,24},{1,5},{5... | collective-permute-start | bytes 6291464 | tf_op jit(solution)/shard_map/ppermute | solution.py:281
  506.0 40.4 %collective-permute-start.50 = (bf16[512,2048]{1,0:T(8,128)(2,1)}, bf16[512,2048]{1,0:T(8,128)(2,1)}, u32[]{:S(2)}, u32[]{:S(2)}) collective-permute-start(bf16[512,2048]{1,0:T(8,128)(2,1)} %copy-done.23), channel_id=1, source_target_pairs={{0,4},{4,0},{8,12},{12,8},{16,20},{20,16},{24,28},{28,24},{1,5},{5... | collective-permute-start | bytes 6291464 | tf_op jit(solution)/shard_map/ppermute | solution.py:281
  520.2 23.3 %collective-permute-start.51 = (bf16[512,1536]{1,0:T(8,128)(2,1)}, bf16[512,1536]{1,0:T(8,128)(2,1)}, u32[]{:S(2)}, u32[]{:S(2)}) collective-permute-start(bf16[512,1536]{1,0:T(8,128)(2,1)} %get-tuple-element.182), channel_id=1, source_target_pairs={{0,8},{4,20},{8,0},{12,28},{16,24},{20,4},{24,16},{28,12},{1,9},{5... | collective-permute-start | bytes 4718600 | tf_op jit(solution)/shard_map/ppermute | solution.py:334
  542.2 34.8 %collective-permute-start.54 = (bf16[512,2048]{1,0:T(8,128)(2,1)}, bf16[512,2048]{1,0:T(8,128)(2,1)}, u32[]{:S(2)}, u32[]{:S(2)}) collective-permute-start(bf16[512,2048]{1,0:T(8,128)(2,1)} %constant_dynamic-update-slice_fusion.2.refs_0_), channel_id=1, source_target_pairs={{0,8},{4,20},{8,0},{12,28},{16,24},{20,4},{24,16},{28,12},{1,9},{5... | collective-permute-start | bytes 6291464 | tf_op jit(solution)/shard_map/ppermute | solution.py:281
  579.1 32.1 %collective-permute-start.57 = (bf16[512,2048]{1,0:T(8,128)(2,1)}, bf16[512,2048]{1,0:T(8,128)(2,1)}, u32[]{:S(2)}, u32[]{:S(2)}) collective-permute-start(bf16[512,2048]{1,0:T(8,128)(2,1)} %constant_dynamic-update-slice_fusion.2.refs_0_), channel_id=1, source_target_pairs={{0,4},{4,0},{8,12},{12,8},{16,20},{20,16},{24,28},{28,24},{1,5},{5... | collective-permute-start | bytes 6291464 | tf_op jit(solution)/shard_map/ppermute | solution.py:281
  579.2 32.1 %collective-permute-start.58 = (bf16[512,2048]{1,0:T(8,128)(2,1)}, bf16[512,2048]{1,0:T(8,128)(2,1)}, u32[]{:S(2)}, u32[]{:S(2)}) collective-permute-start(bf16[512,2048]{1,0:T(8,128)(2,1)} %collective-permute-done.54.refs_1_), channel_id=1, source_target_pairs={{0,4},{4,0},{8,12},{12,8},{16,20},{20,16},{24,28},{28,24},{1,5},{5... | collective-permute-start | bytes 6291464 | tf_op jit(solution)/shard_map/ppermute | solution.py:281
  599.6 24.0 %collective-permute-start.59 = (bf16[512,1536]{1,0:T(8,128)(2,1)}, bf16[512,1536]{1,0:T(8,128)(2,1)}, u32[]{:S(2)}, u32[]{:S(2)}) collective-permute-start(bf16[512,1536]{1,0:T(8,128)(2,1)} %constant_dynamic-update-slice_fusion.4.refs_0_), channel_id=1, source_target_pairs={{0,8},{4,20},{8,0},{12,28},{16,24},{20,4},{24,16},{28,12},{1,9},{5... | collective-permute-start | bytes 4718600 | tf_op jit(solution)/shard_map/ppermute | solution.py:281
  (116 other events, 1617.0 us)
Sparse Core Ops, SparseCore 0:
  99.2 38.9 all-gather.4
  144.3 53.0 all-gather.6
  302.3 74.8 reduce-scatter.4
  381.5 81.9 reduce-scatter.6
  466.2 76.7 reduce-scatter.8
  545.8 77.9 reduce-scatter.10
